TPU v7x, 32 devices: a whole 2x2x4 slice. The times are simulated.
32 devices in a mesh: seq: 8 (over z, y), head: 4 (over x, core).
Axes of the slice: x: 2, y: 2, z: 4, core: 2. Of those that a mesh axis runs over, the one named last changes fastest.
Arguments:
- tokens: bfloat16 [24576, 768], P('seq'), may hold values from -6 to 6
- w_query: bfloat16 [768, 768], P(None, 'head'), may hold values from -0.21875 to 0.21875
- w_key: bfloat16 [768, 768], P(None, 'head'), may hold values from -0.21875 to 0.21875
- w_value: bfloat16 [768, 768], P(None, 'head'), may hold values from -0.21875 to 0.21875
- freq: float32 [64, 128], replicated, may hold values from -1.5 to 1.5
- w_out: bfloat16 [768, 768], replicated, may hold values from -0.21875 to 0.21875
- router: bfloat16 [768, 32], replicated, may hold values from -0.21875 to 0.21875
- w_in: bfloat16 [32, 768, 3072], P(('seq', 'head')), may hold values from -0.21875 to 0.21875
- w_down: bfloat16 [32, 3072, 768], P(('seq', 'head')), may hold values from -0.109375 to 0.109375
- picks: int32 [32, 32, 6], P(None, ('seq', 'head')), may hold values from 0 to 767, as said below
Outputs:
- layer_out: bfloat16 [24576, 768], P(('seq', 'head'))
Inputs may be any that keep to these rules, and one draw needn't show every extreme that they name: `picks`: for each expert and each source block the 6 picked rows are distinct.
All inputs are finite; a program needn't handle non-finite values.
Results may differ from a plain program's by a relative error of at most 0.017.
Values may be sent and summed in bfloat16 or wider, within the bound.
No kernel may reach another device: no remote copies, remote signals or barrier semaphores. Data moves between devices by JAX's collectives and lax.ppermute only.
A program may use at most 128 MiB of HBM per device.

v0:
```python
import math

import jax
import jax.numpy as jnp
from jax import lax
from jax.sharding import PartitionSpec as P

HD = 64
BLOCK = 512


EPS = 1e-06


def features(projected, freq, heads):
    rows = projected.shape[0]
    split = projected.reshape(rows, heads, -1).astype(jnp.float32)
    phase = jnp.einsum("thd,df->thf", split, freq, precision=lax.Precision.HIGHEST)
    scale = 1.0 / math.sqrt(freq.shape[1])
    return (jnp.concatenate([jnp.cos(phase), jnp.sin(phase)], axis=-1) * scale).astype(jnp.bfloat16)


def local_pass(qf, kf, vals, block, start_state):
    total, heads, feat = qf.shape
    width = vals.shape[2]
    count = total // block
    q_blocks = qf.reshape(count, block, heads, feat)
    k_blocks = kf.reshape(count, block, heads, feat)
    v_blocks = vals.reshape(count, block, heads, width)
    causal = jnp.arange(block)[:, None] >= jnp.arange(block)[None, :]

    def advance(state, blocks):
        q_part, k_part, v_part = blocks
        scores = jnp.einsum("bhf,chf->hbc", q_part, k_part, preferred_element_type=jnp.float32)
        scores = jnp.where(causal[None], scores, 0.0).astype(jnp.bfloat16)
        inner = jnp.einsum("hbc,chd->bhd", scores, v_part, preferred_element_type=jnp.float32)
        state_high = state.astype(jnp.bfloat16)
        state_low = (state - state_high.astype(jnp.float32)).astype(jnp.bfloat16)
        carried = jnp.einsum("bhf,hfd->bhd", q_part, state_high, preferred_element_type=jnp.float32)
        carried = carried + jnp.einsum(
            "bhf,hfd->bhd", q_part, state_low, preferred_element_type=jnp.float32
        )
        state = state + jnp.einsum(
            "chf,chd->hfd", k_part, v_part, preferred_element_type=jnp.float32
        )
        return (state, inner + carried)

    final, outs = lax.scan(advance, start_state, (q_blocks, k_blocks, v_blocks))
    return outs.reshape(total, heads, width)


def per_device(tokens, w_query, w_key, w_value, freq, w_out, router, w_in, w_down, picks):
    heads = w_query.shape[1] // HD
    total = tokens.shape[0]
    query = jnp.dot(tokens, w_query, preferred_element_type=jnp.float32).astype(jnp.bfloat16)
    key = jnp.dot(tokens, w_key, preferred_element_type=jnp.float32).astype(jnp.bfloat16)
    value = jnp.dot(tokens, w_value, preferred_element_type=jnp.float32).astype(jnp.bfloat16)
    q_feat = features(query, freq, heads)
    k_feat = features(key, freq, heads)
    vals = value.reshape(total, heads, HD)
    local_state = jnp.einsum("thf,thd->hfd", k_feat, vals, preferred_element_type=jnp.float32)
    zero_state = jnp.zeros_like(local_state)
    mine = lax.axis_index("seq")
    piece = lax.all_gather(
        local_state[None].astype(jnp.bfloat16), "seq", axis=0, tiled=True
    ).astype(jnp.float32)
    order = jnp.arange(piece.shape[0], dtype=jnp.int32)
    keep = (order < mine).astype(jnp.float32)
    prefix = zero_state + jnp.sum(piece * keep[:, None, None, None], axis=0)
    raw = local_pass(q_feat, k_feat, vals, BLOCK, prefix)
    meansq = jnp.mean(raw * raw, axis=-1, keepdims=True)
    attn = (raw * lax.rsqrt(meansq + EPS)).astype(jnp.bfloat16).reshape(total, heads * HD)
    group = lax.axis_size("head")
    rows = total // group
    whole = lax.all_to_all(attn, "head", split_axis=0, concat_axis=1, tiled=True)
    mixed = jnp.dot(whole, w_out, preferred_element_type=jnp.float32)
    resid = lax.dynamic_slice_in_dim(tokens, lax.axis_index("head") * rows, rows, 0)
    hidden_state = (resid.astype(jnp.float32) + mixed).astype(jnp.bfloat16)
    gate = jax.nn.sigmoid(jnp.dot(hidden_state, router, preferred_element_type=jnp.float32)).astype(
        jnp.bfloat16
    )
    experts, single, capacity = picks.shape
    chosen = picks.reshape(-1)
    onehot = (chosen[:, None] == jnp.arange(rows, dtype=jnp.int32)[None, :]).astype(jnp.bfloat16)
    outgoing = jnp.dot(onehot, hidden_state, preferred_element_type=jnp.float32).astype(
        jnp.bfloat16
    )
    outgoing = outgoing.reshape(experts, capacity, -1)
    first = w_in[0]
    second = w_down[0]
    arrived = lax.all_to_all(outgoing, ("seq", "head"), split_axis=0, concat_axis=0, tiled=True)
    width = arrived.shape[2]
    flat = arrived.reshape(-1, width)
    inner = jax.nn.gelu(
        jnp.dot(flat, first, preferred_element_type=jnp.float32), approximate=True
    ).astype(jnp.bfloat16)
    result = jnp.dot(inner, second, preferred_element_type=jnp.float32).astype(jnp.bfloat16)
    result = result.reshape(arrived.shape)
    returned = lax.all_to_all(result, ("seq", "head"), split_axis=0, concat_axis=0, tiled=True)
    combine = onehot.T * jnp.repeat(gate, capacity, axis=1)
    moe = jnp.dot(
        combine, returned.reshape(experts * capacity, -1), preferred_element_type=jnp.float32
    )
    return (hidden_state.astype(jnp.float32) + moe).astype(jnp.bfloat16)


def solution(mesh):
    in_specs = (
        P("seq", None),
        P(None, "head"),
        P(None, "head"),
        P(None, "head"),
        P(),
        P(),
        P(),
        P(("seq", "head"), None, None),
        P(("seq", "head"), None, None),
        P(None, ("seq", "head"), None),
    )
    out_specs = P(("seq", "head"), None)
    return jax.shard_map(
        per_device, mesh=mesh, in_specs=in_specs, out_specs=out_specs, check_vma=False
    )
```

profile of v0, /device:TPU:0, one launch (start us, length us, event | category | flops | bytes accessed | tf_op | source)
XLA Modules:
  0.0 246.8 jit_solution(15940518639932796654)
XLA Ops:
  0.0 4.2 %convolution_convert_fusion.2 = bf16[3072,192]{0,1:T(8,128)(2,1)S(1)} fusion(bf16[3072,768]{1,0:T(8,128)(2,1)} %param.12, bf16[768,192]{0,1:T(8,128)(2,1)} %param.14), kind=kOutput, calls=%fused_computation.49 | convolution fusion | flops 906559488 | bytes 6193152 | tf_op jit(solution)/shard_map/dot_general | solution.py:56
  4.2 1.7 convolution_convert_fusion
  5.9 24.1 %fusion.88 = (f32[3072,3,128]{2,0,1:T(8,128)}, f32[3072,3,128]{2,0,1:T(8,128)}) fusion(bf16[3072,3,64]{0,2,1:T(8,128)(2,1)S(1)} %bitcast.131, f32[64,128]{1,0:T(8,128)S(1)} %copy-done.2), kind=kOutput, calls=%fused_computation.97 | convolution fusion | flops 905969664 | bytes 10649600 | tf_op jit(solution)/shard_map/thd,df->thf/dot_general | solution.py:18
  30.0 24.1 %fusion.87 = (f32[3072,3,128]{2,0,1:T(8,128)}, f32[3072,3,128]{2,0,1:T(8,128)}) fusion(bf16[3072,3,64]{0,2,1:T(8,128)(2,1)S(1)} %bitcast.130, f32[64,128]{1,0:T(8,128)S(1)} %copy-done.2), kind=kOutput, calls=%fused_computation.96 | convolution fusion | flops 905969664 | bytes 10649600 | tf_op jit(solution)/shard_map/thd,df->thf/dot_general | solution.py:18
  54.2 2.7 %convolution_convert_fusion.1 = bf16[3072,192]{0,1:T(8,128)(2,1)} fusion(bf16[3072,768]{1,0:T(8,128)(2,1)S(1)} %copy-done.4, bf16[768,192]{0,1:T(8,128)(2,1)S(1)} %copy-done.6), kind=kOutput, calls=%fused_computation.48 | convolution fusion | flops 906559488 | bytes 6193152 | tf_op jit(solution)/shard_map/dot_general | solution.py:57
  56.8 2.8 %reshape_reshape.3 = bf16[6,512,3,64]{1,0,3,2:T(8,128)(2,1)S(1)} reshape(bf16[3072,192]{0,1:T(8,128)(2,1)} %convolution_convert_fusion.1) | data formatting | bytes 2359296 | tf_op jit(solution)/shard_map/reshape;reshape | solution.py:29
  59.7 5.1 %fusion.60 = bf16[3,256,64]{1,2,0:T(8,128)(2,1)S(1)} fusion(bf16[3072,3,64]{0,2,1:T(8,128)(2,1)} %bitcast.133, f32[3072,3,128]{2,0,1:T(8,128)} %get-tuple-element.90, f32[3072,3,128]{2,0,1:T(8,128)} %get-tuple-element.89), kind=kOutput, calls=%fused_computation.68 | convolution fusion | flops 309116928 | bytes 10715136 | tf_op jit(solution)/shard_map/thf,thd->hfd/dot_general | solution.py:61
  64.8 36.2 %all-gather = bf16[24,256,64]{1,2,0:T(8,128)(2,1)} all-gather(bf16[3,256,64]{1,2,0:T(8,128)(2,1)S(1)} %fusion.60), channel_id=2, replica_groups=mesh['seq'=8,'head'=4] {'seq'}, dimensions={0}, use_global_device_ids=true | all-gather | bytes 884736 | tf_op jit(solution)/shard_map/all_gather | solution.py:64
  101.0 1.4 copy.30
  103.8 11.4 %fusion.35 = (bf16[6,512,3,256]{3,1,2,0:T(8,128)(2,1)}, bf16[6,512,3,256]{3,1,2,0:T(8,128)(2,1)}) fusion(f32[6,512,3,128]{3,1,0,2:T(8,128)} %bitcast.126, f32[6,512,3,128]{3,1,0,2:T(8,128)} %bitcast.125, f32[6,512,3,128]{3,1,0,2:T(8,128)} %bitcast.128, f32[6,512,3,128]{3,1,0,2:T(8,128)} %bitcast.127), kind=kLoop, calls=%fused_computation.39 | loop fusion | flops 14155776 | bytes 28311552 | tf_op jit(solution)/shard_map/convert_element_type | solution.py:20
  115.1 47.0 %while.13 = (s32[]{:T(128)}, f32[3,256,64]{1,2,0:T(8,128)S(1)}, f32[6,512,3,64]{1,3,2,0:T(8,128)}, bf16[6,512,3,256]{3,1,2,0:T(8,128)(2,1)}, bf16[6,512,3,64]{1,...) while((s32[]{:T(128)}, f32[3,256,64]{1,2,0:T(8,128)S(1)}, ...), condition=%wide.region_2.3_spmd.clone, body=%wide.region_1.2_spmd.clone.sunk | while | flops 656637952 | bytes 7606349 | solution.py:48
  115.1 1.5 convolution_bitcast_fusion.3
  116.6 1.5 fusion.122
  118.2 3.2 %fusion.123 = f32[6,512,3,64]{1,3,2,0:T(8,128)} fusion(f32[6,512,3,64]{1,3,2,0:T(8,128)} %get-tuple-element.141, s32[]{:T(128)} %get-tuple-element.139, f32[512,3,64]{0,2,1:T(8,128)S(1)} %fusion.122, pred[512,512]{1,0:T(8,128)(4,1)S(1)} %iota_compare_fusion.5, bf16[6,512,3,256]{3,1,2,0:T(8,128)(2,1)} %get-tuple-element.149, ...), kind=kOutput, calls=%fused_computation.6.clone.1 | convolution fusion | flops 504987648 | bytes 2820096 | tf_op jit(solution)/shard_map/while/body/eval_jaxpr/hbc,chd->bhd/dot_general | solution.py:36
  121.4 1.5 convolution_add_fusion.2
  122.9 1.5 convolution_bitcast_fusion.3
  124.4 1.5 fusion.122
  126.0 3.2 %fusion.123 = f32[6,512,3,64]{1,3,2,0:T(8,128)} fusion(f32[6,512,3,64]{1,3,2,0:T(8,128)} %get-tuple-element.141, s32[]{:T(128)} %get-tuple-element.139, f32[512,3,64]{0,2,1:T(8,128)S(1)} %fusion.122, pred[512,512]{1,0:T(8,128)(4,1)S(1)} %iota_compare_fusion.5, bf16[6,512,3,256]{3,1,2,0:T(8,128)(2,1)} %get-tuple-element.149, ...), kind=kOutput, calls=%fused_computation.6.clone.1 | convolution fusion | flops 504987648 | bytes 2820096 | tf_op jit(solution)/shard_map/while/body/eval_jaxpr/hbc,chd->bhd/dot_general | solution.py:36
  129.2 1.5 convolution_add_fusion.2
  130.8 1.5 convolution_bitcast_fusion.3
  132.3 1.5 fusion.122
  133.8 3.2 %fusion.123 = f32[6,512,3,64]{1,3,2,0:T(8,128)} fusion(f32[6,512,3,64]{1,3,2,0:T(8,128)} %get-tuple-element.141, s32[]{:T(128)} %get-tuple-element.139, f32[512,3,64]{0,2,1:T(8,128)S(1)} %fusion.122, pred[512,512]{1,0:T(8,128)(4,1)S(1)} %iota_compare_fusion.5, bf16[6,512,3,256]{3,1,2,0:T(8,128)(2,1)} %get-tuple-element.149, ...), kind=kOutput, calls=%fused_computation.6.clone.1 | convolution fusion | flops 504987648 | bytes 2820096 | tf_op jit(solution)/shard_map/while/body/eval_jaxpr/hbc,chd->bhd/dot_general | solution.py:36
  137.1 1.5 convolution_add_fusion.2
  138.6 1.5 convolution_bitcast_fusion.3
  140.1 1.5 fusion.122
  141.7 3.2 %fusion.123 = f32[6,512,3,64]{1,3,2,0:T(8,128)} fusion(f32[6,512,3,64]{1,3,2,0:T(8,128)} %get-tuple-element.141, s32[]{:T(128)} %get-tuple-element.139, f32[512,3,64]{0,2,1:T(8,128)S(1)} %fusion.122, pred[512,512]{1,0:T(8,128)(4,1)S(1)} %iota_compare_fusion.5, bf16[6,512,3,256]{3,1,2,0:T(8,128)(2,1)} %get-tuple-element.149, ...), kind=kOutput, calls=%fused_computation.6.clone.1 | convolution fusion | flops 504987648 | bytes 2820096 | tf_op jit(solution)/shard_map/while/body/eval_jaxpr/hbc,chd->bhd/dot_general | solution.py:36
  144.9 1.5 convolution_add_fusion.2
  146.5 1.5 convolution_bitcast_fusion.3
  148.0 1.5 fusion.122
  149.5 3.2 %fusion.123 = f32[6,512,3,64]{1,3,2,0:T(8,128)} fusion(f32[6,512,3,64]{1,3,2,0:T(8,128)} %get-tuple-element.141, s32[]{:T(128)} %get-tuple-element.139, f32[512,3,64]{0,2,1:T(8,128)S(1)} %fusion.122, pred[512,512]{1,0:T(8,128)(4,1)S(1)} %iota_compare_fusion.5, bf16[6,512,3,256]{3,1,2,0:T(8,128)(2,1)} %get-tuple-element.149, ...), kind=kOutput, calls=%fused_computation.6.clone.1 | convolution fusion | flops 504987648 | bytes 2820096 | tf_op jit(solution)/shard_map/while/body/eval_jaxpr/hbc,chd->bhd/dot_general | solution.py:36
  152.8 1.5 convolution_add_fusion.2
  154.3 1.5 convolution_bitcast_fusion.3
  155.8 1.5 fusion.122
  157.4 3.2 %fusion.123 = f32[6,512,3,64]{1,3,2,0:T(8,128)} fusion(f32[6,512,3,64]{1,3,2,0:T(8,128)} %get-tuple-element.141, s32[]{:T(128)} %get-tuple-element.139, f32[512,3,64]{0,2,1:T(8,128)S(1)} %fusion.122, pred[512,512]{1,0:T(8,128)(4,1)S(1)} %iota_compare_fusion.5, bf16[6,512,3,256]{3,1,2,0:T(8,128)(2,1)} %get-tuple-element.149, ...), kind=kOutput, calls=%fused_computation.6.clone.1 | convolution fusion | flops 504987648 | bytes 2820096 | tf_op jit(solution)/shard_map/while/body/eval_jaxpr/hbc,chd->bhd/dot_general | solution.py:36
  160.6 1.5 convolution_add_fusion.2
  162.1 4.8 %copy.31 = f32[6,512,3,64]{1,0,3,2:T(8,128)} copy(f32[6,512,3,64]{1,3,2,0:T(8,128)} %get-tuple-element.42) | data formatting | bytes 4718592 | tf_op jit(solution)/shard_map/while | solution.py:48
  167.3 4.5 %reshape.74 = f32[4,768,192]{1,0,2:T(4,128)} reshape(f32[6,512,3,64]{1,0,3,2:T(8,128)} %copy.31) | data formatting | bytes 4718592 | tf_op jit(solution)/shard_map/reshape | solution.py:49
  171.8 1.7 mul.69
  173.4 3.7 %mul.70 = f32[4,768,192]{1,0,2:T(4,128)} reshape(f32[3072,3,64]{0,2,1:T(8,128)} %mul.69) | data formatting | bytes 4718592 | tf_op jit(solution)/shard_map/mul | solution.py:72
  177.1 3.0 %multiply_convert_fusion = bf16[4,768,192]{1,0,2:T(4,128)(2,1)S(1)} fusion(f32[4,768,192]{1,0,2:T(4,128)} %reshape.74, f32[4,768,192]{1,0,2:T(4,128)} %mul.70), kind=kLoop, calls=%fused_computation.62 | loop fusion | flops 1179648 | bytes 5898240 | tf_op jit(solution)/shard_map/convert_element_type | solution.py:72
  181.3 3.5 %all-to-all-start = ((bf16[4,768,192]{1,2,0:T(8,128)(2,1)}), bf16[4,768,192]{1,2,0:T(8,128)(2,1)S(1)}, u32[]{:S(2)}, u32[]{:S(2)}) async-start(bf16[4,768,192]{1,2,0:T(8,128)(2,1)} %copy.32), calls=%async_computation | async-start | bytes 2359296 | tf_op jit(solution)/shard_map/all_to_all | solution.py:75
  185.0 15.6 %all-to-all-done = bf16[4,768,192]{1,2,0:T(8,128)(2,1)S(1)} async-done(((bf16[4,768,192]{1,2,0:T(8,128)(2,1)}), bf16[4,768,192]{1,2,0:T(8,128)(2,1)S(1)}, u32[]{:S(2)}, u32[]{:S(2)}) %all-to-all-start) | async-done | bytes 1179680 | tf_op jit(solution)/shard_map/all_to_all | solution.py:75
  200.7 2.4 add_convert_fusion
  204.6 17.6 %all_to_all.26 = bf16[32,6,768]{2,1,0:T(8,128)(2,1)S(1)} all-to-all(bf16[32,6,768]{2,1,0:T(8,128)(2,1)S(1)} %reshape.75), channel_id=1, replica_groups=mesh['seq'=8,'head'=4] {'seq','head'}, dimensions={0} | all-to-all | bytes 589824 | tf_op jit(solution)/shard_map/all_to_all | solution.py:91
  222.4 6.2 %fusion.57 = bf16[192,768]{1,0:T(8,128)(2,1)S(1)} fusion(bf16[1,3072,768]{2,1,0:T(8,128)(2,1)} %param.20, bf16[192,768]{1,0:T(8,128)(2,1)S(1)} %reshape.76, bf16[1,768,3072]{2,1,0:T(8,128)(2,1)} %param.19), kind=kOutput, calls=%fused_computation.66 | convolution fusion | flops 1817395200 | bytes 10027008 | tf_op jit(solution)/shard_map/dot_general | solution.py:97
  229.4 2.6 %all-to-all-start.2 = ((bf16[32,6,768]{2,1,0:T(8,128)(2,1)}), bf16[32,6,768]{2,1,0:T(8,128)(2,1)S(1)}, u32[]{:S(2)}, u32[]{:S(2)}) async-start(bf16[32,6,768]{2,1,0:T(8,128)(2,1)} %reshape.77), calls=%async_computation.2 | async-start | bytes 786432 | tf_op jit(solution)/shard_map/all_to_all | solution.py:99
  232.6 12.6 %all-to-all-done.2 = bf16[32,6,768]{2,1,0:T(8,128)(2,1)S(1)} async-done(((bf16[32,6,768]{2,1,0:T(8,128)(2,1)}), bf16[32,6,768]{2,1,0:T(8,128)(2,1)S(1)}, u32[]{:S(2)}, u32[]{:S(2)}) %all-to-all-start.2) | async-done | bytes 294944 | tf_op jit(solution)/shard_map/all_to_all | solution.py:99
  245.2 1.6 fusion.55
  (40 shorter events, 6.6 us)
Async XLA Ops:
  0.0 200.6 %copy-start = (bf16[768,768]{1,0:T(8,128)(2,1)S(1)}, bf16[768,768]{1,0:T(8,128)(2,1)}, u32[]{:S(2)}) copy-start(bf16[768,768]{1,0:T(8,128)(2,1)} %param.17) | copy-start | bytes 3538948
  0.0 4.2 %copy-start.4 = (bf16[3072,768]{1,0:T(8,128)(2,1)S(1)}, bf16[3072,768]{1,0:T(8,128)(2,1)}, u32[]{:S(2)}) copy-start(bf16[3072,768]{1,0:T(8,128)(2,1)} %param.12) | copy-start | bytes 14155780
  0.0 4.2 %copy-start.5 = (bf16[768,192]{0,1:T(8,128)(2,1)S(1)}, bf16[768,192]{0,1:T(8,128)(2,1)}, u32[]{:S(2)}) copy-start(bf16[768,192]{0,1:T(8,128)(2,1)} %param.13) | copy-start | bytes 884740
  4.2 1.7 copy-start.2
  30.0 24.1 %copy-start.6 = (bf16[768,192]{0,1:T(8,128)(2,1)S(1)}, bf16[768,192]{0,1:T(8,128)(2,1)}, u32[]{:S(2)}) copy-start(bf16[768,192]{0,1:T(8,128)(2,1)} %param.15) | copy-start | bytes 884740
  162.1 4.8 %copy-start.1 = (f32[6,512,3,64]{1,3,2,0:T(8,128)S(1)}, f32[6,512,3,64]{1,3,2,0:T(8,128)}, u32[]{:S(2)}) copy-start(f32[6,512,3,64]{1,3,2,0:T(8,128)} %get-tuple-element.42) | copy-start | bytes 7077892
  180.1 4.7 %copy-start.3 = (s32[32,1,6]{0,1,2:T(1,128)S(1)}, s32[32,1,6]{0,1,2:T(1,128)}, u32[]{:S(2)}) copy-start(s32[32,1,6]{0,1,2:T(1,128)} %param.21) | copy-start | bytes 2308
  181.3 19.4 %all-to-all-start = ((bf16[4,768,192]{1,2,0:T(8,128)(2,1)}), bf16[4,768,192]{1,2,0:T(8,128)(2,1)S(1)}, u32[]{:S(2)}, u32[]{:S(2)}) async-start(bf16[4,768,192]{1,2,0:T(8,128)(2,1)} %copy.32), calls=%async_computation | async-start | bytes 2359296 | tf_op jit(solution)/shard_map/all_to_all | solution.py:75
  203.0 1.0 copy-start.8
  222.3 9.7 %copy-start.7 = (bf16[768,32]{0,1:T(8,128)(2,1)S(1)}, bf16[768,32]{0,1:T(8,128)(2,1)}, u32[]{:S(2)}) copy-start(bf16[768,32]{0,1:T(8,128)(2,1)} %param.18) | copy-start | bytes 147460
  222.3 9.7 %copy-start.9 = (bf16[768,768]{1,0:T(8,128)(2,1)S(1)}, bf16[768,768]{1,0:T(8,128)(2,1)}, u32[]{:S(2)}) copy-start(bf16[768,768]{1,0:T(8,128)(2,1)} %copy-done.8) | copy-start | bytes 3538948
  229.4 15.8 %all-to-all-start.2 = ((bf16[32,6,768]{2,1,0:T(8,128)(2,1)}), bf16[32,6,768]{2,1,0:T(8,128)(2,1)S(1)}, u32[]{:S(2)}, u32[]{:S(2)}) async-start(bf16[32,6,768]{2,1,0:T(8,128)(2,1)} %reshape.77), calls=%async_computation.2 | async-start | bytes 786432 | tf_op jit(solution)/shard_map/all_to_all | solution.py:99
where the time goes:
time: 248 us; the launch traced here: 247 us
  matrix products  119 us (48%)
  blocking collectives  53.8 us (22%)
  waiting for transfers between devices  28.3 us (11%)
  local copies, waits for them, and re-layouts  22.2 us (9%)
  other arithmetic  16.6 us (7%)
  starting transfers between devices  6.18 us (2%)
    dot_general x2, matrix products, features(): jnp.einsum('thd,df->thf', split, freq, precision=lax.Precision.HIGHEST)  48.2 us
    all_gather x1, blocking collectives, per_device(): lax.all_gather(local_state[None].astype(jnp.bfloat16), 'seq', axis=0, til...  36.2 us
    dot_general x6, matrix products, advance(): jnp.einsum('hbc,chd->bhd', scores, v_part, preferred_element_type=jnp.flo...  19.3 us
    all_to_all x1, blocking collectives, per_device(): lax.all_to_all(outgoing, ('seq', 'head'), split_axis=0, concat_axis=0, ti...  17.6 us
    all_to_all x1, waiting for transfers between devices, per_device(): lax.all_to_all(attn, 'head', split_axis=0, concat_axis=1, tiled=True)  15.6 us
    all_to_all x1, waiting for transfers between devices, per_device(): lax.all_to_all(result, ('seq', 'head'), split_axis=0, concat_axis=0, tile...  12.6 us
    convert_element_type x1, other arithmetic, features(): (jnp.concatenate([jnp.cos(phase), jnp.sin(phase)], axis=-1) * scale).asty...  11.4 us
    dot_general x6, matrix products, advance(): jnp.einsum('chf,chd->hfd', k_part, v_part, preferred_element_type=jnp.flo...  9.07 us
  transfers between devices with their start and end apart: 2, of which 2 were waited for; matrix products, arithmetic and copies ran while one was open for 0% of the time, Pallas kernels for 0%

commit v1 on v0

v1 whole, which is shorter than its diff:
```python
import functools
import math

import jax
import jax.numpy as jnp
from jax import lax
from jax.experimental import pallas as pl
from jax.experimental.pallas import tpu as pltpu
from jax.sharding import PartitionSpec as P

HD = 64
EPS = 1e-06
CHUNK = 256
PAD = 8
BF = jnp.bfloat16
F32 = jnp.float32
MIB = 2**20
SIN = (3.14158202, -5.16714279, 2.54189901, -0.55463616)
COS = (0.9999933, -4.93393802, 4.04128381, -1.22212701)


def nn(a, b):
    return lax.dot_general(a, b, (((1,), (0,)), ((), ())), preferred_element_type=F32)


def nt(a, b):
    return lax.dot_general(a, b, (((1,), (1,)), ((), ())), preferred_element_type=F32)


def tn(a, b):
    return lax.dot_general(a, b, (((0,), (0,)), ((), ())), preferred_element_type=F32)


def wave(turns, scale):
    big = F32(1.5 * 2.0**23)
    r = turns - ((turns + big) - big)
    u = r * r
    root = math.sqrt(2 * scale)
    a = [F32(v * root) for v in SIN]
    b = [F32(v * root) for v in COS]
    s = r * (a[0] + u * (a[1] + u * (a[2] + u * a[3])))
    c = b[0] + u * (b[1] + u * (b[2] + u * b[3]))
    return F32(scale) - s * s, s * c


def parts(f):
    hi = f.astype(BF)
    rest = f - hi.astype(F32)
    mid = rest.astype(BF)
    lo = (rest - mid.astype(F32)).astype(BF)
    return [hi, mid, lo]


def whole(shape):
    return pl.BlockSpec(shape, lambda *_: (0,) * len(shape))


def params(mib=40):
    return pltpu.CompilerParams(vmem_limit_bytes=mib * MIB)


def cost(flops, nbytes):
    return pl.CostEstimate(flops=int(flops), bytes_accessed=int(nbytes), transcendentals=0)


def key_kernel(tok_ref, wk_ref, wvt_ref, freq_ref, kf_ref, vt_ref, sc_ref, tot_ref, f3, st):
    heads = wk_ref.shape[1] // HD
    half = freq_ref.shape[1]

    @pl.when(pl.program_id(0) == 0)
    def _():
        f3[...] = jnp.concatenate(parts(freq_ref[...] * F32(0.5 / math.pi)), axis=0)
        st[...] = jnp.zeros_like(st)

    tok = tok_ref[...]
    k = nn(tok, wk_ref[...]).astype(BF)
    vt = nt(wvt_ref[...], tok).astype(BF)
    vt_ref[...] = vt
    for h in range(heads):
        kh = k[:, h * HD : (h + 1) * HD]
        phase = nn(jnp.concatenate([kh] * 3, axis=1), f3[...])
        c, s = wave(phase, 1 / math.sqrt(half))
        kf = jnp.concatenate([c.astype(BF), s.astype(BF)], axis=1)
        kf_ref[:, h * 2 * half : (h + 1) * 2 * half] = kf
        mine = slice(h * HD, (h + 1) * HD)
        acc = st[mine, :]
        for j in range(tok.shape[0] // CHUNK):
            sc_ref[j, mine, :] = acc.astype(BF)
            rows = slice(j * CHUNK, (j + 1) * CHUNK)
            acc = acc + nn(vt[mine, rows], kf[rows])
        st[mine, :] = acc
    tot_ref[...] = st[...].astype(BF)


def key_pass(tokens, w_key, wvt, freq, rows):
    total, d = tokens.shape
    wid = w_key.shape[1]
    feat = 2 * freq.shape[1]
    heads = wid // HD
    return pl.pallas_call(
        key_kernel,
        grid=(total // rows,),
        in_specs=[
            pl.BlockSpec((rows, d), lambda i: (i, 0)),
            whole(w_key.shape),
            whole(wvt.shape),
            whole(freq.shape),
        ],
        out_specs=[
            pl.BlockSpec((rows, heads * feat), lambda i: (i, 0)),
            pl.BlockSpec((wid, rows), lambda i: (0, i)),
            pl.BlockSpec((rows // CHUNK, wid, feat), lambda i: (i, 0, 0)),
            whole((wid, feat)),
        ],
        out_shape=[
            jax.ShapeDtypeStruct((total, heads * feat), BF),
            jax.ShapeDtypeStruct((wid, total), BF),
            jax.ShapeDtypeStruct((total // CHUNK, wid, feat), BF),
            jax.ShapeDtypeStruct((wid, feat), BF),
        ],
        scratch_shapes=[pltpu.VMEM((3 * HD, freq.shape[1]), BF), pltpu.VMEM((wid, feat), F32)],
        compiler_params=params(),
        cost_estimate=cost(5e9, 12e6),
        name="key_pass",
    )(tokens, w_key, wvt, freq)


def query_kernel(tok_ref, wqt_ref, ft_ref, kf_ref, vt_ref, sc_ref, *rest):
    qft_ref, raw_ref, f3t = rest[-3:]
    heads = wqt_ref.shape[0] // HD
    half = ft_ref.shape[0]
    feat = 2 * half

    @pl.when(pl.program_id(0) == 0)
    def _():
        f3t[...] = jnp.concatenate(parts(ft_ref[...] * F32(0.5 / math.pi)), axis=1)

    tok = tok_ref[...]
    qt = nt(wqt_ref[...], tok).astype(BF)
    place = [lax.broadcasted_iota(jnp.int32, (CHUNK, CHUNK), i) for i in (0, 1)]
    keep = place[0] <= place[1]
    for h in range(heads):
        mine = slice(h * HD, (h + 1) * HD)
        phase = nn(f3t[...], jnp.concatenate([qt[mine]] * 3, axis=0))
        c, s = wave(phase, 1 / math.sqrt(half))
        qf = jnp.concatenate([c.astype(BF), s.astype(BF)], axis=0)
        qft_ref[h * feat : (h + 1) * feat, :] = qf
        for j in range(tok.shape[0] // CHUNK):
            cols = slice(j * CHUNK, (j + 1) * CHUNK)
            both = jnp.concatenate([kf_ref[cols, h * feat : (h + 1) * feat], sc_ref[j, mine, :]], axis=0)
            both = nn(both, qf[:, cols])
            scores = jnp.where(keep, both[:CHUNK], 0.0).astype(BF)
            raw_ref[mine, cols] = nn(vt_ref[mine, cols], scores) + both[CHUNK:]


def query_pass(tokens, wqt, freq_t, kf, vt, sc, rows, first, count, into=None):
    total, d = tokens.shape
    wid = wqt.shape[0]
    feat = 2 * freq_t.shape[0]
    heads = wid // HD
    held = [] if into is None else list(into)
    return pl.pallas_call(
        query_kernel,
        grid=(count,),
        in_specs=[
            pl.BlockSpec((rows, d), lambda i: (i + first, 0)),
            whole(wqt.shape),
            whole(freq_t.shape),
            pl.BlockSpec((rows, heads * feat), lambda i: (i + first, 0)),
            pl.BlockSpec((wid, rows), lambda i: (0, i + first)),
            pl.BlockSpec((rows // CHUNK, wid, feat), lambda i: (i + first, 0, 0)),
        ]
        + [pl.BlockSpec(memory_space=pl.ANY)] * len(held),
        out_specs=[
            pl.BlockSpec((heads * feat, rows), lambda i: (0, i + first)),
            pl.BlockSpec((wid, rows), lambda i: (0, i + first)),
        ],
        out_shape=[
            jax.ShapeDtypeStruct((heads * feat, total), BF),
            jax.ShapeDtypeStruct((wid, total), F32),
        ],
        input_output_aliases={6 + i: i for i in range(len(held))},
        scratch_shapes=[pltpu.VMEM((freq_t.shape[0], 3 * HD), BF)],
        compiler_params=params(),
        cost_estimate=cost(1.5e9 * count, 4e6 * count),
        name="query_pass",
    )(tokens, wqt, freq_t, kf, vt, sc, *held)


def prefix_states(mine):
    size = lax.axis_size("seq")
    at = lax.axis_index("seq")
    held = mine
    before = jnp.zeros(mine.shape, F32)
    stride = 1
    while stride < size:
        radix = 2 if (size // stride).bit_length() % 2 == 0 else 4
        last = stride * radix >= size
        total = held.astype(F32)
        for k in range(1, radix):
            step = k * stride
            pairs = [(i, i ^ step) for i in range(size) if not last or i < i ^ step]
            value = lax.ppermute(held, "seq", pairs).astype(F32)
            total = total + value
            before = before + jnp.where((at ^ step) < at, value, 0.0)
        held = total.astype(BF)
        stride *= radix
    return before.astype(BF)


def norm_kernel(slots, me_ref, raw_ref, qft_ref, pre_ref, pick_ref, *rest):
    outs, sent_ref, acc = rest[:slots], rest[slots], rest[slots + 1]
    step = pl.program_id(0)
    heads = raw_ref.shape[0] // HD
    feat = pre_ref.shape[1]
    rows = raw_ref.shape[1]
    normed = []
    for h in range(heads):
        mine = slice(h * HD, (h + 1) * HD)
        raw = raw_ref[mine, :] + nn(pre_ref[mine, :], qft_ref[h * feat : (h + 1) * feat, :])
        meansq = jnp.mean(raw * raw, axis=0, keepdims=True)
        normed.append((raw * lax.rsqrt(meansq + F32(EPS))).astype(BF))
    attn = jnp.concatenate(normed, axis=0)
    for k in range(slots):

        @pl.when(step == k)
        def _():
            outs[k][...] = attn

    at = lax.broadcasted_iota(jnp.int32, (pick_ref.shape[0], rows), 1) + (me_ref[0] ^ step) * rows
    onehot = (pick_ref[...] == at).astype(F32).astype(BF)
    picked = nt(onehot, attn)

    @pl.when(step == 0)
    def _():
        acc[...] = picked

    @pl.when(step > 0)
    def _():
        acc[...] += picked

    @pl.when(step == slots - 1)
    def _():
        sent_ref[...] = acc[...].astype(BF)


def norm_pass(me, raw, qft, pre, pick_col, slots):
    wid, total = raw.shape
    rows = total // slots
    n = pick_col.shape[0]
    block = lambda i, me_ref: (0, me_ref[0] ^ i)
    return pl.pallas_call(
        functools.partial(norm_kernel, slots),
        grid_spec=pltpu.PrefetchScalarGridSpec(
            num_scalar_prefetch=1,
            grid=(slots,),
            in_specs=[
                pl.BlockSpec((wid, rows), block),
                pl.BlockSpec((qft.shape[0], rows), block),
                whole(pre.shape),
                whole(pick_col.shape),
            ],
            out_specs=[whole((wid, rows))] * slots + [whole((n, wid))],
            scratch_shapes=[pltpu.VMEM((n, wid), F32)],
        ),
        out_shape=[jax.ShapeDtypeStruct((wid, rows), BF)] * slots + [jax.ShapeDtypeStruct((n, wid), BF)],
        compiler_params=params(),
        cost_estimate=cost(3e9, 8e6),
        name="norm_pass",
    )(me, raw, qft, pre, pick_col)


def select_kernel(tok_ref, pick_ref, out_ref, acc):
    step = pl.program_id(0)
    rows = tok_ref.shape[0]
    at = lax.broadcasted_iota(jnp.int32, (pick_ref.shape[0], rows), 1) + step * rows
    onehot = (pick_ref[...] == at).astype(F32).astype(BF)
    picked = nn(onehot, tok_ref[...])

    @pl.when(step == 0)
    def _():
        acc[...] = picked

    @pl.when(step > 0)
    def _():
        acc[...] += picked

    out_ref[...] = acc[...].astype(BF)


def select_rows(tokens, pick_col, rows):
    total, d = tokens.shape
    n = pick_col.shape[0]
    return pl.pallas_call(
        select_kernel,
        grid=(total // rows,),
        in_specs=[pl.BlockSpec((rows, d), lambda i: (i, 0)), whole(pick_col.shape)],
        out_specs=whole((n, d)),
        out_shape=jax.ShapeDtypeStruct((n, d), BF),
        scratch_shapes=[pltpu.VMEM((n, d), F32)],
        compiler_params=params(),
        cost_estimate=cost(1e9, 5e6),
        name="select_rows",
    )(tokens, pick_col)


def expert_kernel(cap, attn_ref, tok_ref, wo_ref, wi_ref, wd_ref, out_ref, taken, acc):
    step = pl.program_id(0)
    n, d = tok_ref.shape

    @pl.when(step == 0)
    def _():
        mixed = tok_ref[...].astype(F32)
        for h in range(wo_ref.shape[0]):
            part = attn_ref[:, h]
            mixed = mixed + nn(part.reshape(n, part.shape[-1]), wo_ref[h])
        taken[...] = mixed.astype(BF)
        acc[...] = jnp.zeros_like(acc)

    inner = jax.nn.gelu(nn(taken[...], wi_ref[0]), approximate=True).astype(BF)
    acc[...] += nn(inner, wd_ref[0])

    @pl.when(step == pl.num_programs(0) - 1)
    def _():
        m = out_ref.shape[0]
        slot = lax.broadcasted_iota(jnp.int32, (m, n), 0)
        row = lax.broadcasted_iota(jnp.int32, (m, n), 1)
        spread = ((slot // PAD) * cap + slot % PAD == row) & (slot % PAD < cap)
        out_ref[...] = nn(spread.astype(F32).astype(BF), acc[...].astype(BF)).astype(BF)


def expert_pass(arrived, tok_sel, w_out, w_in, w_down, cap, tiles=6):
    n, d = tok_sel.shape
    ff = w_in.shape[2]
    m = n // cap * PAD
    return pl.pallas_call(
        functools.partial(expert_kernel, cap),
        grid=(tiles,),
        in_specs=[
            whole(arrived.shape),
            whole(tok_sel.shape),
            whole(w_out.shape),
            pl.BlockSpec((1, d, ff // tiles), lambda i: (0, 0, i)),
            pl.BlockSpec((1, ff // tiles, d), lambda i: (0, i, 0)),
        ],
        out_specs=whole((m, d)),
        out_shape=jax.ShapeDtypeStruct((m, d), BF),
        scratch_shapes=[pltpu.VMEM((n, d), BF), pltpu.VMEM((n, d), F32)],
        compiler_params=params(),
        cost_estimate=cost(2e9, 12e6),
        name="expert_pass",
    )(arrived, tok_sel, w_out, w_in, w_down)


def hidden_kernel(slots, me_ref, tok_ref, wo_ref, router_ref, pick_ref, *rest):
    attns, hid_ref, comb_ref = rest[:slots], rest[slots], rest[slots + 1]
    mixed = tok_ref[...].astype(F32)
    for k in range(slots):
        mixed = mixed + tn(attns[k][...], wo_ref[me_ref[0] ^ k])
    hidden = mixed.astype(BF)
    hid_ref[...] = hidden
    gate = jax.nn.sigmoid(nn(hidden, router_ref[...])).astype(BF)
    e, n = gate.shape[1], pick_ref.shape[1]
    source = lax.broadcasted_iota(jnp.int32, (e, n), 0)
    slot = lax.broadcasted_iota(jnp.int32, (e, n), 1)
    spread = nn(gate, (slot // PAD == source).astype(F32).astype(BF))
    at = lax.broadcasted_iota(jnp.int32, (hidden.shape[0], n), 0)
    comb_ref[...] = jnp.where(pick_ref[...] == at, spread, 0.0).astype(BF)


def hidden_pass(me, tokens, w_out, router, pick_row, attns, rows):
    d = tokens.shape[1]
    slots = len(attns)
    n = pick_row.shape[1]
    return pl.pallas_call(
        functools.partial(hidden_kernel, slots),
        grid_spec=pltpu.PrefetchScalarGridSpec(
            num_scalar_prefetch=1,
            grid=(1,),
            in_specs=[
                pl.BlockSpec((rows, d), lambda i, me_ref: (me_ref[0], 0)),
                whole(w_out.shape),
                whole(router.shape),
                whole(pick_row.shape),
            ]
            + [whole(a.shape) for a in attns],
            out_specs=[whole((rows, d)), whole((rows, n))],
        ),
        out_shape=[jax.ShapeDtypeStruct((rows, d), BF), jax.ShapeDtypeStruct((rows, n), BF)],
        compiler_params=params(),
        cost_estimate=cost(2e9, 6e6),
        name="hidden_pass",
    )(me, tokens, w_out, router, pick_row, *attns)


def combine_kernel(hid_ref, comb_ref, back_ref, out_ref):
    out_ref[...] = (hid_ref[...].astype(F32) + nn(comb_ref[...], back_ref[...])).astype(BF)


def combine_pass(hidden, comb, back):
    rows, d = hidden.shape
    n = comb.shape[1]
    tiles = 2
    return pl.pallas_call(
        combine_kernel,
        grid=(tiles,),
        in_specs=[
            pl.BlockSpec((rows // tiles, d), lambda i: (i, 0)),
            pl.BlockSpec((rows // tiles, n), lambda i: (i, 0)),
            whole(back.shape),
        ],
        out_specs=pl.BlockSpec((rows // tiles, d), lambda i: (i, 0)),
        out_shape=jax.ShapeDtypeStruct((rows, d), BF),
        compiler_params=params(),
        cost_estimate=cost(5e8, 4e6),
        name="combine_pass",
    )(hidden, comb, back)


def per_device(tokens, w_query, w_key, w_value, freq, w_out, router, w_in, w_down, picks):
    total, d = tokens.shape
    group = lax.axis_size("head")
    ring = lax.axis_size("seq")
    me = lax.axis_index("head")
    me_arr = me.astype(jnp.int32)[None]
    rows = total // group
    experts, _, cap = picks.shape
    wid = w_query.shape[1]

    own = picks[:, 0, :]
    near = [own]
    for k in range(1, group):
        near.append(lax.ppermute(own, "head", [(i, i ^ k) for i in range(group)]))
    block = jnp.arange(group, dtype=jnp.int32)
    slot = block ^ me
    ordered = sum(
        jnp.where((slot == k)[None, :, None], near[k][:, None, :], 0) for k in range(group)
    )
    ordered = ordered + block[None, :, None] * rows
    pick_col = ordered.reshape(experts * group * cap, 1)
    mine_col = lax.dynamic_index_in_dim(
        ordered.reshape(ring, group, group * cap), me, axis=1, keepdims=False
    ).reshape(ring * group * cap, 1)
    pick_row = jnp.pad(own, ((0, 0), (0, PAD - cap)), constant_values=-1).reshape(1, experts * PAD)

    chosen = select_rows(tokens, mine_col, rows).reshape(ring, group * cap, d)
    tok_sel = lax.all_to_all(chosen, "seq", split_axis=0, concat_axis=0, tiled=True)
    tok_sel = tok_sel.reshape(ring * group * cap, d)

    kf, vt, sc, state = key_pass(tokens, w_key, w_value.T, freq, rows)
    pre = prefix_states(state)
    wqt, freq_t = w_query.T, freq.T
    held = query_pass(tokens, wqt, freq_t, kf, vt, sc, rows, 0, 1)
    qft, raw = query_pass(tokens, wqt, freq_t, kf, vt, sc, rows, 1, group - 1, held)
    *attns, sent = norm_pass(me_arr, raw, qft, pre, pick_col, group)

    sent = sent.reshape(experts, group * cap, wid)
    arrived = lax.all_to_all(sent, ("seq", "head"), split_axis=0, concat_axis=0, tiled=True)
    attns = [attns[0]] + [
        lax.ppermute(attns[k], "head", [(i, i ^ k) for i in range(group)]) for k in range(1, group)
    ]
    w_out = w_out.reshape(group, wid, d)
    result = expert_pass(
        arrived.reshape(ring, group, group * cap, wid), tok_sel, w_out, w_in, w_down, cap
    )
    back = lax.all_to_all(
        result.reshape(experts, PAD, d), ("seq", "head"), split_axis=0, concat_axis=0, tiled=True
    )
    hidden, comb = hidden_pass(me_arr, tokens, w_out, router, pick_row, attns, rows)
    return combine_pass(hidden, comb, back.reshape(experts * PAD, d))


def solution(mesh):
    in_specs = (
        P("seq", None),
        P(None, "head"),
        P(None, "head"),
        P(None, "head"),
        P(),
        P(),
        P(),
        P(("seq", "head"), None, None),
        P(("seq", "head"), None, None),
        P(None, ("seq", "head"), None),
    )
    out_specs = P(("seq", "head"), None)
    return jax.shard_map(
        per_device, mesh=mesh, in_specs=in_specs, out_specs=out_specs, check_vma=False
    )
```

time: 248 us -> 132 us (0.53)
  matrix products: 119 us -> 0 us
  Pallas kernels: 0 us -> 38 us
  blocking collectives: 53.8 us -> 18.9 us
  starting transfers between devices: 6.18 us -> 22.9 us
  other arithmetic: 16.6 us -> 1.17 us
  waiting for transfers between devices: 28.3 us -> 16.8 us
  local copies, waits for them, and re-layouts: 22.2 us -> 33.2 us
    dot_general x35 -> x0, matrix products: 119 us -> none  [the longest x2 48.2 us: features(): jnp.einsum('thd,df->thf', split, freq, precision=lax.Precision.HIGHEST)]
    pallas_call x0 -> x8, Pallas kernels: none -> 38 us  [the longest x2 12.7 us: query_pass(): pl.pallas_call(query_kernel, grid=(count,), in_specs=[pl.BlockSpec((rows,...]
    all_gather x1 -> x0, blocking collectives: 36.2 us -> none  [per_device(): lax.all_gather(local_state[None].astype(jnp.bfloat16), 'seq', axis=0, til...]
    unnamed x23 -> x59, local copies, waits for them, and re-layouts: 2.52 us -> 31.4 us
    all_to_all x2, waiting for transfers between devices: 28.3 us -> 0.01 us  [the longest x1 0.01 us: per_device(): lax.all_to_all(result.reshape(experts, PAD, d), ('seq', 'head'), split_ax...]
    ppermute x0 -> x10, waiting for transfers between devices: none -> 16.8 us  [the longest x3 16.8 us: per_device(): lax.ppermute(attns[k], 'head', [(i, i ^ k) for i in range(group)])]
    ppermute x0 -> x10, starting transfers between devices: none -> 16.7 us  [the longest x4 11.7 us: prefix_states(): value = lax.ppermute(held, 'seq', pairs).astype(F32)]
    convert_element_type x3 -> x2, other arithmetic: 14.3 us -> 1.01 us  [the longest x1 0.98 us: prefix_states(): return before.astype(BF)]
  transfers between devices with their start and end apart: 2 -> 12, of which waited for: 2 -> 2; matrix products, arithmetic and copies ran while one was open for 0% -> 3% of each run, Pallas kernels for 0% -> 23%
where the time goes in v1:
time: 132 us; the launch traced here: 131 us
  Pallas kernels  38 us (29%)
  local copies, waits for them, and re-layouts  33.2 us (25%)
  starting transfers between devices  22.9 us (17%)
  blocking collectives  18.9 us (14%)
  waiting for transfers between devices  16.8 us (13%)
    unnamed x59, local copies, waits for them, and re-layouts  31.4 us
    all_to_all x1, blocking collectives, per_device(): lax.all_to_all(sent, ('seq', 'head'), split_axis=0, concat_axis=0, tiled=...  18.9 us
    ppermute x3, waiting for transfers between devices, per_device(): lax.ppermute(attns[k], 'head', [(i, i ^ k) for i in range(group)])  16.8 us
    pallas_call x2, Pallas kernels, query_pass(): pl.pallas_call(query_kernel, grid=(count,), in_specs=[pl.BlockSpec((rows,...  12.7 us
    ppermute x4, starting transfers between devices, prefix_states(): value = lax.ppermute(held, 'seq', pairs).astype(F32)  11.7 us
    pallas_call x1, Pallas kernels, key_pass(): pl.pallas_call(key_kernel, grid=(total // rows,), in_specs=[pl.BlockSpec(...  8.35 us
    pallas_call x1, Pallas kernels, expert_pass(): pl.pallas_call(functools.partial(expert_kernel, cap), grid=(tiles,), in_s...  5.74 us
    pallas_call x1, Pallas kernels, norm_pass(): pl.pallas_call(functools.partial(norm_kernel, slots), grid_spec=pltpu.Pre...  4.6 us
  transfers between devices with their start and end apart: 12, of which 2 were waited for; matrix products, arithmetic and copies ran while one was open for 3% of the time, Pallas kernels for 23%

profile of v1, /device:TPU:0, one launch (start us, length us, event | category | flops | bytes accessed | tf_op | source)
XLA Modules:
  0.0 131.4 jit_solution(12740094993658588095)
XLA Ops:
  0.0 0.7 copy.36
  0.7 0.5 collective-permute-start.4
  1.1 2.5 %collective-permute-start.5 = (s32[32,6]{0,1:T(8,128)S(1)}, s32[32,6]{0,1:T(8,128)S(1)}, u32[]{:S(2)}, u32[]{:S(2)}) collective-permute-start(s32[32,6]{0,1:T(8,128)S(1)} %bitcast.31), channel_id=1, source_target_pairs={{0,2},{1,3},{2,0},{3,1},{4,6},{5,7},{6,4},{7,5},{8,10},{9,11},{10,... | collective-permute-start | bytes 2312 | tf_op jit(solution)/shard_map/ppermute | solution.py:433
  3.6 0.1 collective-permute-start.6
  3.8 1.1 copy.23.wk_ref
  4.9 2.3 %copy-done = bf16[3072,768]{1,0:T(8,128)(2,1)S(1)} copy-done((bf16[3072,768]{1,0:T(8,128)(2,1)S(1)}, bf16[3072,768]{1,0:T(8,128)(2,1)}, u32[]{:S(2)}) %copy-start) | copy-done | bytes 4718616
  7.2 0.8 copy-done.14
  8.0 1.0 copy-done.16
  9.0 8.3 %key_pass.1 = (bf16[3072,768]{1,0:T(8,128)(2,1)S(1)}, bf16[192,3072]{1,0:T(8,128)(2,1)S(1)}, bf16[12,192,256]{2,1,0:T(8,128)(2,1)S(1)}, bf16[192,256]{1,0:T(8,128)(2,1)S(1)}) custom-call(bf16[3072,768]{1,0:T(8,128)(2,1)S(1)} %copy-done, bf16[768,192]{1,0:T(8,128)(2,1)S(1)} %copy.23.wk_ref, bf16[192,768]{1,0:T(8,128)(2,1)S(1)} %bitcast.26, ...), custom_call_target="tpu_custom_call" | custom-call | flops 5000000000 | bytes 12000000 | tf_op jit(solution)/shard_map/key_pass/pallas_call | solution.py:100
  17.3 2.1 %copy-done.4 = bf16[3072,768]{1,0:T(8,128)(2,1)} copy-done((bf16[3072,768]{1,0:T(8,128)(2,1)}, bf16[3072,768]{1,0:T(8,128)(2,1)S(1)}, u32[]{:S(2)}) %copy-start.4) | copy-done | bytes 4718616
  19.5 1.7 %collective-permute-start = (bf16[192,256]{1,0:T(8,128)(2,1)S(1)}, bf16[192,256]{1,0:T(8,128)(2,1)S(1)}, u32[]{:S(2)}, u32[]{:S(2)}) collective-permute-start(bf16[192,256]{1,0:T(8,128)(2,1)S(1)} %get-tuple-element.27), channel_id=1, source_target_pairs={{0,4},{4,0},{8,12},{12,8},{16,20},{20,16},{24,28},{28,24},{1,5},{5... | collective-permute-start | bytes 294920 | tf_op jit(solution)/shard_map/ppermute | solution.py:203
  21.6 2.3 %copy-done.1 = bf16[3072,768]{1,0:T(8,128)(2,1)S(1)} copy-done((bf16[3072,768]{1,0:T(8,128)(2,1)S(1)}, bf16[3072,768]{1,0:T(8,128)(2,1)}, u32[]{:S(2)}) %copy-start.1) | copy-done | bytes 4718616
  23.9 3.8 %query_pass.2 = (bf16[768,3072]{1,0:T(8,128)(2,1)S(1)}, f32[192,3072]{1,0:T(8,128)S(1)}) custom-call(bf16[3072,768]{1,0:T(8,128)(2,1)S(1)} %copy-done.1, bf16[192,768]{1,0:T(8,128)(2,1)S(1)} %bitcast.21, f32[128,64]{1,0:T(8,128)S(1)} %bitcast.23, bf16[3072,768]{1,0:T(8,128)(2,1)} %copy-done.4, bf16[192,3072]{1,0:T(8,128)(2,1)S(1)} %get-tuple-element.21.vt_ref, ...), custom_call_target="tpu_custom_call" | custom-call | flops 1500000000 | bytes 4000000 | tf_op jit(solution)/shard_map/query_pass/pallas_call | solution.py:162
  27.8 8.8 %query_pass.3 = (bf16[768,3072]{1,0:T(8,128)(2,1)S(1)}, f32[192,3072]{1,0:T(8,128)S(1)}) custom-call(bf16[3072,768]{1,0:T(8,128)(2,1)S(1)} %copy-done.1, bf16[192,768]{1,0:T(8,128)(2,1)S(1)} %bitcast.22, f32[128,64]{1,0:T(8,128)S(1)} %bitcast.24, bf16[3072,768]{1,0:T(8,128)(2,1)} %copy-done.4, ...), custom_call_target="tpu_custom_call", output_to_operand_aliasing={{0}: (6, {}), {1}: (7, {})} | custom-call | flops 4499999744 | bytes 12000000 | tf_op jit(solution)/shard_map/query_pass/pallas_call | solution.py:162
  36.6 2.1 %copy-done.7 = bf16[768,3072]{1,0:T(8,128)(2,1)} copy-done((bf16[768,3072]{1,0:T(8,128)(2,1)}, bf16[768,3072]{1,0:T(8,128)(2,1)S(1)}, u32[]{:S(2)}) %copy-start.7) | copy-done | bytes 4718616
  38.8 1.4 %copy-done.9 = f32[192,3072]{1,0:T(8,128)} copy-done((f32[192,3072]{1,0:T(8,128)}, f32[192,3072]{1,0:T(8,128)S(1)}, u32[]{:S(2)}) %copy-start.9) | copy-done | bytes 2359320
  40.7 0.1 broadcast_in_dim.119
  41.2 0.1 add_add_fusion
  41.8 3.5 %collective-permute-start.1 = (bf16[192,256]{1,0:T(8,128)(2,1)S(1)}, bf16[192,256]{1,0:T(8,128)(2,1)S(1)}, u32[]{:S(2)}, u32[]{:S(2)}) collective-permute-start(bf16[192,256]{1,0:T(8,128)(2,1)S(1)} %fusion.4), channel_id=1, source_target_pairs={{0,8},{4,12},{16,24},{20,28},{1,9},{5,13},{17,25},{21,29},{2,10},{... | collective-permute-start | bytes 294920 | tf_op jit(solution)/shard_map/ppermute | solution.py:203
  45.3 4.5 %collective-permute-start.2 = (bf16[192,256]{1,0:T(8,128)(2,1)S(1)}, bf16[192,256]{1,0:T(8,128)(2,1)S(1)}, u32[]{:S(2)}, u32[]{:S(2)}) collective-permute-start(bf16[192,256]{1,0:T(8,128)(2,1)S(1)} %fusion.4), channel_id=1, source_target_pairs={{0,16},{4,20},{8,24},{12,28},{1,17},{5,21},{9,25},{13,29},{2,18},{... | collective-permute-start | bytes 294920 | tf_op jit(solution)/shard_map/ppermute | solution.py:203
  49.8 1.9 %collective-permute-start.3 = (bf16[192,256]{1,0:T(8,128)(2,1)S(1)}, bf16[192,256]{1,0:T(8,128)(2,1)}, u32[]{:S(2)}, u32[]{:S(2)}) collective-permute-start(bf16[192,256]{1,0:T(8,128)(2,1)S(1)} %fusion.4), channel_id=1, source_target_pairs={{0,24},{4,28},{8,16},{12,20},{1,25},{5,29},{9,17},{13,21},{2,26},{... | collective-permute-start | bytes 294920 | tf_op jit(solution)/shard_map/ppermute | solution.py:203
  51.7 0.2 reshape.187.pick_ref
  52.0 2.3 %copy-done.2 = bf16[3072,768]{1,0:T(8,128)(2,1)S(1)} copy-done((bf16[3072,768]{1,0:T(8,128)(2,1)S(1)}, bf16[3072,768]{1,0:T(8,128)(2,1)}, u32[]{:S(2)}) %copy-start.2) | copy-done | bytes 4718616
  54.4 2.8 %select_rows.1 = bf16[192,768]{1,0:T(8,128)(2,1)} custom-call(bf16[3072,768]{1,0:T(8,128)(2,1)S(1)} %copy-done.2, s32[192,1]{1,0:T(8,128)S(1)} %reshape.188.pick_ref), custom_call_target="tpu_custom_call" | custom-call | flops 1000000000 | bytes 5000000 | tf_op jit(solution)/shard_map/select_rows/pallas_call | solution.py:294
  57.2 3.4 %all-to-all-start.1 = ((bf16[8,24,768]{2,1,0:T(8,128)(2,1)}), bf16[8,24,768]{2,1,0:T(8,128)(2,1)S(1)}, u32[]{:S(2)}, u32[]{:S(2)}) async-start(bf16[8,24,768]{2,1,0:T(8,128)(2,1)} %bitcast.7), calls=%async_computation.1 | async-start | bytes 589824 | tf_op jit(solution)/shard_map/all_to_all | solution.py:447
  60.6 1.0 fusion.3.pre_ref
  61.6 2.3 %copy-done.8 = bf16[768,3072]{1,0:T(8,128)(2,1)S(1)} copy-done((bf16[768,3072]{1,0:T(8,128)(2,1)S(1)}, bf16[768,3072]{1,0:T(8,128)(2,1)}, u32[]{:S(2)}) %copy-start.8) | copy-done | bytes 4718616
  64.0 4.6 %norm_pass.1 = (bf16[192,768]{1,0:T(8,128)(2,1)S(1)}, bf16[192,768]{1,0:T(8,128)(2,1)S(1)}, bf16[192,768]{1,0:T(8,128)(2,1)S(1)}, bf16[192,768]{1,0:T(8,128)(2,1)S(1)}, bf16[768,192]{1,0:T(8,128)(2,1)S(1)}) custom-call(s32[1]{0:T(128)} %bitcast.me_ref, f32[192,3072]{1,0:T(8,128)S(1)} %copy-done.10, bf16[768,3072]{1,0:T(8,128)(2,1)S(1)} %copy-done.8, ...), custom_call_target="tpu_custom_call" | custom-call | flops 3000000000 | bytes 8000000 | tf_op jit(solution)/shard_map/norm_pass/pallas_call | solution.py:252
  68.6 0.7 copy-done.17
  69.3 0.7 copy-done.19
  70.0 0.7 copy-done.21
  70.7 0.7 copy-done.23
  71.5 18.9 %all_to_all.15 = bf16[32,24,192]{2,1,0:T(8,128)(2,1)S(1)} all-to-all(bf16[32,24,192]{2,1,0:T(8,128)(2,1)S(1)} %bitcast.25), channel_id=1, replica_groups=mesh['seq'=8,'head'=4] {'seq','head'}, dimensions={0} | all-to-all | bytes 589824 | tf_op jit(solution)/shard_map/all_to_all | solution.py:458
  90.4 2.3 %copy-done.5 = bf16[1,768,3072]{2,1,0:T(8,128)(2,1)S(1)} copy-done((bf16[1,768,3072]{2,1,0:T(8,128)(2,1)S(1)}, bf16[1,768,3072]{2,1,0:T(8,128)(2,1)}, u32[]{:S(2)}) %copy-start.5) | copy-done | bytes 4718616
  92.7 2.3 %copy-done.6 = bf16[1,3072,768]{2,1,0:T(8,128)(2,1)S(1)} copy-done((bf16[1,3072,768]{2,1,0:T(8,128)(2,1)S(1)}, bf16[1,3072,768]{2,1,0:T(8,128)(2,1)}, u32[]{:S(2)}) %copy-start.6) | copy-done | bytes 4718616
  95.1 1.3 copy-done.11
  96.3 5.7 %expert_pass.1 = bf16[256,768]{1,0:T(8,128)(2,1)} custom-call(bf16[8,4,24,192]{3,2,1,0:T(8,128)(2,1)S(1)} %bitcast.16, bf16[192,768]{1,0:T(8,128)(2,1)S(1)} %bitcast.18, bf16[4,192,768]{2,1,0:T(8,128)(2,1)S(1)} %bitcast.19, bf16[1,768,3072]{2,1,0:T(8,128)(2,1)S(1)} %copy-done.5, bf16[1,3072,768]{2,1,0:T(8,128)(2,1)S(1)} %copy-done.6), custom_call_target="tpu_custom_call" | custom-call | flops 2000000000 | bytes 12000000 | tf_op jit(solution)/shard_map/expert_pass/pallas_call | solution.py:336
  102.1 2.8 %all-to-all-start.2 = ((bf16[32,8,768]{2,1,0:T(8,128)(2,1)}), bf16[32,8,768]{2,1,0:T(8,128)(2,1)S(1)}, u32[]{:S(2)}, u32[]{:S(2)}) async-start(bf16[32,8,768]{2,1,0:T(8,128)(2,1)} %bitcast.9), calls=%async_computation.2 | async-start | bytes 786432 | tf_op jit(solution)/shard_map/all_to_all | solution.py:466
  104.9 0.1 collective-permute-start.7
  105.1 1.7 %collective-permute-start.8 = (bf16[192,768]{1,0:T(8,128)(2,1)S(1)}, bf16[192,768]{1,0:T(8,128)(2,1)S(1)}, u32[]{:S(2)}, u32[]{:S(2)}) collective-permute-start(bf16[192,768]{1,0:T(8,128)(2,1)S(1)} %copy-done.20), channel_id=1, source_target_pairs={{0,2},{1,3},{2,0},{3,1},{4,6},{5,7},{6,4},{7,5},{8,10},{9,11},{10,... | collective-permute-start | bytes 884744 | tf_op jit(solution)/shard_map/ppermute | solution.py:460
  106.7 0.1 collective-permute-start.9
  107.0 0.2 copy.29.router_ref
  107.1 11.5 %collective-permute-done.8.rest_2_ = bf16[192,768]{1,0:T(8,128)(2,1)S(1)} collective-permute-done((bf16[192,768]{1,0:T(8,128)(2,1)S(1)}, bf16[192,768]{1,0:T(8,128)(2,1)S(1)}, u32[]{:S(2)}, u32[]{:S(2)}) %collective-permute-start.8) | collective-permute-done | bytes 294944 | tf_op jit(solution)/shard_map/ppermute | solution.py:460
  118.6 5.4 %collective-permute-done.9.rest_3_ = bf16[192,768]{1,0:T(8,128)(2,1)S(1)} collective-permute-done((bf16[192,768]{1,0:T(8,128)(2,1)S(1)}, bf16[192,768]{1,0:T(8,128)(2,1)S(1)}, u32[]{:S(2)}, u32[]{:S(2)}) %collective-permute-start.9) | collective-permute-done | bytes 294944 | tf_op jit(solution)/shard_map/ppermute | solution.py:460
  124.0 2.3 %copy-done.3 = bf16[3072,768]{1,0:T(8,128)(2,1)S(1)} copy-done((bf16[3072,768]{1,0:T(8,128)(2,1)S(1)}, bf16[3072,768]{1,0:T(8,128)(2,1)}, u32[]{:S(2)}) %copy-start.3) | copy-done | bytes 4718616
  126.3 1.3 copy-done.12
  127.6 2.4 %hidden_pass.1 = (bf16[768,768]{1,0:T(8,128)(2,1)S(1)}, bf16[768,256]{1,0:T(8,128)(2,1)S(1)}) custom-call(s32[1]{0:T(128)} %bitcast.me_ref, bf16[3072,768]{1,0:T(8,128)(2,1)S(1)} %copy-done.3, bf16[4,192,768]{2,1,0:T(8,128)(2,1)S(1)} %bitcast.20, bf16[768,32]{1,0:T(8,128)(2,1)S(1)} %copy.29.router_ref, s32[1,256]{1,0:T(1,128)S(1)} %reshape.178.pick_ref, ...), custom_call_target="tpu_custom_call" | custom-call | flops 2000000000 | bytes 6000000 | tf_op jit(solution)/shard_map/hidden_pass/pallas_call | solution.py:375
  130.0 1.5 %combine_pass.1 = bf16[768,768]{1,0:T(8,128)(2,1)} custom-call(bf16[768,768]{1,0:T(8,128)(2,1)S(1)} %get-tuple-element.32.hid_ref, bf16[768,256]{1,0:T(8,128)(2,1)S(1)} %get-tuple-element.33.comb_ref, bf16[256,768]{1,0:T(8,128)(2,1)S(1)} %bitcast.17), custom_call_target="tpu_custom_call" | custom-call | flops 500000000 | bytes 4000000 | tf_op jit(solution)/shard_map/combine_pass/pallas_call | solution.py:404
  (76 shorter events, 2.0 us)
Async XLA Ops:
  0.7 40.3 %collective-permute-start.4 = (s32[32,6]{0,1:T(8,128)S(1)}, s32[32,6]{0,1:T(8,128)S(1)}, u32[]{:S(2)}, u32[]{:S(2)}) collective-permute-start(s32[32,6]{0,1:T(8,128)S(1)} %bitcast.30), channel_id=1, source_target_pairs={{0,1},{1,0},{2,3},{3,2},{4,5},{5,4},{6,7},{7,6},{8,9},{9,8},{10,11... | collective-permute-start | bytes 2312 | tf_op jit(solution)/shard_map/ppermute | solution.py:433
  1.1 39.9 %collective-permute-start.5 = (s32[32,6]{0,1:T(8,128)S(1)}, s32[32,6]{0,1:T(8,128)S(1)}, u32[]{:S(2)}, u32[]{:S(2)}) collective-permute-start(s32[32,6]{0,1:T(8,128)S(1)} %bitcast.31), channel_id=1, source_target_pairs={{0,2},{1,3},{2,0},{3,1},{4,6},{5,7},{6,4},{7,5},{8,10},{9,11},{10,... | collective-permute-start | bytes 2312 | tf_op jit(solution)/shard_map/ppermute | solution.py:433
  3.6 37.5 %collective-permute-start.6 = (s32[32,6]{0,1:T(8,128)S(1)}, s32[32,6]{0,1:T(8,128)S(1)}, u32[]{:S(2)}, u32[]{:S(2)}) collective-permute-start(s32[32,6]{0,1:T(8,128)S(1)} %bitcast.32), channel_id=1, source_target_pairs={{0,3},{1,2},{2,1},{3,0},{4,7},{5,6},{6,5},{7,4},{8,11},{9,10},{10,... | collective-permute-start | bytes 2312 | tf_op jit(solution)/shard_map/ppermute | solution.py:433
  4.9 2.3 %copy-start = (bf16[3072,768]{1,0:T(8,128)(2,1)S(1)}, bf16[3072,768]{1,0:T(8,128)(2,1)}, u32[]{:S(2)}) copy-start(bf16[3072,768]{1,0:T(8,128)(2,1)} %tok_ref.9) | copy-start | bytes 14155780
  7.2 0.8 copy-start.14
  8.0 1.0 copy-start.16
  9.0 12.2 %copy-start.15 = (f32[64,128]{1,0:T(8,128)S(1)}, f32[64,128]{1,0:T(8,128)}, u32[]{:S(2)}) copy-start(f32[64,128]{1,0:T(8,128)} %freq_ref.1) | copy-start | bytes 98308
  9.0 12.4 %copy-start.26 = (s32[32,1,6]{0,1,2:T(1,128)S(1)}, s32[32,1,6]{0,1,2:T(1,128)}, u32[]{:S(2)}) copy-start(s32[32,1,6]{0,1,2:T(1,128)} %param.19) | copy-start | bytes 2308
  9.0 12.6 %copy-start.13 = (bf16[768,192]{0,1:T(8,128)(2,1)S(1)}, bf16[768,192]{0,1:T(8,128)(2,1)}, u32[]{:S(2)}) copy-start(bf16[768,192]{0,1:T(8,128)(2,1)} %param.11) | copy-start | bytes 884740
  17.3 2.1 %copy-start.4 = (bf16[3072,768]{1,0:T(8,128)(2,1)}, bf16[3072,768]{1,0:T(8,128)(2,1)S(1)}, u32[]{:S(2)}) copy-start(bf16[3072,768]{1,0:T(8,128)(2,1)S(1)} %get-tuple-element.20.kf_ref) | copy-start | bytes 14155780
  19.5 22.2 %collective-permute-start = (bf16[192,256]{1,0:T(8,128)(2,1)S(1)}, bf16[192,256]{1,0:T(8,128)(2,1)S(1)}, u32[]{:S(2)}, u32[]{:S(2)}) collective-permute-start(bf16[192,256]{1,0:T(8,128)(2,1)S(1)} %get-tuple-element.27), channel_id=1, source_target_pairs={{0,4},{4,0},{8,12},{12,8},{16,20},{20,16},{24,28},{28,24},{1,5},{5... | collective-permute-start | bytes 294920 | tf_op jit(solution)/shard_map/ppermute | solution.py:203
  21.6 2.3 %copy-start.1 = (bf16[3072,768]{1,0:T(8,128)(2,1)S(1)}, bf16[3072,768]{1,0:T(8,128)(2,1)}, u32[]{:S(2)}) copy-start(bf16[3072,768]{1,0:T(8,128)(2,1)} %tok_ref.9) | copy-start | bytes 14155780
  36.6 2.1 %copy-start.7 = (bf16[768,3072]{1,0:T(8,128)(2,1)}, bf16[768,3072]{1,0:T(8,128)(2,1)S(1)}, u32[]{:S(2)}) copy-start(bf16[768,3072]{1,0:T(8,128)(2,1)S(1)} %get-tuple-element.26.qft_ref) | copy-start | bytes 14155780
  38.8 1.4 %copy-start.9 = (f32[192,3072]{1,0:T(8,128)}, f32[192,3072]{1,0:T(8,128)S(1)}, u32[]{:S(2)}) copy-start(f32[192,3072]{1,0:T(8,128)S(1)} %get-tuple-element.25.raw_ref) | copy-start | bytes 7077892
  41.8 18.8 %collective-permute-start.1 = (bf16[192,256]{1,0:T(8,128)(2,1)S(1)}, bf16[192,256]{1,0:T(8,128)(2,1)S(1)}, u32[]{:S(2)}, u32[]{:S(2)}) collective-permute-start(bf16[192,256]{1,0:T(8,128)(2,1)S(1)} %fusion.4), channel_id=1, source_target_pairs={{0,8},{4,12},{16,24},{20,28},{1,9},{5,13},{17,25},{21,29},{2,10},{... | collective-permute-start | bytes 294920 | tf_op jit(solution)/shard_map/ppermute | solution.py:203
  45.3 15.4 %collective-permute-start.2 = (bf16[192,256]{1,0:T(8,128)(2,1)S(1)}, bf16[192,256]{1,0:T(8,128)(2,1)S(1)}, u32[]{:S(2)}, u32[]{:S(2)}) collective-permute-start(bf16[192,256]{1,0:T(8,128)(2,1)S(1)} %fusion.4), channel_id=1, source_target_pairs={{0,16},{4,20},{8,24},{12,28},{1,17},{5,21},{9,25},{13,29},{2,18},{... | collective-permute-start | bytes 294920 | tf_op jit(solution)/shard_map/ppermute | solution.py:203
  49.8 10.8 %collective-permute-start.3 = (bf16[192,256]{1,0:T(8,128)(2,1)S(1)}, bf16[192,256]{1,0:T(8,128)(2,1)}, u32[]{:S(2)}, u32[]{:S(2)}) collective-permute-start(bf16[192,256]{1,0:T(8,128)(2,1)S(1)} %fusion.4), channel_id=1, source_target_pairs={{0,24},{4,28},{8,16},{12,20},{1,25},{5,29},{9,17},{13,21},{2,26},{... | collective-permute-start | bytes 294920 | tf_op jit(solution)/shard_map/ppermute | solution.py:203
  52.0 2.3 %copy-start.2 = (bf16[3072,768]{1,0:T(8,128)(2,1)S(1)}, bf16[3072,768]{1,0:T(8,128)(2,1)}, u32[]{:S(2)}) copy-start(bf16[3072,768]{1,0:T(8,128)(2,1)} %tok_ref.9) | copy-start | bytes 14155780
  54.4 7.3 %copy-start.10 = (f32[192,3072]{1,0:T(8,128)S(1)}, f32[192,3072]{1,0:T(8,128)}, u32[]{:S(2)}) copy-start(f32[192,3072]{1,0:T(8,128)} %copy-done.9) | copy-start | bytes 7077892
  57.2 14.3 %all-to-all-start.1 = ((bf16[8,24,768]{2,1,0:T(8,128)(2,1)}), bf16[8,24,768]{2,1,0:T(8,128)(2,1)S(1)}, u32[]{:S(2)}, u32[]{:S(2)}) async-start(bf16[8,24,768]{2,1,0:T(8,128)(2,1)} %bitcast.7), calls=%async_computation.1 | async-start | bytes 589824 | tf_op jit(solution)/shard_map/all_to_all | solution.py:447
  61.6 2.3 %copy-start.8 = (bf16[768,3072]{1,0:T(8,128)(2,1)S(1)}, bf16[768,3072]{1,0:T(8,128)(2,1)}, u32[]{:S(2)}) copy-start(bf16[768,3072]{1,0:T(8,128)(2,1)} %copy-done.7) | copy-start | bytes 14155780
  68.6 0.7 copy-start.17
  69.3 0.7 copy-start.19
  70.0 0.7 copy-start.21
  70.7 0.7 copy-start.23
  90.4 2.3 %copy-start.5 = (bf16[1,768,3072]{2,1,0:T(8,128)(2,1)S(1)}, bf16[1,768,3072]{2,1,0:T(8,128)(2,1)}, u32[]{:S(2)}) copy-start(bf16[1,768,3072]{2,1,0:T(8,128)(2,1)} %wi_ref.1) | copy-start | bytes 14155780
  92.7 2.3 %copy-start.6 = (bf16[1,3072,768]{2,1,0:T(8,128)(2,1)S(1)}, bf16[1,3072,768]{2,1,0:T(8,128)(2,1)}, u32[]{:S(2)}) copy-start(bf16[1,3072,768]{2,1,0:T(8,128)(2,1)} %wd_ref.1) | copy-start | bytes 14155780
  95.1 1.3 copy-start.11
  96.3 8.6 %copy-start.22 = (bf16[192,768]{1,0:T(8,128)(2,1)S(1)}, bf16[192,768]{1,0:T(8,128)(2,1)}, u32[]{:S(2)}) copy-start(bf16[192,768]{1,0:T(8,128)(2,1)} %copy-done.21) | copy-start | bytes 884740
  96.3 8.7 %copy-start.20 = (bf16[192,768]{1,0:T(8,128)(2,1)S(1)}, bf16[192,768]{1,0:T(8,128)(2,1)}, u32[]{:S(2)}) copy-start(bf16[192,768]{1,0:T(8,128)(2,1)} %copy-done.19) | copy-start | bytes 884740
  96.3 10.4 %copy-start.18 = (bf16[192,768]{1,0:T(8,128)(2,1)S(1)}, bf16[192,768]{1,0:T(8,128)(2,1)}, u32[]{:S(2)}) copy-start(bf16[192,768]{1,0:T(8,128)(2,1)} %copy-done.17) | copy-start | bytes 884740
  96.3 10.6 %copy-start.25 = (bf16[768,32]{0,1:T(8,128)(2,1)S(1)}, bf16[768,32]{0,1:T(8,128)(2,1)}, u32[]{:S(2)}) copy-start(bf16[768,32]{0,1:T(8,128)(2,1)} %param.16) | copy-start | bytes 147460
  96.3 27.6 %copy-start.24 = (bf16[192,768]{1,0:T(8,128)(2,1)S(1)}, bf16[192,768]{1,0:T(8,128)(2,1)}, u32[]{:S(2)}) copy-start(bf16[192,768]{1,0:T(8,128)(2,1)} %copy-done.23) | copy-start | bytes 884740
  102.1 27.9 %all-to-all-start.2 = ((bf16[32,8,768]{2,1,0:T(8,128)(2,1)}), bf16[32,8,768]{2,1,0:T(8,128)(2,1)S(1)}, u32[]{:S(2)}, u32[]{:S(2)}) async-start(bf16[32,8,768]{2,1,0:T(8,128)(2,1)} %bitcast.9), calls=%async_computation.2 | async-start | bytes 786432 | tf_op jit(solution)/shard_map/all_to_all | solution.py:466
  104.9 2.2 %collective-permute-start.7 = (bf16[192,768]{1,0:T(8,128)(2,1)S(1)}, bf16[192,768]{1,0:T(8,128)(2,1)S(1)}, u32[]{:S(2)}, u32[]{:S(2)}) collective-permute-start(bf16[192,768]{1,0:T(8,128)(2,1)S(1)} %copy-done.22), channel_id=1, source_target_pairs={{0,1},{1,0},{2,3},{3,2},{4,5},{5,4},{6,7},{7,6},{8,9},{9,8},{10,11... | collective-permute-start | bytes 884744 | tf_op jit(solution)/shard_map/ppermute | solution.py:460
  105.1 13.5 %collective-permute-start.8 = (bf16[192,768]{1,0:T(8,128)(2,1)S(1)}, bf16[192,768]{1,0:T(8,128)(2,1)S(1)}, u32[]{:S(2)}, u32[]{:S(2)}) collective-permute-start(bf16[192,768]{1,0:T(8,128)(2,1)S(1)} %copy-done.20), channel_id=1, source_target_pairs={{0,2},{1,3},{2,0},{3,1},{4,6},{5,7},{6,4},{7,5},{8,10},{9,11},{10,... | collective-permute-start | bytes 884744 | tf_op jit(solution)/shard_map/ppermute | solution.py:460
  106.7 17.2 %collective-permute-start.9 = (bf16[192,768]{1,0:T(8,128)(2,1)S(1)}, bf16[192,768]{1,0:T(8,128)(2,1)S(1)}, u32[]{:S(2)}, u32[]{:S(2)}) collective-permute-start(bf16[192,768]{1,0:T(8,128)(2,1)S(1)} %copy-done.18), channel_id=1, source_target_pairs={{0,3},{1,2},{2,1},{3,0},{4,7},{5,6},{6,5},{7,4},{8,11},{9,10},{10,... | collective-permute-start | bytes 884744 | tf_op jit(solution)/shard_map/ppermute | solution.py:460
  124.0 2.3 %copy-start.3 = (bf16[3072,768]{1,0:T(8,128)(2,1)S(1)}, bf16[3072,768]{1,0:T(8,128)(2,1)}, u32[]{:S(2)}) copy-start(bf16[3072,768]{1,0:T(8,128)(2,1)} %tok_ref.9) | copy-start | bytes 14155780
  126.3 1.3 copy-start.12

commit v2 on v1

v2 whole, which is shorter than its diff:
```python
import functools
import math

import jax
import jax.numpy as jnp
from jax import lax
from jax.experimental import pallas as pl
from jax.experimental.pallas import tpu as pltpu
from jax.sharding import PartitionSpec as P

HD = 64
EPS = 1e-06
CHUNK = 256
PAD = 8
BF = jnp.bfloat16
F32 = jnp.float32
MIB = 2**20
SIN = (3.14158202, -5.16714279, 2.54189901, -0.55463616)
COS = (0.9999933, -4.93393802, 4.04128381, -1.22212701)


def nn(a, b):
    return lax.dot_general(a, b, (((1,), (0,)), ((), ())), preferred_element_type=F32)


def nt(a, b):
    return lax.dot_general(a, b, (((1,), (1,)), ((), ())), preferred_element_type=F32)


def tn(a, b):
    return lax.dot_general(a, b, (((0,), (0,)), ((), ())), preferred_element_type=F32)


def wave(turns, scale):
    big = F32(1.5 * 2.0**23)
    r = turns - ((turns + big) - big)
    u = r * r
    root = math.sqrt(2 * scale)
    a = [F32(v * root) for v in SIN]
    b = [F32(v * root) for v in COS]
    s = r * (a[0] + u * (a[1] + u * (a[2] + u * a[3])))
    c = b[0] + u * (b[1] + u * (b[2] + u * b[3]))
    return F32(scale) - s * s, s * c


def parts(f):
    hi = f.astype(BF)
    rest = f - hi.astype(F32)
    mid = rest.astype(BF)
    lo = (rest - mid.astype(F32)).astype(BF)
    return [hi, mid, lo]


def whole(shape):
    return pl.BlockSpec(shape, lambda *_: (0,) * len(shape))


def params(mib=60):
    return pltpu.CompilerParams(vmem_limit_bytes=mib * MIB)


def cost(flops, nbytes):
    return pl.CostEstimate(flops=int(flops), bytes_accessed=int(nbytes), transcendentals=0)


def key_kernel(tok_ref, wkt_ref, wvt_ref, freq_ref, kf_ref, vt_ref, sc_ref, tot_ref, f3, st):
    heads = wkt_ref.shape[0] // HD
    half = freq_ref.shape[1]

    @pl.when(pl.program_id(0) == 0)
    def _():
        f3[...] = jnp.concatenate(parts(freq_ref[...] * F32(0.5 / math.pi)), axis=0)
        st[...] = jnp.zeros_like(st)

    tok = tok_ref[...]
    k = nt(tok, wkt_ref[...]).astype(BF)
    vt = nt(wvt_ref[...], tok).astype(BF)
    vt_ref[...] = vt
    for h in range(heads):
        kh = k[:, h * HD : (h + 1) * HD]
        phase = nn(jnp.concatenate([kh] * 3, axis=1), f3[...])
        c, s = wave(phase, 1 / math.sqrt(half))
        kf = jnp.concatenate([c.astype(BF), s.astype(BF)], axis=1)
        kf_ref[:, h * 2 * half : (h + 1) * 2 * half] = kf
        mine = slice(h * HD, (h + 1) * HD)
        acc = st[mine, :]
        for j in range(tok.shape[0] // CHUNK):
            sc_ref[j, mine, :] = acc.astype(BF)
            rows = slice(j * CHUNK, (j + 1) * CHUNK)
            acc = acc + nn(vt[mine, rows], kf[rows])
        st[mine, :] = acc

    @pl.when(pl.program_id(0) == pl.num_programs(0) - 1)
    def _():
        state = st[...].astype(BF)
        for i in range(tot_ref.shape[0]):
            tot_ref[i] = state


def key_pass(tokens, wkt, wvt, freq, rows, copies):
    total, d = tokens.shape
    wid = wkt.shape[0]
    feat = 2 * freq.shape[1]
    heads = wid // HD
    return pl.pallas_call(
        key_kernel,
        grid=(total // rows,),
        in_specs=[
            pl.BlockSpec((rows, d), lambda i: (i, 0)),
            whole(wkt.shape),
            whole(wvt.shape),
            whole(freq.shape),
        ],
        out_specs=[
            pl.BlockSpec((rows, heads * feat), lambda i: (i, 0)),
            pl.BlockSpec((wid, rows), lambda i: (0, i)),
            pl.BlockSpec((rows // CHUNK, wid, feat), lambda i: (i, 0, 0)),
            whole((copies, wid, feat)),
        ],
        out_shape=[
            jax.ShapeDtypeStruct((total, heads * feat), BF),
            jax.ShapeDtypeStruct((wid, total), BF),
            jax.ShapeDtypeStruct((total // CHUNK, wid, feat), BF),
            jax.ShapeDtypeStruct((copies, wid, feat), BF),
        ],
        scratch_shapes=[pltpu.VMEM((3 * HD, freq.shape[1]), BF), pltpu.VMEM((wid, feat), F32)],
        compiler_params=params(),
        cost_estimate=cost(5e9, 12e6),
        name="key_pass",
    )(tokens, wkt, wvt, freq)


def chosen(slot, pick_refs):
    row = pick_refs[0][...]
    for k in range(1, len(pick_refs)):
        row = jnp.where(slot == k, pick_refs[k][...], row)
    return row


def marks(row, rows):
    at = lax.broadcasted_iota(jnp.int32, (rows, row.shape[1]), 0)
    return (at == row).astype(F32).astype(BF)


def query_kernel(slots, me_ref, tok_ref, wqt_ref, ft_ref, kf_ref, vt_ref, sc_ref, *rest):
    pick_refs = rest[:slots]
    qft_ref, raw_ref, seen_ref, f3t, both_w = rest[slots:]
    wid, d = wqt_ref.shape
    heads = wid // HD
    half = ft_ref.shape[0]
    feat = 2 * half
    step = pl.program_id(0)

    @pl.when(step == 0)
    def _():
        f3t[...] = jnp.concatenate(parts(ft_ref[...] * F32(0.5 / math.pi)), axis=1)
        both_w[:wid] = wqt_ref[...]
        line = lax.broadcasted_iota(jnp.int32, (wid, d), 0)
        column = lax.broadcasted_iota(jnp.int32, (wid, d), 1)
        both_w[wid:] = (line + me_ref[0] * wid == column).astype(F32).astype(BF)

    tok = tok_ref[...]
    out = nt(both_w[...], tok).astype(BF)
    qt = out[:wid]
    seen_ref[0] = nn(out[wid:], marks(chosen(me_ref[0] ^ step, pick_refs), tok.shape[0])).astype(BF)
    place = [lax.broadcasted_iota(jnp.int32, (CHUNK, CHUNK), i) for i in (0, 1)]
    keep = place[0] <= place[1]
    for h in range(heads):
        mine = slice(h * HD, (h + 1) * HD)
        phase = nn(f3t[...], jnp.concatenate([qt[mine]] * 3, axis=0))
        c, s = wave(phase, 1 / math.sqrt(half))
        qf = jnp.concatenate([c.astype(BF), s.astype(BF)], axis=0)
        qft_ref[h * feat : (h + 1) * feat, :] = qf
        for j in range(tok.shape[0] // CHUNK):
            cols = slice(j * CHUNK, (j + 1) * CHUNK)
            both = jnp.concatenate([kf_ref[cols, h * feat : (h + 1) * feat], sc_ref[j, mine, :]], axis=0)
            both = nn(both, qf[:, cols])
            scores = jnp.where(keep, both[:CHUNK], 0.0).astype(BF)
            raw_ref[mine, cols] = nn(vt_ref[mine, cols], scores) + both[CHUNK:]


def query_pass(me, tokens, wqt, freq_t, kf, vt, sc, picks):
    total, d = tokens.shape
    slots = len(picks)
    rows = total // slots
    n = picks[0].shape[1]
    wid = wqt.shape[0]
    feat = 2 * freq_t.shape[0]
    heads = wid // HD
    return pl.pallas_call(
        functools.partial(query_kernel, slots),
        grid_spec=pltpu.PrefetchScalarGridSpec(
            num_scalar_prefetch=1,
            grid=(slots,),
            in_specs=[
                pl.BlockSpec((rows, d), lambda i, m: (i, 0)),
                whole(wqt.shape),
                whole(freq_t.shape),
                pl.BlockSpec((rows, heads * feat), lambda i, m: (i, 0)),
                pl.BlockSpec((wid, rows), lambda i, m: (0, i)),
                pl.BlockSpec((rows // CHUNK, wid, feat), lambda i, m: (i, 0, 0)),
            ]
            + [whole(p.shape) for p in picks],
            out_specs=[
                pl.BlockSpec((heads * feat, rows), lambda i, m: (0, i)),
                pl.BlockSpec((wid, rows), lambda i, m: (0, i)),
                pl.BlockSpec((1, wid, n), lambda i, m: (i, 0, 0)),
            ],
            scratch_shapes=[pltpu.VMEM((freq_t.shape[0], 3 * HD), BF), pltpu.VMEM((2 * wid, d), BF)],
        ),
        out_shape=[
            jax.ShapeDtypeStruct((heads * feat, total), BF),
            jax.ShapeDtypeStruct((wid, total), F32),
            jax.ShapeDtypeStruct((slots, wid, n), BF),
        ],
        compiler_params=params(),
        cost_estimate=cost(6e9, 16e6),
        name="query_pass",
    )(me, tokens, wqt, freq_t, kf, vt, sc, *picks)


def norm_kernel(slots, cap, me_ref, raw_ref, qft_ref, states_ref, seen_ref, *rest):
    pick_refs, outs = rest[:slots], rest[slots : 2 * slots]
    sent_ref, acc, pre_ref = rest[2 * slots :]
    step = pl.program_id(0)
    block = me_ref[0] ^ step
    heads = raw_ref.shape[0] // HD
    feat = pre_ref.shape[1]

    @pl.when(step == 0)
    def _():
        before = jnp.zeros(pre_ref.shape, F32)
        for i in range(states_ref.shape[0]):
            before = before + jnp.where(i < me_ref[1], states_ref[i].astype(F32), 0.0)
        pre_ref[...] = before.astype(BF)
        acc[...] = jnp.zeros_like(acc)

    normed = []
    for h in range(heads):
        mine = slice(h * HD, (h + 1) * HD)
        raw = raw_ref[mine, :] + nn(pre_ref[mine, :], qft_ref[h * feat : (h + 1) * feat, :])
        meansq = jnp.mean(raw * raw, axis=0, keepdims=True)
        normed.append((raw * lax.rsqrt(meansq + F32(EPS))).astype(BF))
    attn = jnp.concatenate(normed, axis=0)
    for k in range(slots):

        @pl.when(step == k)
        def _():
            outs[k][...] = attn

    picked = nn(attn, marks(chosen(step, pick_refs), attn.shape[1])).astype(BF)
    both = jnp.concatenate([picked, seen_ref[0]], axis=0)
    n = both.shape[1]
    experts = n // cap
    at = lax.broadcasted_iota(jnp.int32, (1, n), 1)
    row = (at % experts * slots + block) * cap + at // experts
    acc[...] += nt(marks(row, acc.shape[0]), both)

    @pl.when(step == slots - 1)
    def _():
        sent_ref[...] = acc[...].astype(BF)


def norm_pass(me, raw, qft, states, seen, picks, cap):
    wid, total = raw.shape
    slots = len(picks)
    rows = total // slots
    n = slots * picks[0].shape[1]
    block = lambda i, m: (0, m[0] ^ i)
    return pl.pallas_call(
        functools.partial(norm_kernel, slots, cap),
        grid_spec=pltpu.PrefetchScalarGridSpec(
            num_scalar_prefetch=1,
            grid=(slots,),
            in_specs=[
                pl.BlockSpec((wid, rows), block),
                pl.BlockSpec((qft.shape[0], rows), block),
                whole(states.shape),
                pl.BlockSpec((1,) + seen.shape[1:], lambda i, m: (m[0] ^ i, 0, 0)),
            ]
            + [whole(p.shape) for p in picks],
            out_specs=[whole((wid, rows))] * slots + [whole((n, 2 * wid))],
            scratch_shapes=[pltpu.VMEM((n, 2 * wid), F32), pltpu.VMEM(states.shape[1:], BF)],
        ),
        out_shape=[jax.ShapeDtypeStruct((wid, rows), BF)] * slots
        + [jax.ShapeDtypeStruct((n, 2 * wid), BF)],
        compiler_params=params(),
        cost_estimate=cost(3e9, 8e6),
        name="norm_pass",
    )(me, raw, qft, states, seen, *picks)


def expert_kernel(cap, tiles, got_hbm, wo_hbm, wi_hbm, wd_hbm, out_ref, got, wo, wi, wd, taken, acc, sems):
    slots, ring, each, both = got.shape
    wid = both // 2
    n, d = ring * each, wo.shape[2]
    ff = wi.shape[1]
    tile = ff // tiles
    landing = [pltpu.make_async_copy(got_hbm.at[:, h], got.at[h], sems.at[h]) for h in range(slots)]
    copies = [pltpu.make_async_copy(wo_hbm, wo, sems.at[slots])]
    first = slots + 1
    for t in range(tiles):
        cut = pl.ds(t * tile, tile)
        copies.append(pltpu.make_async_copy(wi_hbm.at[0, :, cut], wi.at[:, cut], sems.at[first + 2 * t]))
        copies.append(pltpu.make_async_copy(wd_hbm.at[0, cut, :], wd.at[cut, :], sems.at[first + 1 + 2 * t]))
    for c in landing + copies:
        c.start()
    for c in landing:
        c.wait()
    parts_in = [got[h].reshape(n, both) for h in range(slots)]
    mixed = jnp.concatenate([g.astype(F32)[:, wid:] for g in parts_in], axis=1)
    copies[0].wait()
    for h, g in enumerate(parts_in):
        mixed = mixed + nn(g[:, :wid], wo[h])
    taken[...] = mixed.astype(BF)
    acc[...] = jnp.zeros((n, d), F32)
    for t in range(tiles):
        cut = slice(t * tile, (t + 1) * tile)
        copies[1 + 2 * t].wait()
        inner = jax.nn.gelu(nn(taken[...], wi[:, cut]), approximate=True).astype(BF)
        copies[2 + 2 * t].wait()
        acc[...] += nn(inner, wd[cut, :])
    m = out_ref.shape[0]
    at = lax.broadcasted_iota(jnp.int32, (1, n), 1)
    out_ref[...] = nn(marks(at // cap * PAD + at % cap, m), acc[...].astype(BF)).astype(BF)


def expert_pass(arrived, w_out, w_in, w_down, cap, tiles=6):
    ring, slots, each, both = arrived.shape
    d, ff = w_in.shape[1:]
    m = ring * each // cap * PAD
    return pl.pallas_call(
        functools.partial(expert_kernel, cap, tiles),
        in_specs=[pl.BlockSpec(memory_space=pl.ANY)] * 4,
        out_specs=pl.BlockSpec(memory_space=pltpu.VMEM),
        out_shape=jax.ShapeDtypeStruct((m, d), BF),
        scratch_shapes=[
            pltpu.VMEM((slots, ring, each, both), BF),
            pltpu.VMEM(w_out.shape, BF),
            pltpu.VMEM((d, ff), BF),
            pltpu.VMEM((ff, d), BF),
            pltpu.VMEM((ring * each, d), BF),
            pltpu.VMEM((ring * each, d), F32),
            pltpu.SemaphoreType.DMA((slots + 1 + 2 * tiles,)),
        ],
        compiler_params=params(),
        cost_estimate=cost(2e9, 12e6),
        name="expert_pass",
    )(arrived, w_out, w_in, w_down)


def mix_kernel(slots, me_ref, tok_ref, wo_ref, *rest):
    attns, out_ref = rest[:-1], rest[-1]
    mixed = tok_ref[...].astype(F32)
    for k in slots:
        mixed = mixed + tn(attns[k][...], wo_ref[me_ref[0] ^ k])
    out_ref[...] = mixed


def mix_pass(me, tokens, w_out, attns, rows):
    d = tokens.shape[1]
    return pl.pallas_call(
        functools.partial(mix_kernel, range(len(attns))),
        grid_spec=pltpu.PrefetchScalarGridSpec(
            num_scalar_prefetch=1,
            grid=(1,),
            in_specs=[pl.BlockSpec((rows, d), lambda i, m: (m[0], 0)), whole(w_out.shape)]
            + [whole(a.shape) for a in attns],
            out_specs=whole((rows, d)),
        ),
        out_shape=jax.ShapeDtypeStruct((rows, d), F32),
        compiler_params=params(),
        cost_estimate=cost(2e9, 6e6),
        name="mix_pass",
    )(me, tokens, w_out, *attns)


def combine_kernel(me_ref, mix_ref, wo_ref, attn_ref, router_ref, pick_ref, back_ref, out_ref):
    hidden = (mix_ref[...] + tn(attn_ref[...], wo_ref[0])).astype(BF)
    gate = jax.nn.sigmoid(nt(hidden, router_ref[...])).astype(BF)
    e, n = gate.shape[1], pick_ref.shape[1]
    rows = hidden.shape[0]
    source = lax.broadcasted_iota(jnp.int32, (1, n), 1) // PAD
    spread = nn(gate, marks(source, e))
    at = lax.broadcasted_iota(jnp.int32, (rows, n), 0) + pl.program_id(0) * rows
    comb = jnp.where(pick_ref[...] == at, spread, 0.0).astype(BF)
    out_ref[...] = (hidden.astype(F32) + nn(comb, back_ref[...])).astype(BF)


def combine_pass(me, mixed, w_out, attn, router_t, pick_row, back, tiles=3):
    rows, d = mixed.shape
    last = w_out.shape[0] - 1
    tile = rows // tiles
    return pl.pallas_call(
        combine_kernel,
        grid_spec=pltpu.PrefetchScalarGridSpec(
            num_scalar_prefetch=1,
            grid=(tiles,),
            in_specs=[
                pl.BlockSpec((tile, d), lambda i, m: (i, 0)),
                pl.BlockSpec((1,) + w_out.shape[1:], lambda i, m: (m[0] ^ last, 0, 0)),
                pl.BlockSpec((attn.shape[0], tile), lambda i, m: (0, i)),
                whole(router_t.shape),
                whole(pick_row.shape),
                whole(back.shape),
            ],
            out_specs=pl.BlockSpec((tile, d), lambda i, m: (i, 0)),
        ),
        out_shape=jax.ShapeDtypeStruct((rows, d), BF),
        compiler_params=params(),
        cost_estimate=cost(2e9, 6e6),
        name="combine_pass",
    )(me, mixed, w_out, attn, router_t, pick_row, back)


def per_device(tokens, w_query, w_key, w_value, freq, w_out, router, w_in, w_down, picks):
    total, d = tokens.shape
    group = lax.axis_size("head")
    ring = lax.axis_size("seq")
    me = lax.axis_index("head")
    me_arr = jnp.stack([me, lax.axis_index("seq")]).astype(jnp.int32)
    rows = total // group
    experts, _, cap = picks.shape
    wid = w_query.shape[1]

    own = picks[:, 0, :]
    near = [own.T.reshape(1, cap * experts)]
    swap = lambda x, k: lax.ppermute(x, "head", [(i, i ^ k) for i in range(group)])
    near += [swap(near[0], k) for k in range(1, group)]
    pick_row = jnp.pad(own, ((0, 0), (0, PAD - cap)), constant_values=-1).reshape(1, experts * PAD)

    kf, vt, sc, state = key_pass(tokens, w_key.T, w_value.T, freq, rows, ring)
    states = lax.all_to_all(state, "seq", split_axis=0, concat_axis=0, tiled=True)
    qft, raw, seen = query_pass(me_arr, tokens, w_query.T, freq.T, kf, vt, sc, near)
    *attns, sent = norm_pass(me_arr, raw, qft, states, seen, near, cap)

    sent = sent.reshape(experts, group * cap, 2 * wid)
    arrived = lax.all_to_all(sent, ("seq", "head"), split_axis=0, concat_axis=0, tiled=True)
    early = [swap(attns[k], k) for k in range(1, group - 1)]
    arrived, *early = lax.optimization_barrier([arrived, *early])
    w_out = w_out.reshape(group, wid, d)
    result = expert_pass(
        arrived.reshape(ring, group, group * cap, 2 * wid), w_out, w_in, w_down, cap
    )
    back = lax.all_to_all(
        result.reshape(experts, PAD, d), ("seq", "head"), split_axis=0, concat_axis=0, tiled=True
    )
    late = swap(attns[-1], group - 1)
    mixed = mix_pass(me_arr, tokens, w_out, [attns[0], *early], rows)
    return combine_pass(
        me_arr, mixed, w_out, late, router.T, pick_row, back.reshape(experts * PAD, d)
    )


def solution(mesh):
    in_specs = (
        P("seq", None),
        P(None, "head"),
        P(None, "head"),
        P(None, "head"),
        P(),
        P(),
        P(),
        P(("seq", "head"), None, None),
        P(("seq", "head"), None, None),
        P(None, ("seq", "head"), None),
    )
    out_specs = P(("seq", "head"), None)
    return jax.shard_map(
        per_device, mesh=mesh, in_specs=in_specs, out_specs=out_specs, check_vma=False
    )
```

time: 132 us -> 103 us (0.78)
  local copies, waits for them, and re-layouts: 33.2 us -> 4.64 us
  blocking collectives: 18.9 us -> 0 us
  Pallas kernels: 38 us -> 53.9 us
  waiting for transfers between devices: 16.8 us -> 21.7 us
  starting transfers between devices: 22.9 us -> 21.2 us
    unnamed x59 -> x29, local copies, waits for them, and re-layouts: 31.4 us -> 3.88 us
    all_to_all x1 -> x0, blocking collectives: 18.9 us -> none  [per_device(): lax.all_to_all(sent, ('seq', 'head'), split_axis=0, concat_axis=0, tiled=...]
    pallas_call x7 -> x5, Pallas kernels: 29.7 us -> 42.2 us  [the longest x1 14.9 us: query_pass(): pl.pallas_call(functools.partial(query_kernel, slots), grid_spec=pltpu.Pr...]
    ppermute x10 -> x6, starting transfers between devices: 16.7 us -> 5.46 us  [per_device(): lax.ppermute(x, 'head', [(i, i ^ k) for i in range(group)])]
    all_to_all x1 -> x2, starting transfers between devices: 3.42 us -> 12.4 us  [the longest x1 7.3 us: per_device(): lax.all_to_all(state, 'seq', split_axis=0, concat_axis=0, tiled=True)]
    pallas_call x1, Pallas kernels: 8.35 us -> 11.7 us  [key_pass(): pl.pallas_call(key_kernel, grid=(total // rows,), in_specs=[pl.BlockSpec(...]
    ppermute x10 -> x6, waiting for transfers between devices: 16.8 us -> 19.6 us  [per_device(): lax.ppermute(x, 'head', [(i, i ^ k) for i in range(group)])]
    all_to_all x1 -> x2, waiting for transfers between devices: 0.01 us -> 1.87 us  [the longest x1 1.84 us: per_device(): lax.all_to_all(sent, ('seq', 'head'), split_axis=0, concat_axis=0, tiled=...]
  transfers between devices with their start and end apart: 12 -> 9, of which waited for: 2 -> 6; matrix products, arithmetic and copies ran while one was open for 3% -> 2% of each run, Pallas kernels for 23% -> 20%
where the time goes in v2:
time: 103 us; the launch traced here: 102 us
  Pallas kernels  53.9 us (52%)
  waiting for transfers between devices  21.7 us (21%)
  starting transfers between devices  21.2 us (21%)
  local copies, waits for them, and re-layouts  4.64 us (5%)
    ppermute x6, waiting for transfers between devices, per_device(): lax.ppermute(x, 'head', [(i, i ^ k) for i in range(group)])  19.6 us
    pallas_call x1, Pallas kernels, query_pass(): pl.pallas_call(functools.partial(query_kernel, slots), grid_spec=pltpu.Pr...  14.9 us
    pallas_call x1, Pallas kernels, key_pass(): pl.pallas_call(key_kernel, grid=(total // rows,), in_specs=[pl.BlockSpec(...  11.7 us
    pallas_call x1, Pallas kernels, norm_pass(): pl.pallas_call(functools.partial(norm_kernel, slots, cap), grid_spec=pltp...  8.89 us
    pallas_call x1, Pallas kernels, expert_pass(): pl.pallas_call(functools.partial(expert_kernel, cap, tiles), in_specs=[pl...  7.54 us
    all_to_all x1, starting transfers between devices, per_device(): lax.all_to_all(state, 'seq', split_axis=0, concat_axis=0, tiled=True)  7.3 us
    pallas_call x1, Pallas kernels, combine_pass(): pl.pallas_call(combine_kernel, grid_spec=pltpu.PrefetchScalarGridSpec(num...  5.79 us
    ppermute x6, starting transfers between devices, per_device(): lax.ppermute(x, 'head', [(i, i ^ k) for i in range(group)])  5.46 us
  transfers between devices with their start and end apart: 9, of which 6 were waited for; matrix products, arithmetic and copies ran while one was open for 2% of the time, Pallas kernels for 20%

profile of v2, /device:TPU:0, one launch (start us, length us, event | category | flops | bytes accessed | tf_op | source)
XLA Modules:
  0.0 102.3 jit_solution(18301155057507009353)
XLA Ops:
  0.0 0.0 copy-start.6
  0.0 0.0 copy-start.5
  0.0 11.7 %key_pass.1 = (bf16[3072,768]{1,0:T(8,128)(2,1)}, bf16[192,3072]{1,0:T(8,128)(2,1)}, bf16[12,192,256]{2,1,0:T(8,128)(2,1)}, bf16[8,192,256]{2,1,0:T(8,128)(2,1)}) custom-call(bf16[3072,768]{1,0:T(8,128)(2,1)} %tok_ref.5, bf16[192,768]{1,0:T(8,128)(2,1)} %bitcast.28, bf16[192,768]{1,0:T(8,128)(2,1)} %bitcast.29, f32[64,128]{1,0:T(8,128)} %freq_ref.1), custom_call_target="tpu_custom_call" | custom-call | flops 5000000000 | bytes 12000000 | tf_op jit(solution)/shard_map/key_pass/pallas_call | solution.py:105
  11.7 7.3 %all-to-all-start = ((bf16[8,192,256]{2,1,0:T(8,128)(2,1)}), bf16[8,192,256]{2,1,0:T(8,128)(2,1)S(1)}, u32[]{:S(2)}, u32[]{:S(2)}) async-start(bf16[8,192,256]{2,1,0:T(8,128)(2,1)} %get-tuple-element.25), calls=%async_computation | async-start | bytes 1572864 | tf_op jit(solution)/shard_map/all_to_all | solution.py:433
  19.0 0.0 copy-done.6
  19.0 0.1 reshape.22.rest_0_
  19.1 0.0 collective-permute-start
  19.1 1.6 %collective-permute-start.1 = (s32[1,192]{1,0:T(1,128)S(1)}, s32[1,192]{1,0:T(1,128)S(1)}, u32[]{:S(2)}, u32[]{:S(2)}) collective-permute-start(s32[1,192]{1,0:T(1,128)S(1)} %reshape.22.rest_0_), channel_id=1, source_target_pairs={{0,2},{1,3},{2,0},{3,1},{4,6},{5,7},{6,4},{7,5},{8,10},{9,11},{10,... | collective-permute-start | bytes 2312 | tf_op jit(solution)/shard_map/ppermute | solution.py:428
  20.6 0.3 collective-permute-start.2
  21.0 0.7 pad_add_fusion.me_ref
  21.6 0.0 copy-done.5
  21.6 0.7 copy.13
  22.3 0.0 collective-permute-done.rest_1_
  22.3 0.0 copy-start.10
  22.3 0.4 collective-permute-done.1.rest_2_
  22.7 0.0 copy-start.11
  22.7 0.9 collective-permute-done.2.rest_3_
  23.6 0.0 copy-start.12
  23.6 0.0 copy-done.7
  23.6 0.0 copy-done.10
  23.6 0.0 copy-done.11
  23.7 0.6 copy-done.12
  24.2 14.9 %query_pass.1 = (bf16[768,3072]{1,0:T(8,128)(2,1)}, f32[192,3072]{1,0:T(8,128)}, bf16[4,192,192]{2,1,0:T(8,128)(2,1)}) custom-call(s32[2]{0:T(128)} %pad_add_fusion.me_ref, bf16[3072,768]{1,0:T(8,128)(2,1)} %tok_ref.5, bf16[192,768]{1,0:T(8,128)(2,1)} %bitcast.30, f32[128,64]{1,0:T(8,128)} %bitcast.25, bf16[3072,768]{1,0:T(8,128)(2,1)} %get-tuple-element.20.kf_ref, ...), custom_call_target="tpu_custom_call" | custom-call | flops 6000000000 | bytes 16000000 | tf_op jit(solution)/shard_map/query_pass/pallas_call | solution.py:190
  39.1 0.0 all-to-all-done.states_ref
  39.1 0.0 copy-start.1
  39.2 0.9 copy-done.1
  40.0 8.9 %norm_pass.1 = (bf16[192,768]{1,0:T(8,128)(2,1)}, bf16[192,768]{1,0:T(8,128)(2,1)}, bf16[192,768]{1,0:T(8,128)(2,1)}, bf16[192,768]{1,0:T(8,128)(2,1)}, bf16[768,384]{1,0:T(8,128)(2,1)}) custom-call(s32[2]{0:T(128)} %pad_add_fusion.me_ref, f32[192,3072]{1,0:T(8,128)} %get-tuple-element.23.raw_ref, bf16[768,3072]{1,0:T(8,128)(2,1)} %get-tuple-element.24.qft_ref, ...), custom_call_target="tpu_custom_call" | custom-call | flops 3000000000 | bytes 8000000 | tf_op jit(solution)/shard_map/norm_pass/pallas_call | solution.py:270
  48.9 5.1 %all-to-all-start.1 = ((bf16[32,24,384]{2,1,0:T(8,128)(2,1)}), bf16[32,24,384]{2,1,0:T(8,128)(2,1)S(1)}, u32[]{:S(2)}, u32[]{:S(2)}) async-start(bf16[32,24,384]{2,1,0:T(8,128)(2,1)} %bitcast.23), calls=%async_computation.1 | async-start | bytes 1179648 | tf_op jit(solution)/shard_map/all_to_all | solution.py:438
  54.0 0.3 collective-permute-start.3
  54.4 1.7 %collective-permute-start.4 = (bf16[192,768]{1,0:T(8,128)(2,1)}, bf16[192,768]{1,0:T(8,128)(2,1)S(1)}, u32[]{:S(2)}, u32[]{:S(2)}) collective-permute-start(bf16[192,768]{1,0:T(8,128)(2,1)} %get-tuple-element.30), channel_id=1, source_target_pairs={{0,2},{1,3},{2,0},{3,1},{4,6},{5,7},{6,4},{7,5},{8,10},{9,11},{10,... | collective-permute-start | bytes 884744 | tf_op jit(solution)/shard_map/ppermute | solution.py:428
  56.0 0.0 collective-permute-done.3.rest_1_
  56.0 12.9 %collective-permute-done.4.rest_2_ = bf16[192,768]{1,0:T(8,128)(2,1)S(1)} collective-permute-done((bf16[192,768]{1,0:T(8,128)(2,1)}, bf16[192,768]{1,0:T(8,128)(2,1)S(1)}, u32[]{:S(2)}, u32[]{:S(2)}) %collective-permute-start.4) | collective-permute-done | bytes 294944 | tf_op jit(solution)/shard_map/ppermute | solution.py:428
  68.9 1.8 %all-to-all-done.1 = bf16[32,24,384]{2,1,0:T(8,128)(2,1)S(1)} async-done(((bf16[32,24,384]{2,1,0:T(8,128)(2,1)}), bf16[32,24,384]{2,1,0:T(8,128)(2,1)S(1)}, u32[]{:S(2)}, u32[]{:S(2)}) %all-to-all-start.1) | async-done | bytes 589856 | tf_op jit(solution)/shard_map/all_to_all | solution.py:438
  70.8 0.8 copy-done
  71.6 7.5 %expert_pass.1 = bf16[256,768]{1,0:T(8,128)(2,1)} custom-call(bf16[8,4,24,384]{3,2,1,0:T(8,128)(2,1)} %bitcast.21, bf16[4,192,768]{2,1,0:T(8,128)(2,1)} %bitcast.18, bf16[1,768,3072]{2,1,0:T(8,128)(2,1)} %wi_hbm.1, bf16[1,3072,768]{2,1,0:T(8,128)(2,1)} %wd_hbm.1), custom_call_target="tpu_custom_call" | custom-call | flops 2000000000 | bytes 12000000 | tf_op jit(solution)/shard_map/expert_pass/pallas_call | solution.py:332
  79.1 3.4 %all-to-all-start.2 = ((bf16[32,8,768]{2,1,0:T(8,128)(2,1)}), bf16[32,8,768]{2,1,0:T(8,128)(2,1)S(1)}, u32[]{:S(2)}, u32[]{:S(2)}) async-start(bf16[32,8,768]{2,1,0:T(8,128)(2,1)} %bitcast.22), calls=%async_computation.2 | async-start | bytes 786432 | tf_op jit(solution)/shard_map/all_to_all | solution.py:445
  82.5 0.0 copy-done.8
  82.5 1.6 %collective-permute-start.5 = (bf16[192,768]{1,0:T(8,128)(2,1)S(1)}, bf16[192,768]{1,0:T(8,128)(2,1)S(1)}, u32[]{:S(2)}, u32[]{:S(2)}) collective-permute-start(bf16[192,768]{1,0:T(8,128)(2,1)S(1)} %copy-done.8), channel_id=1, source_target_pairs={{0,3},{1,2},{2,1},{3,0},{4,7},{5,6},{6,5},{7,4},{8,11},{9,10},{10,... | collective-permute-start | bytes 884744 | tf_op jit(solution)/shard_map/ppermute | solution.py:428
  84.1 0.1 copy.17
  84.2 0.7 reshape.24.pick_ref
  84.9 0.0 copy-done.3
  84.9 0.0 copy-done.4
  84.9 5.1 %mix_pass.1.mix_ref = f32[768,768]{1,0:T(8,128)} custom-call(s32[2]{0:T(128)} %pad_add_fusion.me_ref, bf16[3072,768]{1,0:T(8,128)(2,1)} %tok_ref.5, bf16[4,192,768]{2,1,0:T(8,128)(2,1)} %bitcast.19, bf16[192,768]{1,0:T(8,128)(2,1)} %get-tuple-element.27.rest_0_, bf16[192,768]{1,0:T(8,128)(2,1)} %copy-done.3, bf16[192,768]{1,0:T(8,128)(2,1)} %copy-done.4), custom_call_target="tpu_custom_call" | custom-call | flops 2000000000 | bytes 6000000 | tf_op jit(solution)/shard_map/mix_pass/pallas_call | solution.py:362
  90.0 5.4 %collective-permute-done.5.attn_ref = bf16[192,768]{1,0:T(8,128)(2,1)S(1)} collective-permute-done((bf16[192,768]{1,0:T(8,128)(2,1)S(1)}, bf16[192,768]{1,0:T(8,128)(2,1)S(1)}, u32[]{:S(2)}, u32[]{:S(2)}) %collective-permute-start.5) | collective-permute-done | bytes 294944 | tf_op jit(solution)/shard_map/ppermute | solution.py:428
  95.4 0.3 all-to-all-done.2
  95.7 0.4 copy-done.9
  96.1 0.3 copy-done.2
  96.5 5.8 %combine_pass.1 = bf16[768,768]{1,0:T(8,128)(2,1)} custom-call(s32[2]{0:T(128)} %pad_add_fusion.me_ref, f32[768,768]{1,0:T(8,128)} %mix_pass.1.mix_ref, bf16[4,192,768]{2,1,0:T(8,128)(2,1)} %bitcast.20, bf16[192,768]{1,0:T(8,128)(2,1)} %copy-done.9, bf16[32,768]{1,0:T(8,128)(2,1)} %bitcast.31, s32[1,256]{1,0:T(1,128)} %reshape.24.pick_ref, ...), custom_call_target="tpu_custom_call" | custom-call | flops 2000000000 | bytes 6000000 | tf_op jit(solution)/shard_map/combine_pass/pallas_call | solution.py:394
  (9 shorter events, 0.0 us)
Async XLA Ops:
  0.0 19.0 %copy-start.6 = (s32[32,1,6]{0,1,2:T(1,128)S(1)}, s32[32,1,6]{0,1,2:T(1,128)}, u32[]{:S(2)}) copy-start(s32[32,1,6]{0,1,2:T(1,128)} %param.19) | copy-start | bytes 2308
  0.0 21.6 %copy-start.5 = (f32[64,128]{1,0:T(8,128)S(1)}, f32[64,128]{1,0:T(8,128)}, u32[]{:S(2)}) copy-start(f32[64,128]{1,0:T(8,128)} %freq_ref.1) | copy-start | bytes 98308
  11.7 27.5 %all-to-all-start = ((bf16[8,192,256]{2,1,0:T(8,128)(2,1)}), bf16[8,192,256]{2,1,0:T(8,128)(2,1)S(1)}, u32[]{:S(2)}, u32[]{:S(2)}) async-start(bf16[8,192,256]{2,1,0:T(8,128)(2,1)} %get-tuple-element.25), calls=%async_computation | async-start | bytes 1572864 | tf_op jit(solution)/shard_map/all_to_all | solution.py:433
  19.1 4.6 %copy-start.7 = (s32[1,192]{1,0:T(1,128)}, s32[1,192]{1,0:T(1,128)S(1)}, u32[]{:S(2)}) copy-start(s32[1,192]{1,0:T(1,128)S(1)} %reshape.22.rest_0_) | copy-start | bytes 2308
  19.1 3.3 %collective-permute-start = (s32[1,192]{1,0:T(1,128)S(1)}, s32[1,192]{1,0:T(1,128)S(1)}, u32[]{:S(2)}, u32[]{:S(2)}) collective-permute-start(s32[1,192]{1,0:T(1,128)S(1)} %reshape.22.rest_0_), channel_id=1, source_target_pairs={{0,1},{1,0},{2,3},{3,2},{4,5},{5,4},{6,7},{7,6},{8,9},{9,8},{10,11... | collective-permute-start | bytes 2312 | tf_op jit(solution)/shard_map/ppermute | solution.py:428
  19.1 3.6 %collective-permute-start.1 = (s32[1,192]{1,0:T(1,128)S(1)}, s32[1,192]{1,0:T(1,128)S(1)}, u32[]{:S(2)}, u32[]{:S(2)}) collective-permute-start(s32[1,192]{1,0:T(1,128)S(1)} %reshape.22.rest_0_), channel_id=1, source_target_pairs={{0,2},{1,3},{2,0},{3,1},{4,6},{5,7},{6,4},{7,5},{8,10},{9,11},{10,... | collective-permute-start | bytes 2312 | tf_op jit(solution)/shard_map/ppermute | solution.py:428
  20.6 3.0 %collective-permute-start.2 = (s32[1,192]{1,0:T(1,128)S(1)}, s32[1,192]{1,0:T(1,128)S(1)}, u32[]{:S(2)}, u32[]{:S(2)}) collective-permute-start(s32[1,192]{1,0:T(1,128)S(1)} %reshape.22.rest_0_), channel_id=1, source_target_pairs={{0,3},{1,2},{2,1},{3,0},{4,7},{5,6},{6,5},{7,4},{8,11},{9,10},{10,... | collective-permute-start | bytes 2312 | tf_op jit(solution)/shard_map/ppermute | solution.py:428
  22.3 1.3 %copy-start.10 = (s32[1,192]{1,0:T(1,128)}, s32[1,192]{1,0:T(1,128)S(1)}, u32[]{:S(2)}) copy-start(s32[1,192]{1,0:T(1,128)S(1)} %collective-permute-done.rest_1_) | copy-start | bytes 2308
  22.7 0.9 copy-start.11
  23.6 0.6 copy-start.12
  39.1 0.9 copy-start.1
  48.9 21.9 %all-to-all-start.1 = ((bf16[32,24,384]{2,1,0:T(8,128)(2,1)}), bf16[32,24,384]{2,1,0:T(8,128)(2,1)S(1)}, u32[]{:S(2)}, u32[]{:S(2)}) async-start(bf16[32,24,384]{2,1,0:T(8,128)(2,1)} %bitcast.23), calls=%async_computation.1 | async-start | bytes 1179648 | tf_op jit(solution)/shard_map/all_to_all | solution.py:438
  54.0 2.0 %collective-permute-start.3 = (bf16[192,768]{1,0:T(8,128)(2,1)}, bf16[192,768]{1,0:T(8,128)(2,1)S(1)}, u32[]{:S(2)}, u32[]{:S(2)}) collective-permute-start(bf16[192,768]{1,0:T(8,128)(2,1)} %get-tuple-element.29), channel_id=1, source_target_pairs={{0,1},{1,0},{2,3},{3,2},{4,5},{5,4},{6,7},{7,6},{8,9},{9,8},{10,11... | collective-permute-start | bytes 884744 | tf_op jit(solution)/shard_map/ppermute | solution.py:428
  54.4 14.6 %collective-permute-start.4 = (bf16[192,768]{1,0:T(8,128)(2,1)}, bf16[192,768]{1,0:T(8,128)(2,1)S(1)}, u32[]{:S(2)}, u32[]{:S(2)}) collective-permute-start(bf16[192,768]{1,0:T(8,128)(2,1)} %get-tuple-element.30), channel_id=1, source_target_pairs={{0,2},{1,3},{2,0},{3,1},{4,6},{5,7},{6,4},{7,5},{8,10},{9,11},{10,... | collective-permute-start | bytes 884744 | tf_op jit(solution)/shard_map/ppermute | solution.py:428
  56.0 28.8 %copy-start.3 = (bf16[192,768]{1,0:T(8,128)(2,1)}, bf16[192,768]{1,0:T(8,128)(2,1)S(1)}, u32[]{:S(2)}) copy-start(bf16[192,768]{1,0:T(8,128)(2,1)S(1)} %collective-permute-done.3.rest_1_) | copy-start | bytes 884740
  68.9 15.9 %copy-start.4 = (bf16[192,768]{1,0:T(8,128)(2,1)}, bf16[192,768]{1,0:T(8,128)(2,1)S(1)}, u32[]{:S(2)}) copy-start(bf16[192,768]{1,0:T(8,128)(2,1)S(1)} %collective-permute-done.4.rest_2_) | copy-start | bytes 884740
  70.8 0.8 copy-start
  71.6 10.9 %copy-start.8 = (bf16[192,768]{1,0:T(8,128)(2,1)S(1)}, bf16[192,768]{1,0:T(8,128)(2,1)}, u32[]{:S(2)}) copy-start(bf16[192,768]{1,0:T(8,128)(2,1)} %get-tuple-element.33) | copy-start | bytes 884740
  79.1 16.5 %all-to-all-start.2 = ((bf16[32,8,768]{2,1,0:T(8,128)(2,1)}), bf16[32,8,768]{2,1,0:T(8,128)(2,1)S(1)}, u32[]{:S(2)}, u32[]{:S(2)}) async-start(bf16[32,8,768]{2,1,0:T(8,128)(2,1)} %bitcast.22), calls=%async_computation.2 | async-start | bytes 786432 | tf_op jit(solution)/shard_map/all_to_all | solution.py:445
  82.5 12.9 %collective-permute-start.5 = (bf16[192,768]{1,0:T(8,128)(2,1)S(1)}, bf16[192,768]{1,0:T(8,128)(2,1)S(1)}, u32[]{:S(2)}, u32[]{:S(2)}) collective-permute-start(bf16[192,768]{1,0:T(8,128)(2,1)S(1)} %copy-done.8), channel_id=1, source_target_pairs={{0,3},{1,2},{2,1},{3,0},{4,7},{5,6},{6,5},{7,4},{8,11},{9,10},{10,... | collective-permute-start | bytes 884744 | tf_op jit(solution)/shard_map/ppermute | solution.py:428
  95.4 0.7 copy-start.9
  95.7 0.8 copy-start.2

commit v3 on v2

v3 whole, which is shorter than its diff:
```python
import functools
import math

import jax
import jax.numpy as jnp
from jax import lax
from jax.experimental import pallas as pl
from jax.experimental.pallas import tpu as pltpu
from jax.sharding import PartitionSpec as P

HD = 64
EPS = 1e-06
CHUNK = 256
PAD = 8
BF = jnp.bfloat16
F32 = jnp.float32
MIB = 2**20
KEPT = 24
PIECES = ((0,), (1,), (2, 3))
SIN = (3.14158202, -5.16714279, 2.54189901, -0.55463616)
COS = (0.9999933, -4.93393802, 4.04128381, -1.22212701)


def nn(a, b):
    return lax.dot_general(a, b, (((1,), (0,)), ((), ())), preferred_element_type=F32)


def nt(a, b):
    return lax.dot_general(a, b, (((1,), (1,)), ((), ())), preferred_element_type=F32)


def tn(a, b):
    return lax.dot_general(a, b, (((0,), (0,)), ((), ())), preferred_element_type=F32)


def wave(turns, scale):
    big = F32(1.5 * 2.0**23)
    r = turns - ((turns + big) - big)
    u = r * r
    root = math.sqrt(2 * scale)
    a = [F32(v * root) for v in SIN]
    b = [F32(v * root) for v in COS]
    s = r * (a[0] + u * (a[1] + u * (a[2] + u * a[3])))
    c = b[0] + u * (b[1] + u * (b[2] + u * b[3]))
    return F32(scale) - s * s, s * c


def parts(f):
    hi = f.astype(BF)
    rest = f - hi.astype(F32)
    mid = rest.astype(BF)
    lo = (rest - mid.astype(F32)).astype(BF)
    return [hi, mid, lo]


def whole(shape):
    return pl.BlockSpec(shape, lambda *_: (0,) * len(shape))


def params(mib=60):
    return pltpu.CompilerParams(vmem_limit_bytes=mib * MIB)


def far(x):
    return pltpu.with_memory_space_constraint(x, pltpu.HBM)


def cost(flops, nbytes):
    return pl.CostEstimate(flops=int(flops), bytes_accessed=int(nbytes), transcendentals=0)


HERE = pl.BlockSpec(memory_space=pltpu.VMEM)
AWAY = pl.BlockSpec(memory_space=pl.ANY)
FAR = pl.BlockSpec(memory_space=pltpu.HBM)


def key_kernel(size, tok_hbm, wkt_hbm, wvt_hbm, freq_hbm, *rest):
    tok_ref, kf_ref, vt_ref, sc_ref, tot_ref, wkt_ref, wvt_ref, freq_ref, sems = rest
    total = tok_ref.shape[0]
    weights = [
        pltpu.make_async_copy(a, b, sems.at[i])
        for i, (a, b) in enumerate([(wkt_hbm, wkt_ref), (wvt_hbm, wvt_ref), (freq_hbm, freq_ref)])
    ]
    loads = [
        pltpu.make_async_copy(tok_hbm.at[pl.ds(first, size)], tok_ref.at[pl.ds(first, size)], sems.at[3 + i])
        for i, first in enumerate(range(0, total, size))
    ]
    for copy in [weights[0], loads[0], *weights[1:], *loads[1:]]:
        copy.start()
    for copy in weights:
        copy.wait()
    wid = wkt_ref.shape[0]
    heads = wid // HD
    half = freq_ref.shape[1]
    feat = 2 * half
    f3 = jnp.concatenate(parts(freq_ref[...] * F32(0.5 / math.pi)), axis=0)
    state = [jnp.zeros((HD, feat), F32) for _ in range(heads)]
    for first in range(0, total, size):
        span = slice(first, first + size)
        loads[first // size].wait()
        tok = tok_ref[span, :]
        k = nt(tok, wkt_ref[...]).astype(BF)
        vt = nt(wvt_ref[...], tok).astype(BF)
        vt_ref[:, span] = vt
        for h in range(heads):
            mine = slice(h * HD, (h + 1) * HD)
            phase = nn(jnp.concatenate([k[:, mine]] * 3, axis=1), f3)
            c, s = wave(phase, 1 / math.sqrt(half))
            kf = jnp.concatenate([c.astype(BF), s.astype(BF)], axis=1)
            kf_ref[span, h * feat : (h + 1) * feat] = kf
            for j in range(0, size, CHUNK):
                sc_ref[(first + j) // CHUNK, mine, :] = state[h].astype(BF)
                state[h] = state[h] + nn(vt[mine, j : j + CHUNK], kf[j : j + CHUNK])
    for h in range(heads):
        tot_ref[h * HD : (h + 1) * HD, :] = state[h].astype(BF)


def key_pass(tokens, wkt, wvt, freq, size):
    total, d = tokens.shape
    wid = wkt.shape[0]
    feat = 2 * freq.shape[1]
    heads = wid // HD
    return pl.pallas_call(
        functools.partial(key_kernel, size),
        in_specs=[FAR] * 4,
        out_specs=[HERE] * 5,
        out_shape=[
            jax.ShapeDtypeStruct(tokens.shape, BF),
            jax.ShapeDtypeStruct((total, heads * feat), BF),
            jax.ShapeDtypeStruct((wid, total), BF),
            jax.ShapeDtypeStruct((total // CHUNK, wid, feat), BF),
            jax.ShapeDtypeStruct((wid, feat), BF),
        ],
        scratch_shapes=[
            pltpu.VMEM(wkt.shape, BF),
            pltpu.VMEM(wvt.shape, BF),
            pltpu.VMEM(freq.shape, F32),
            pltpu.SemaphoreType.DMA((3 + total // size,)),
        ],
        compiler_params=params(KEPT),
        cost_estimate=cost(5e9, 12e6),
        name="key_pass",
    )(*map(far, (tokens, wkt, wvt, freq)))


def chosen(slot, pick_refs):
    row = pick_refs[0][...]
    for k in range(1, len(pick_refs)):
        row = jnp.where(slot == k, pick_refs[k][...], row)
    return row


def marks(row, rows):
    at = lax.broadcasted_iota(jnp.int32, (rows, row.shape[1]), 0)
    return (at == row).astype(F32).astype(BF)


def query_kernel(blocks, slots, tok_ref, wqt_ref, freq_ref, kf_ref, vt_ref, sc_ref, *rest):
    pick_refs = rest[:slots]
    qft_ref, raw_ref, seen_ref = rest[-3:]
    wid, d = wqt_ref.shape
    heads = wid // HD
    half = freq_ref.shape[1]
    feat = 2 * half
    rows = tok_ref.shape[0] // slots
    me = lax.axis_index("head")
    f3t = jnp.concatenate(parts(freq_ref[...].T * F32(0.5 / math.pi)), axis=1)
    line = lax.broadcasted_iota(jnp.int32, (wid, d), 0)
    column = lax.broadcasted_iota(jnp.int32, (wid, d), 1)
    both_w = jnp.concatenate([wqt_ref[...], (line + me * wid == column).astype(F32).astype(BF)], axis=0)
    place = [lax.broadcasted_iota(jnp.int32, (CHUNK, CHUNK), i) for i in (0, 1)]
    keep = place[0] <= place[1]
    for block in blocks:
        first = block * rows
        tok = tok_ref[first : first + rows, :]
        out = nt(both_w, tok).astype(BF)
        seen_ref[block] = nn(out[wid:], marks(chosen(me ^ block, pick_refs), rows)).astype(BF)
        for h in range(heads):
            mine = slice(h * HD, (h + 1) * HD)
            phase = nn(f3t, jnp.concatenate([out[mine]] * 3, axis=0))
            c, s = wave(phase, 1 / math.sqrt(half))
            qf = jnp.concatenate([c.astype(BF), s.astype(BF)], axis=0)
            qft_ref[block, h * feat : (h + 1) * feat, :] = qf
            for j in range(0, rows, CHUNK):
                cols = slice(j, j + CHUNK)
                there = slice(first + j, first + j + CHUNK)
                both = jnp.concatenate(
                    [kf_ref[there, h * feat : (h + 1) * feat], sc_ref[(first + j) // CHUNK, mine, :]], axis=0
                )
                both = nn(both, qf[:, cols])
                scores = jnp.where(keep, both[:CHUNK], 0.0).astype(BF)
                raw_ref[block, mine, cols] = nn(vt_ref[mine, there], scores) + both[CHUNK:]


def query_pass(blocks, tokens, wqt, freq, kf, vt, sc, picks, after, into):
    total, d = tokens.shape
    slots = len(picks)
    rows = total // slots
    n = picks[0].shape[1]
    wid = wqt.shape[0]
    feat = 2 * freq.shape[1]
    heads = wid // HD
    args = [tokens, wqt, freq, kf, vt, sc, *picks, after, *into]
    return pl.pallas_call(
        functools.partial(query_kernel, blocks, slots),
        in_specs=[HERE] * (len(args) - len(into) - 1) + [AWAY] * (len(into) + 1),
        out_specs=[HERE] * 3,
        out_shape=[
            jax.ShapeDtypeStruct((slots, heads * feat, rows), BF),
            jax.ShapeDtypeStruct((slots, wid, rows), F32),
            jax.ShapeDtypeStruct((slots, wid, n), BF),
        ],
        input_output_aliases={len(args) - len(into) + i: i for i in range(len(into))},
        compiler_params=params(KEPT),
        cost_estimate=cost(1.5e9 * len(blocks), 4e6 * len(blocks)),
        name="query_pass",
    )(*args)


def norm_kernel(slots, cap, rounds, raw_ref, qft_ref, seen_ref, *rest):
    got_refs, pick_refs = rest[:rounds], rest[rounds : rounds + slots]
    outs = rest[rounds + slots : rounds + 2 * slots]
    sent_hbm, ready, acc, sent, sems = rest[rounds + 2 * slots :]
    me, at = lax.axis_index("head"), lax.axis_index("seq")
    wid = raw_ref.shape[1]
    heads = wid // HD
    feat = got_refs[0].shape[1]
    before = jnp.zeros(got_refs[0].shape, F32)
    for i, got in enumerate(got_refs):
        before = before + jnp.where((at & (1 << i)) > 0, got[...].astype(F32), 0.0)
    before = before.astype(BF)
    copies = [pltpu.make_async_copy(ready.at[k], outs[k], sems.at[k]) for k in range(slots)]
    for k in range(slots):
        block = me ^ k
        for h in range(heads):
            mine = slice(h * HD, (h + 1) * HD)
            raw = raw_ref[block, mine, :] + nn(before[mine, :], qft_ref[block, h * feat : (h + 1) * feat, :])
            meansq = jnp.mean(raw * raw, axis=0, keepdims=True)
            ready[k, mine, :] = (raw * lax.rsqrt(meansq + F32(EPS))).astype(BF)
        copies[k].start()
        attn = ready[k]
        picked = nn(attn, marks(pick_refs[k][...], attn.shape[1])).astype(BF)
        both = jnp.concatenate([picked, seen_ref[block]], axis=0)
        n = both.shape[1]
        experts = n // cap
        entry = lax.broadcasted_iota(jnp.int32, (1, n), 1)
        row = (entry % experts * slots + block) * cap + entry // experts
        part = nt(marks(row, acc.shape[0]), both)
        acc[...] = part if k == 0 else acc[...] + part
    sent[...] = acc[...].astype(BF)
    last = pltpu.make_async_copy(sent, sent_hbm, sems.at[slots])
    last.start()
    for copy in copies:
        copy.wait()
    last.wait()


def norm_pass(raw, qft, seen, got, picks, cap):
    slots, wid, rows = raw.shape
    n = slots * picks[0].shape[1]
    return pl.pallas_call(
        functools.partial(norm_kernel, slots, cap, len(got)),
        in_specs=[HERE] * (3 + len(got) + slots),
        out_specs=[FAR] * (slots + 1),
        out_shape=[pltpu.HBM((wid, rows), BF)] * slots + [pltpu.HBM((n, 2 * wid), BF)],
        scratch_shapes=[
            pltpu.VMEM((slots, wid, rows), BF),
            pltpu.VMEM((n, 2 * wid), F32),
            pltpu.VMEM((n, 2 * wid), BF),
            pltpu.SemaphoreType.DMA((slots + 1,)),
        ],
        compiler_params=params(KEPT + n * wid * 20 // MIB),
        cost_estimate=cost(3e9, 8e6),
        name="norm_pass",
    )(raw, qft, seen, *got, *picks)


def expert_kernel(cap, tiles, got_hbm, wo_hbm, wi_hbm, wd_hbm, out_ref, got, wo, wi, wd, taken, acc, sems):
    slots, ring, each, both = got.shape
    wid = both // 2
    n, d = ring * each, wo.shape[2]
    ff = wi.shape[1]
    tile = ff // tiles
    landing = [pltpu.make_async_copy(got_hbm.at[:, h], got.at[h], sems.at[h]) for h in range(slots)]
    copies = [pltpu.make_async_copy(wo_hbm, wo, sems.at[slots])]
    first = slots + 1
    for t in range(tiles):
        cut = pl.ds(t * tile, tile)
        copies.append(pltpu.make_async_copy(wi_hbm.at[0, :, cut], wi.at[:, cut], sems.at[first + 2 * t]))
        copies.append(pltpu.make_async_copy(wd_hbm.at[0, cut, :], wd.at[cut, :], sems.at[first + 1 + 2 * t]))
    for c in landing + copies:
        c.start()
    for c in landing:
        c.wait()
    parts_in = [got[h].reshape(n, both) for h in range(slots)]
    mixed = jnp.concatenate([g.astype(F32)[:, wid:] for g in parts_in], axis=1)
    copies[0].wait()
    for h, g in enumerate(parts_in):
        mixed = mixed + nn(g[:, :wid], wo[h])
    taken[...] = mixed.astype(BF)
    acc[...] = jnp.zeros((n, d), F32)
    for t in range(tiles):
        cut = slice(t * tile, (t + 1) * tile)
        copies[1 + 2 * t].wait()
        inner = jax.nn.gelu(nn(taken[...], wi[:, cut]), approximate=True).astype(BF)
        copies[2 + 2 * t].wait()
        acc[...] += nn(inner, wd[cut, :])
    m = out_ref.shape[0]
    at = lax.broadcasted_iota(jnp.int32, (1, n), 1)
    out_ref[...] = nn(marks(at // cap * PAD + at % cap, m), acc[...].astype(BF)).astype(BF)


def expert_pass(arrived, w_out, w_in, w_down, cap, tiles=6):
    ring, slots, each, both = arrived.shape
    d, ff = w_in.shape[1:]
    m = ring * each // cap * PAD
    return pl.pallas_call(
        functools.partial(expert_kernel, cap, tiles),
        in_specs=[AWAY] + [FAR] * 3,
        out_specs=HERE,
        out_shape=jax.ShapeDtypeStruct((m, d), BF),
        scratch_shapes=[
            pltpu.VMEM((slots, ring, each, both), BF),
            pltpu.VMEM(w_out.shape, BF),
            pltpu.VMEM((d, ff), BF),
            pltpu.VMEM((ff, d), BF),
            pltpu.VMEM((ring * each, d), BF),
            pltpu.VMEM((ring * each, d), F32),
            pltpu.SemaphoreType.DMA((slots + 1 + 2 * tiles,)),
        ],
        compiler_params=params(40),
        cost_estimate=cost(2e9, 12e6),
        name="expert_pass",
    )(arrived, *map(far, (w_out, w_in, w_down)))


def mix_kernel(slots, me_ref, tok_ref, wo_ref, *rest):
    attns, out_ref = rest[:-1], rest[-1]
    mixed = tok_ref[...].astype(F32)
    for k in slots:
        mixed = mixed + tn(attns[k][...], wo_ref[me_ref[0] ^ k])
    out_ref[...] = mixed


def mix_pass(me, tokens, w_out, attns, rows):
    d = tokens.shape[1]
    return pl.pallas_call(
        functools.partial(mix_kernel, range(len(attns))),
        grid_spec=pltpu.PrefetchScalarGridSpec(
            num_scalar_prefetch=1,
            grid=(1,),
            in_specs=[pl.BlockSpec((rows, d), lambda i, m: (m[0], 0)), whole(w_out.shape)]
            + [whole(a.shape) for a in attns],
            out_specs=whole((rows, d)),
        ),
        out_shape=jax.ShapeDtypeStruct((rows, d), F32),
        compiler_params=params(),
        cost_estimate=cost(2e9, 6e6),
        name="mix_pass",
    )(me, tokens, w_out, *attns)


def combine_kernel(me_ref, mix_ref, wo_ref, attn_ref, router_ref, pick_ref, back_ref, out_ref):
    hidden = (mix_ref[...] + tn(attn_ref[...], wo_ref[0])).astype(BF)
    gate = jax.nn.sigmoid(nt(hidden, router_ref[...])).astype(BF)
    e, n = gate.shape[1], pick_ref.shape[1]
    rows = hidden.shape[0]
    source = lax.broadcasted_iota(jnp.int32, (1, n), 1) // PAD
    spread = nn(gate, marks(source, e))
    at = lax.broadcasted_iota(jnp.int32, (rows, n), 0) + pl.program_id(0) * rows
    comb = jnp.where(pick_ref[...] == at, spread, 0.0).astype(BF)
    out_ref[...] = (hidden.astype(F32) + nn(comb, back_ref[...])).astype(BF)


def combine_pass(me, mixed, w_out, attn, router_t, pick_row, back, tiles=3):
    rows, d = mixed.shape
    last = w_out.shape[0] - 1
    tile = rows // tiles
    return pl.pallas_call(
        combine_kernel,
        grid_spec=pltpu.PrefetchScalarGridSpec(
            num_scalar_prefetch=1,
            grid=(tiles,),
            in_specs=[
                pl.BlockSpec((tile, d), lambda i, m: (i, 0)),
                pl.BlockSpec((1,) + w_out.shape[1:], lambda i, m: (m[0] ^ last, 0, 0)),
                pl.BlockSpec((attn.shape[0], tile), lambda i, m: (0, i)),
                whole(router_t.shape),
                whole(pick_row.shape),
                whole(back.shape),
            ],
            out_specs=pl.BlockSpec((tile, d), lambda i, m: (i, 0)),
        ),
        out_shape=jax.ShapeDtypeStruct((rows, d), BF),
        compiler_params=params(),
        cost_estimate=cost(2e9, 6e6),
        name="combine_pass",
    )(me, mixed, w_out, attn, router_t, pick_row, back)


def per_device(tokens, w_query, w_key, w_value, freq, w_out, router, w_in, w_down, picks):
    total, d = tokens.shape
    group = lax.axis_size("head")
    ring = lax.axis_size("seq")
    me = lax.axis_index("head")
    me_arr = jnp.stack([me, lax.axis_index("seq")]).astype(jnp.int32)
    rows = total // group
    experts, _, cap = picks.shape
    wid = w_query.shape[1]

    own = picks[:, 0, :]
    near = [own.T.reshape(1, cap * experts)]
    swap = lambda x, k: lax.ppermute(x, "head", [(i, i ^ k) for i in range(group)])
    near += [swap(near[0], k) for k in range(1, group)]
    pick_row = jnp.pad(own, ((0, 0), (0, PAD - cap)), constant_values=-1).reshape(1, experts * PAD)

    tok_here, kf, vt, sc, held = key_pass(tokens, w_key.T, w_value.T, freq, rows)
    got = []
    made = []
    stride = 1
    while stride < ring:
        last = 2 * stride >= ring
        pairs = [(i, i ^ stride) for i in range(ring) if not last or i & stride == 0]
        got.append(lax.ppermute(held, "seq", pairs))
        blocks = PIECES[len(got) - 1] if len(got) <= len(PIECES) else ()
        if blocks:
            made = query_pass(blocks, tok_here, w_query.T, freq, kf, vt, sc, near, held, made)
        held = (held.astype(F32) + got[-1].astype(F32)).astype(BF)
        stride *= 2
    qft, raw, seen = made
    *attns, sent = norm_pass(raw, qft, seen, got, near, cap)

    sent = sent.reshape(experts, group * cap, 2 * wid)
    arrived = lax.all_to_all(sent, ("seq", "head"), split_axis=0, concat_axis=0, tiled=True)
    early = [swap(attns[k], k) for k in range(1, group - 1)]
    arrived, *early = lax.optimization_barrier([arrived, *early])
    w_out = w_out.reshape(group, wid, d)
    result = expert_pass(
        arrived.reshape(ring, group, group * cap, 2 * wid), w_out, w_in, w_down, cap
    )
    back = lax.all_to_all(
        result.reshape(experts, PAD, d), ("seq", "head"), split_axis=0, concat_axis=0, tiled=True
    )
    late = swap(attns[-1], group - 1)
    mixed = mix_pass(me_arr, tokens, w_out, [attns[0], *early], rows)
    return combine_pass(
        me_arr, mixed, w_out, late, router.T, pick_row, back.reshape(experts * PAD, d)
    )


def solution(mesh):
    in_specs = (
        P("seq", None),
        P(None, "head"),
        P(None, "head"),
        P(None, "head"),
        P(),
        P(),
        P(),
        P(("seq", "head"), None, None),
        P(("seq", "head"), None, None),
        P(None, ("seq", "head"), None),
    )
    out_specs = P(("seq", "head"), None)
    return jax.shard_map(
        per_device, mesh=mesh, in_specs=in_specs, out_specs=out_specs, check_vma=False
    )
```

time: 103 us -> 90 us (0.87)
  Pallas kernels: 53.9 us -> 43.1 us
  local copies, waits for them, and re-layouts: 4.64 us -> 2.41 us
  starting transfers between devices: 21.2 us -> 22.7 us
  waiting for transfers between devices: 21.7 us -> 20.5 us
    pallas_call x4 -> x6, Pallas kernels: 43 us -> 32.2 us  [the longest x3 10.8 us: query_pass(): pl.pallas_call(functools.partial(query_kernel, blocks, slots), in_specs=[...]
    ppermute x0 -> x3, starting transfers between devices: none -> 8.57 us  [per_device(): got.append(lax.ppermute(held, 'seq', pairs))]
    all_to_all x1 -> x0, starting transfers between devices: 7.3 us -> none  [per_device(): lax.all_to_all(state, 'seq', split_axis=0, concat_axis=0, tiled=True)]
    unnamed x29 -> x18, local copies, waits for them, and re-layouts: 3.88 us -> 1.64 us
    ppermute x6, waiting for transfers between devices: 19.6 us -> 18 us  [per_device(): lax.ppermute(x, 'head', [(i, i ^ k) for i in range(group)])]
    ppermute x6, starting transfers between devices: 5.46 us -> 6.6 us  [per_device(): lax.ppermute(x, 'head', [(i, i ^ k) for i in range(group)])]
  transfers between devices with their start and end apart: 9 -> 11, of which waited for: 6 -> 5; matrix products, arithmetic and copies ran while one was open for 2% -> 2% of each run, Pallas kernels for 20% -> 29%
where the time goes in v3:
time: 90 us; the launch traced here: 89.6 us
  Pallas kernels  43.1 us (48%)
  starting transfers between devices  22.7 us (25%)
  waiting for transfers between devices  20.5 us (23%)
  local copies, waits for them, and re-layouts  2.41 us (3%)
    ppermute x6, waiting for transfers between devices, per_device(): lax.ppermute(x, 'head', [(i, i ^ k) for i in range(group)])  18 us
    pallas_call x3, Pallas kernels, query_pass(): pl.pallas_call(functools.partial(query_kernel, blocks, slots), in_specs=[...  10.8 us
    pallas_call x1, Pallas kernels, key_pass(): pl.pallas_call(functools.partial(key_kernel, size), in_specs=[FAR] * 4, o...  10.1 us
    ppermute x3, starting transfers between devices, per_device(): got.append(lax.ppermute(held, 'seq', pairs))  8.57 us
    pallas_call x1, Pallas kernels, expert_pass(): pl.pallas_call(functools.partial(expert_kernel, cap, tiles), in_specs=[AW...  7.28 us
    ppermute x6, starting transfers between devices, per_device(): lax.ppermute(x, 'head', [(i, i ^ k) for i in range(group)])  6.6 us
    pallas_call x1, Pallas kernels, combine_pass(): pl.pallas_call(combine_kernel, grid_spec=pltpu.PrefetchScalarGridSpec(num...  5.79 us
    pallas_call x1, Pallas kernels, mix_pass(): pl.pallas_call(functools.partial(mix_kernel, range(len(attns))), grid_spe...  5.11 us
  transfers between devices with their start and end apart: 11, of which 5 were waited for; matrix products, arithmetic and copies ran while one was open for 2% of the time, Pallas kernels for 29%

profile of v3, /device:TPU:0, one launch (start us, length us, event | category | flops | bytes accessed | tf_op | source)
XLA Modules:
  0.0 89.6 jit_solution(8296701797799923381)
XLA Ops:
  0.0 0.7 copy.23
  0.7 0.1 reshape.22.rest_0_.rest_3_
  0.8 0.5 collective-permute-start
  1.2 2.6 %collective-permute-start.1 = (s32[1,192]{1,0:T(1,128)S(1)}, s32[1,192]{1,0:T(1,128)S(1)}, u32[]{:S(2)}, u32[]{:S(2)}) collective-permute-start(s32[1,192]{1,0:T(1,128)S(1)} %reshape.22.rest_0_.rest_3_), channel_id=1, source_target_pairs={{0,2},{1,3},{2,0},{3,1},{4,6},{5,7},{6,4},{7,5},{8,10},{9,11},{10,... | collective-permute-start | bytes 2312 | tf_op jit(solution)/shard_map/ppermute | solution.py:413
  3.8 0.1 collective-permute-start.2
  3.9 0.0 copy-start
  3.9 0.0 copy-start.1
  3.9 10.1 %key_pass.1 = (bf16[3072,768]{1,0:T(8,128)(2,1)S(1)}, bf16[3072,768]{1,0:T(8,128)(2,1)S(1)}, bf16[192,3072]{1,0:T(8,128)(2,1)S(1)}, bf16[12,192,256]{2,1,0:T(8,128)(2,1)S(1)}, bf16[192,256]{1,0:T(8,128)(2,1)S(1)}) custom-call(bf16[3072,768]{1,0:T(8,128)(2,1)} %tok_ref.1, bf16[192,768]{1,0:T(8,128)(2,1)} %bitcast.28, bf16[192,768]{1,0:T(8,128)(2,1)} %bitcast.29, ...), custom_call_target="tpu_custom_call" | custom-call | flops 5000000000 | bytes 12000000 | tf_op jit(solution)/shard_map/key_pass/pallas_call | solution.py:123
  14.0 1.8 %collective-permute-start.3 = (bf16[192,256]{1,0:T(8,128)(2,1)S(1)}, bf16[192,256]{1,0:T(8,128)(2,1)S(1)}, u32[]{:S(2)}, u32[]{:S(2)}) collective-permute-start(bf16[192,256]{1,0:T(8,128)(2,1)S(1)} %get-tuple-element.31.rest_4_), channel_id=1, source_target_pairs={{0,4},{4,0},{8,12},{12,8},{16,20},{20,16},{24,28},{28,24},{1,5},{5... | collective-permute-start | bytes 294920 | tf_op jit(solution)/shard_map/ppermute | solution.py:424
  15.8 0.0 collective-permute-done.rest_1_.rest_4_
  15.8 0.0 collective-permute-done.1.rest_2_.rest_5_
  15.8 0.0 collective-permute-done.2.rest_3_.rest_6_
  15.8 0.0 copy-done
  15.8 0.0 copy-done.1
  15.8 2.7 %query_pass.3 = (bf16[4,768,768]{2,1,0:T(8,128)(2,1)S(1)}, f32[4,192,768]{2,1,0:T(8,128)S(1)}, bf16[4,192,192]{2,1,0:T(8,128)(2,1)S(1)}) custom-call(bf16[3072,768]{1,0:T(8,128)(2,1)S(1)} %get-tuple-element.27.tok_ref, bf16[192,768]{1,0:T(8,128)(2,1)S(1)} %bitcast.17, f32[64,128]{1,0:T(8,128)S(1)} %copy-done.1, ...), custom_call_target="tpu_custom_call" | custom-call | flops 1500000000 | bytes 4000000 | tf_op jit(solution)/shard_map/query_pass/pallas_call | solution.py:204
  18.5 0.5 collective-permute-done.3.rest_0_
  19.1 1.9 %collective-permute-start.4 = (bf16[192,256]{1,0:T(8,128)(2,1)S(1)}, bf16[192,256]{1,0:T(8,128)(2,1)S(1)}, u32[]{:S(2)}, u32[]{:S(2)}) collective-permute-start(bf16[192,256]{1,0:T(8,128)(2,1)S(1)} %add_convert_fusion.1.rest_4_), channel_id=1, source_target_pairs={{0,8},{4,12},{8,0},{12,4},{16,24},{20,28},{24,16},{28,20},{1,9},{5... | collective-permute-start | bytes 294920 | tf_op jit(solution)/shard_map/ppermute | solution.py:424
  21.0 2.7 %query_pass.4 = (bf16[4,768,768]{2,1,0:T(8,128)(2,1)S(1)}, f32[4,192,768]{2,1,0:T(8,128)S(1)}, bf16[4,192,192]{2,1,0:T(8,128)(2,1)S(1)}) custom-call(bf16[3072,768]{1,0:T(8,128)(2,1)S(1)} %get-tuple-element.27.tok_ref, bf16[192,768]{1,0:T(8,128)(2,1)S(1)} %bitcast.18, ...), custom_call_target="tpu_custom_call", output_to_operand_aliasing={{0}: (11, {}), {1}: (12, {}), {2}: (13, {})} | custom-call | flops 1500000000 | bytes 4000000 | tf_op jit(solution)/shard_map/query_pass/pallas_call | solution.py:204
  23.7 0.1 collective-permute-done.4.rest_1_
  23.8 4.9 %collective-permute-start.5 = (bf16[192,256]{1,0:T(8,128)(2,1)S(1)}, bf16[192,256]{1,0:T(8,128)(2,1)S(1)}, u32[]{:S(2)}, u32[]{:S(2)}) collective-permute-start(bf16[192,256]{1,0:T(8,128)(2,1)S(1)} %add_convert_fusion.rest_4_), channel_id=1, source_target_pairs={{0,16},{4,20},{8,24},{12,28},{1,17},{5,21},{9,25},{13,29},{2,18},{... | collective-permute-start | bytes 294920 | tf_op jit(solution)/shard_map/ppermute | solution.py:424
  28.7 5.4 %query_pass.5 = (bf16[4,768,768]{2,1,0:T(8,128)(2,1)S(1)}, f32[4,192,768]{2,1,0:T(8,128)S(1)}, bf16[4,192,192]{2,1,0:T(8,128)(2,1)S(1)}) custom-call(bf16[3072,768]{1,0:T(8,128)(2,1)S(1)} %get-tuple-element.27.tok_ref, bf16[192,768]{1,0:T(8,128)(2,1)S(1)} %bitcast.19, ...), custom_call_target="tpu_custom_call", output_to_operand_aliasing={{0}: (11, {}), {1}: (12, {}), {2}: (13, {})} | custom-call | flops 3000000000 | bytes 8000000 | tf_op jit(solution)/shard_map/query_pass/pallas_call | solution.py:204
  34.1 0.0 collective-permute-done.5.rest_2_
  34.1 4.0 %norm_pass.1 = (bf16[192,768]{1,0:T(8,128)(2,1)}, bf16[192,768]{1,0:T(8,128)(2,1)}, bf16[192,768]{1,0:T(8,128)(2,1)}, bf16[192,768]{1,0:T(8,128)(2,1)}, bf16[768,384]{1,0:T(8,128)(2,1)}) custom-call(f32[4,192,768]{2,1,0:T(8,128)S(1)} %get-tuple-element.38.raw_ref, bf16[4,768,768]{2,1,0:T(8,128)(2,1)S(1)} %get-tuple-element.39.qft_ref, ...), custom_call_target="tpu_custom_call" | custom-call | flops 3000000000 | bytes 8000000 | tf_op jit(solution)/shard_map/norm_pass/pallas_call | solution.py:261
  38.1 4.1 %all-to-all-start = ((bf16[32,24,384]{2,1,0:T(8,128)(2,1)}), bf16[32,24,384]{2,1,0:T(8,128)(2,1)S(1)}, u32[]{:S(2)}, u32[]{:S(2)}) async-start(bf16[32,24,384]{2,1,0:T(8,128)(2,1)} %bitcast.24), calls=%async_computation | async-start | bytes 1179648 | tf_op jit(solution)/shard_map/all_to_all | solution.py:434
  42.3 0.3 collective-permute-start.6
  42.6 1.7 %collective-permute-start.7 = (bf16[192,768]{1,0:T(8,128)(2,1)}, bf16[192,768]{1,0:T(8,128)(2,1)S(1)}, u32[]{:S(2)}, u32[]{:S(2)}) collective-permute-start(bf16[192,768]{1,0:T(8,128)(2,1)} %get-tuple-element.44), channel_id=1, source_target_pairs={{0,2},{1,3},{2,0},{3,1},{4,6},{5,7},{6,4},{7,5},{8,10},{9,11},{10,... | collective-permute-start | bytes 884744 | tf_op jit(solution)/shard_map/ppermute | solution.py:413
  44.3 0.0 collective-permute-done.6.rest_1_
  44.3 0.0 copy-start.3
  44.3 12.9 %collective-permute-done.7.rest_2_ = bf16[192,768]{1,0:T(8,128)(2,1)S(1)} collective-permute-done((bf16[192,768]{1,0:T(8,128)(2,1)}, bf16[192,768]{1,0:T(8,128)(2,1)S(1)}, u32[]{:S(2)}, u32[]{:S(2)}) %collective-permute-start.7) | collective-permute-done | bytes 294944 | tf_op jit(solution)/shard_map/ppermute | solution.py:413
  57.1 0.0 copy-start.4
  57.2 1.8 %all-to-all-done = bf16[32,24,384]{2,1,0:T(8,128)(2,1)S(1)} async-done(((bf16[32,24,384]{2,1,0:T(8,128)(2,1)}), bf16[32,24,384]{2,1,0:T(8,128)(2,1)S(1)}, u32[]{:S(2)}, u32[]{:S(2)}) %all-to-all-start) | async-done | bytes 589856 | tf_op jit(solution)/shard_map/all_to_all | solution.py:434
  59.0 0.0 copy-start.5
  59.0 7.3 %expert_pass.1 = bf16[256,768]{1,0:T(8,128)(2,1)} custom-call(bf16[8,4,24,384]{3,2,1,0:T(8,128)(2,1)S(1)} %bitcast.20, bf16[4,192,768]{2,1,0:T(8,128)(2,1)} %bitcast.21, bf16[1,768,3072]{2,1,0:T(8,128)(2,1)} %wi_hbm.1, bf16[1,3072,768]{2,1,0:T(8,128)(2,1)} %wd_hbm.1), custom_call_target="tpu_custom_call" | custom-call | flops 2000000000 | bytes 12000000 | tf_op jit(solution)/shard_map/expert_pass/pallas_call | solution.py:317
  66.3 0.0 copy-done.3
  66.3 0.0 copy-done.4
  66.3 3.4 %all-to-all-start.1 = ((bf16[32,8,768]{2,1,0:T(8,128)(2,1)}), bf16[32,8,768]{2,1,0:T(8,128)(2,1)S(1)}, u32[]{:S(2)}, u32[]{:S(2)}) async-start(bf16[32,8,768]{2,1,0:T(8,128)(2,1)} %bitcast.10), calls=%async_computation.1 | async-start | bytes 786432 | tf_op jit(solution)/shard_map/all_to_all | solution.py:441
  69.8 0.0 copy-done.5
  69.8 0.1 copy.21
  69.9 0.7 reshape.24.pick_ref
  70.5 0.0 copy-done.6
  70.5 1.5 %collective-permute-start.8 = (bf16[192,768]{1,0:T(8,128)(2,1)S(1)}, bf16[192,768]{1,0:T(8,128)(2,1)S(1)}, u32[]{:S(2)}, u32[]{:S(2)}) collective-permute-start(bf16[192,768]{1,0:T(8,128)(2,1)S(1)} %copy-done.6), channel_id=1, source_target_pairs={{0,3},{1,2},{2,1},{3,0},{4,7},{5,6},{6,5},{7,4},{8,11},{9,10},{10,... | collective-permute-start | bytes 884744 | tf_op jit(solution)/shard_map/ppermute | solution.py:413
  72.1 0.7 pad_add_fusion.me_ref
  72.7 5.1 %mix_pass.1.mix_ref = f32[768,768]{1,0:T(8,128)} custom-call(s32[2]{0:T(128)} %pad_add_fusion.me_ref, bf16[3072,768]{1,0:T(8,128)(2,1)} %tok_ref.1, bf16[4,192,768]{2,1,0:T(8,128)(2,1)} %bitcast.22, bf16[192,768]{1,0:T(8,128)(2,1)} %get-tuple-element.41.rest_0_, bf16[192,768]{1,0:T(8,128)(2,1)} %copy-done.3, bf16[192,768]{1,0:T(8,128)(2,1)} %copy-done.4), custom_call_target="tpu_custom_call" | custom-call | flops 2000000000 | bytes 6000000 | tf_op jit(solution)/shard_map/mix_pass/pallas_call | solution.py:347
  77.8 5.1 %collective-permute-done.8.attn_ref = bf16[192,768]{1,0:T(8,128)(2,1)S(1)} collective-permute-done((bf16[192,768]{1,0:T(8,128)(2,1)S(1)}, bf16[192,768]{1,0:T(8,128)(2,1)S(1)}, u32[]{:S(2)}, u32[]{:S(2)}) %collective-permute-start.8) | collective-permute-done | bytes 294944 | tf_op jit(solution)/shard_map/ppermute | solution.py:413
  82.9 0.0 all-to-all-done.1
  82.9 0.7 copy-done.7
  83.6 0.1 copy-done.2
  83.8 5.8 %combine_pass.1 = bf16[768,768]{1,0:T(8,128)(2,1)} custom-call(s32[2]{0:T(128)} %pad_add_fusion.me_ref, f32[768,768]{1,0:T(8,128)} %mix_pass.1.mix_ref, bf16[4,192,768]{2,1,0:T(8,128)(2,1)} %bitcast.23, bf16[192,768]{1,0:T(8,128)(2,1)} %copy-done.7, bf16[32,768]{1,0:T(8,128)(2,1)} %bitcast.30, s32[1,256]{1,0:T(1,128)} %reshape.24.pick_ref, ...), custom_call_target="tpu_custom_call" | custom-call | flops 2000000000 | bytes 6000000 | tf_op jit(solution)/shard_map/combine_pass/pallas_call | solution.py:379
  (6 shorter events, 0.1 us)
Async XLA Ops:
  0.8 15.0 %collective-permute-start = (s32[1,192]{1,0:T(1,128)S(1)}, s32[1,192]{1,0:T(1,128)S(1)}, u32[]{:S(2)}, u32[]{:S(2)}) collective-permute-start(s32[1,192]{1,0:T(1,128)S(1)} %reshape.22.rest_0_.rest_3_), channel_id=1, source_target_pairs={{0,1},{1,0},{2,3},{3,2},{4,5},{5,4},{6,7},{7,6},{8,9},{9,8},{10,11... | collective-permute-start | bytes 2312 | tf_op jit(solution)/shard_map/ppermute | solution.py:413
  1.2 14.6 %collective-permute-start.1 = (s32[1,192]{1,0:T(1,128)S(1)}, s32[1,192]{1,0:T(1,128)S(1)}, u32[]{:S(2)}, u32[]{:S(2)}) collective-permute-start(s32[1,192]{1,0:T(1,128)S(1)} %reshape.22.rest_0_.rest_3_), channel_id=1, source_target_pairs={{0,2},{1,3},{2,0},{3,1},{4,6},{5,7},{6,4},{7,5},{8,10},{9,11},{10,... | collective-permute-start | bytes 2312 | tf_op jit(solution)/shard_map/ppermute | solution.py:413
  3.8 12.0 %collective-permute-start.2 = (s32[1,192]{1,0:T(1,128)S(1)}, s32[1,192]{1,0:T(1,128)S(1)}, u32[]{:S(2)}, u32[]{:S(2)}) collective-permute-start(s32[1,192]{1,0:T(1,128)S(1)} %reshape.22.rest_0_.rest_3_), channel_id=1, source_target_pairs={{0,3},{1,2},{2,1},{3,0},{4,7},{5,6},{6,5},{7,4},{8,11},{9,10},{10,... | collective-permute-start | bytes 2312 | tf_op jit(solution)/shard_map/ppermute | solution.py:413
  3.9 11.9 %copy-start = (bf16[768,192]{0,1:T(8,128)(2,1)S(1)}, bf16[768,192]{0,1:T(8,128)(2,1)}, u32[]{:S(2)}) copy-start(bf16[768,192]{0,1:T(8,128)(2,1)} %param.11) | copy-start | bytes 884740
  3.9 11.9 %copy-start.1 = (f32[64,128]{1,0:T(8,128)S(1)}, f32[64,128]{1,0:T(8,128)}, u32[]{:S(2)}) copy-start(f32[64,128]{1,0:T(8,128)} %freq_ref.5) | copy-start | bytes 98308
  14.0 5.1 %collective-permute-start.3 = (bf16[192,256]{1,0:T(8,128)(2,1)S(1)}, bf16[192,256]{1,0:T(8,128)(2,1)S(1)}, u32[]{:S(2)}, u32[]{:S(2)}) collective-permute-start(bf16[192,256]{1,0:T(8,128)(2,1)S(1)} %get-tuple-element.31.rest_4_), channel_id=1, source_target_pairs={{0,4},{4,0},{8,12},{12,8},{16,20},{20,16},{24,28},{28,24},{1,5},{5... | collective-permute-start | bytes 294920 | tf_op jit(solution)/shard_map/ppermute | solution.py:424
  19.1 4.7 %collective-permute-start.4 = (bf16[192,256]{1,0:T(8,128)(2,1)S(1)}, bf16[192,256]{1,0:T(8,128)(2,1)S(1)}, u32[]{:S(2)}, u32[]{:S(2)}) collective-permute-start(bf16[192,256]{1,0:T(8,128)(2,1)S(1)} %add_convert_fusion.1.rest_4_), channel_id=1, source_target_pairs={{0,8},{4,12},{8,0},{12,4},{16,24},{20,28},{24,16},{28,20},{1,9},{5... | collective-permute-start | bytes 294920 | tf_op jit(solution)/shard_map/ppermute | solution.py:424
  23.8 10.3 %collective-permute-start.5 = (bf16[192,256]{1,0:T(8,128)(2,1)S(1)}, bf16[192,256]{1,0:T(8,128)(2,1)S(1)}, u32[]{:S(2)}, u32[]{:S(2)}) collective-permute-start(bf16[192,256]{1,0:T(8,128)(2,1)S(1)} %add_convert_fusion.rest_4_), channel_id=1, source_target_pairs={{0,16},{4,20},{8,24},{12,28},{1,17},{5,21},{9,25},{13,29},{2,18},{... | collective-permute-start | bytes 294920 | tf_op jit(solution)/shard_map/ppermute | solution.py:424
  38.1 20.9 %all-to-all-start = ((bf16[32,24,384]{2,1,0:T(8,128)(2,1)}), bf16[32,24,384]{2,1,0:T(8,128)(2,1)S(1)}, u32[]{:S(2)}, u32[]{:S(2)}) async-start(bf16[32,24,384]{2,1,0:T(8,128)(2,1)} %bitcast.24), calls=%async_computation | async-start | bytes 1179648 | tf_op jit(solution)/shard_map/all_to_all | solution.py:434
  42.3 2.0 %collective-permute-start.6 = (bf16[192,768]{1,0:T(8,128)(2,1)}, bf16[192,768]{1,0:T(8,128)(2,1)S(1)}, u32[]{:S(2)}, u32[]{:S(2)}) collective-permute-start(bf16[192,768]{1,0:T(8,128)(2,1)} %get-tuple-element.43), channel_id=1, source_target_pairs={{0,1},{1,0},{2,3},{3,2},{4,5},{5,4},{6,7},{7,6},{8,9},{9,8},{10,11... | collective-permute-start | bytes 884744 | tf_op jit(solution)/shard_map/ppermute | solution.py:413
  42.6 14.6 %collective-permute-start.7 = (bf16[192,768]{1,0:T(8,128)(2,1)}, bf16[192,768]{1,0:T(8,128)(2,1)S(1)}, u32[]{:S(2)}, u32[]{:S(2)}) collective-permute-start(bf16[192,768]{1,0:T(8,128)(2,1)} %get-tuple-element.44), channel_id=1, source_target_pairs={{0,2},{1,3},{2,0},{3,1},{4,6},{5,7},{6,4},{7,5},{8,10},{9,11},{10,... | collective-permute-start | bytes 884744 | tf_op jit(solution)/shard_map/ppermute | solution.py:413
  44.3 22.0 %copy-start.3 = (bf16[192,768]{1,0:T(8,128)(2,1)}, bf16[192,768]{1,0:T(8,128)(2,1)S(1)}, u32[]{:S(2)}) copy-start(bf16[192,768]{1,0:T(8,128)(2,1)S(1)} %collective-permute-done.6.rest_1_) | copy-start | bytes 884740
  57.1 9.2 %copy-start.4 = (bf16[192,768]{1,0:T(8,128)(2,1)}, bf16[192,768]{1,0:T(8,128)(2,1)S(1)}, u32[]{:S(2)}) copy-start(bf16[192,768]{1,0:T(8,128)(2,1)S(1)} %collective-permute-done.7.rest_2_) | copy-start | bytes 884740
  59.0 10.8 %copy-start.5 = (s32[32,1,6]{0,1,2:T(1,128)S(1)}, s32[32,1,6]{0,1,2:T(1,128)}, u32[]{:S(2)}) copy-start(s32[32,1,6]{0,1,2:T(1,128)} %param.19) | copy-start | bytes 2308
  59.0 11.5 %copy-start.6 = (bf16[192,768]{1,0:T(8,128)(2,1)S(1)}, bf16[192,768]{1,0:T(8,128)(2,1)}, u32[]{:S(2)}) copy-start(bf16[192,768]{1,0:T(8,128)(2,1)} %get-tuple-element.47) | copy-start | bytes 884740
  66.3 16.6 %all-to-all-start.1 = ((bf16[32,8,768]{2,1,0:T(8,128)(2,1)}), bf16[32,8,768]{2,1,0:T(8,128)(2,1)S(1)}, u32[]{:S(2)}, u32[]{:S(2)}) async-start(bf16[32,8,768]{2,1,0:T(8,128)(2,1)} %bitcast.10), calls=%async_computation.1 | async-start | bytes 786432 | tf_op jit(solution)/shard_map/all_to_all | solution.py:441
  70.5 12.4 %collective-permute-start.8 = (bf16[192,768]{1,0:T(8,128)(2,1)S(1)}, bf16[192,768]{1,0:T(8,128)(2,1)S(1)}, u32[]{:S(2)}, u32[]{:S(2)}) collective-permute-start(bf16[192,768]{1,0:T(8,128)(2,1)S(1)} %copy-done.6), channel_id=1, source_target_pairs={{0,3},{1,2},{2,1},{3,0},{4,7},{5,6},{6,5},{7,4},{8,11},{9,10},{10,... | collective-permute-start | bytes 884744 | tf_op jit(solution)/shard_map/ppermute | solution.py:413
  82.9 0.7 copy-start.7
  82.9 0.8 copy-start.2

commit v4 on v3

v4 whole, which is shorter than its diff:
```python
import functools
import math

import jax
import jax.numpy as jnp
from jax import lax
from jax.experimental import pallas as pl
from jax.experimental.pallas import tpu as pltpu
from jax.sharding import PartitionSpec as P

HD = 64
EPS = 1e-06
CHUNK = 256
PAD = 8
BF = jnp.bfloat16
F32 = jnp.float32
MIB = 2**20
KEPT = 24
LANES = 128
SIN = (3.14158202, -5.16714279, 2.54189901, -0.55463616)
COS = (0.9999933, -4.93393802, 4.04128381, -1.22212701)


def nn(a, b):
    return lax.dot_general(a, b, (((1,), (0,)), ((), ())), preferred_element_type=F32)


def nt(a, b):
    return lax.dot_general(a, b, (((1,), (1,)), ((), ())), preferred_element_type=F32)


def tn(a, b):
    return lax.dot_general(a, b, (((0,), (0,)), ((), ())), preferred_element_type=F32)


def wave(turns, scale):
    big = F32(1.5 * 2.0**23)
    r = turns - ((turns + big) - big)
    u = r * r
    root = math.sqrt(2 * scale)
    a = [F32(v * root) for v in SIN]
    b = [F32(v * root) for v in COS]
    s = r * (a[0] + u * (a[1] + u * (a[2] + u * a[3])))
    c = b[0] + u * (b[1] + u * (b[2] + u * b[3]))
    return F32(scale) - s * s, s * c


def parts(f):
    hi = f.astype(BF)
    rest = f - hi.astype(F32)
    mid = rest.astype(BF)
    lo = (rest - mid.astype(F32)).astype(BF)
    return [hi, mid, lo]


def whole(shape):
    return pl.BlockSpec(shape, lambda *_: (0,) * len(shape))


def params(mib=60):
    return pltpu.CompilerParams(vmem_limit_bytes=mib * MIB)


def far(x):
    return pltpu.with_memory_space_constraint(x, pltpu.HBM)


def cost(flops, nbytes):
    return pl.CostEstimate(flops=int(flops), bytes_accessed=int(nbytes), transcendentals=0)


HERE = pl.BlockSpec(memory_space=pltpu.VMEM)
AWAY = pl.BlockSpec(memory_space=pl.ANY)
FAR = pl.BlockSpec(memory_space=pltpu.HBM)


def key_kernel(size, tok_hbm, wkt_hbm, wvt_hbm, freq_hbm, pick_ref, *rest):
    tok_ref, kf_ref, vt_ref, sc_ref, tot_ref, own_ref, w_ref, freq_ref, sems = rest
    total = tok_ref.shape[0]
    wid = wkt_hbm.shape[0]
    heads = wid // HD
    half = freq_ref.shape[1]
    feat = 2 * half
    count = total // size
    weights = [
        pltpu.make_async_copy(w, w_ref.at[pl.ds(i * wid, wid)], sems.at[i])
        for i, w in enumerate((wkt_hbm, wvt_hbm))
    ]
    weights.append(pltpu.make_async_copy(freq_hbm, freq_ref, sems.at[2]))
    loads = [
        pltpu.make_async_copy(
            tok_hbm.at[pl.ds(i * size, size)], tok_ref.at[pl.ds(i * size, size)], sems.at[3 + i]
        )
        for i in range(count)
    ]
    for copy in [weights[0], loads[0], *weights[1:], *loads[1:]]:
        copy.start()
    for copy in weights:
        copy.wait()
    f3 = jnp.concatenate(parts(freq_ref[...] * F32(0.5 / math.pi)), axis=0)
    state = [jnp.zeros((HD, feat), F32) for _ in range(heads)]
    units = [(i, j, h) for i in range(count) for j in range(0, size, CHUNK) for h in range(heads)]
    per = len(units) // count
    key, val, phase, feats = {}, {}, {}, {}

    def project(i):
        loads[i].wait()
        span = slice(i * size, (i + 1) * size)
        out = nt(tok_ref[span, :], w_ref[...]).astype(BF)
        key[i] = out[:, :wid]
        val[i] = out[:, wid:].T
        vt_ref[:, span] = val[i]

    def turn(u):
        i, j, h = u
        k = key[i][j : j + CHUNK, h * HD : (h + 1) * HD]
        phase[u] = nn(jnp.concatenate([k] * 3, axis=1), f3)

    def feature(u):
        i, j, h = u
        c, s = wave(phase.pop(u), 1 / math.sqrt(half))
        feats[u] = jnp.concatenate([c.astype(BF), s.astype(BF)], axis=1)
        kf_ref[i * size + j : i * size + j + CHUNK, h * feat : (h + 1) * feat] = feats[u]

    def gather(u):
        i, j, h = u
        mine = slice(h * HD, (h + 1) * HD)
        sc_ref[(i * size + j) // CHUNK, mine, :] = state[h].astype(BF)
        state[h] = state[h] + nn(val[i][mine, j : j + CHUNK], feats.pop(u))

    project(0)
    for t in range(len(units) + 2):
        if t % per == per // 2 and t // per + 1 < count:
            project(t // per + 1)
        if t < len(units):
            turn(units[t])
        if 0 <= t - 1 < len(units):
            feature(units[t - 1])
        if 0 <= t - 2 < len(units):
            gather(units[t - 2])
    for h in range(heads):
        tot_ref[h * HD : (h + 1) * HD, :] = state[h].astype(BF)
    own_ref[...] = jnp.concatenate([pick_ref[c] for c in range(pick_ref.shape[0])], axis=1)


def key_pass(tokens, wkt, wvt, freq, picks, size):
    total, d = tokens.shape
    wid = wkt.shape[0]
    feat = 2 * freq.shape[1]
    heads = wid // HD
    return pl.pallas_call(
        functools.partial(key_kernel, size),
        in_specs=[FAR] * 4 + [HERE],
        out_specs=[HERE] * 6,
        out_shape=[
            jax.ShapeDtypeStruct(tokens.shape, BF),
            jax.ShapeDtypeStruct((total, heads * feat), BF),
            jax.ShapeDtypeStruct((wid, total), BF),
            jax.ShapeDtypeStruct((total // CHUNK, wid, feat), BF),
            jax.ShapeDtypeStruct((wid, feat), BF),
            jax.ShapeDtypeStruct((1, picks.size), jnp.int32),
        ],
        scratch_shapes=[
            pltpu.VMEM((2 * wid, d), BF),
            pltpu.VMEM(freq.shape, F32),
            pltpu.SemaphoreType.DMA((3 + total // size,)),
        ],
        compiler_params=params(KEPT),
        cost_estimate=cost(5e9, 12e6),
        name="key_pass",
    )(*map(far, (tokens, wkt, wvt, freq)), picks)


def chosen(slot, pick_refs):
    row = pick_refs[0][...]
    for k in range(1, len(pick_refs)):
        row = jnp.where(slot == k, pick_refs[k][...], row)
    return row


def marks(row, rows):
    at = lax.broadcasted_iota(jnp.int32, (rows, row.shape[1]), 0)
    return (at == row).astype(F32).astype(BF)


def query_kernel(chunks, slots, picked, tok_ref, freq_ref, wqt_ref, kf_ref, vt_ref, sc_ref, *rest):
    pick_refs = rest[:picked]
    qft_ref, raw_ref = rest[-2 - (picked > 0) :][:2]
    wid = wqt_ref.shape[0]
    heads = wid // HD
    half = freq_ref.shape[1]
    feat = 2 * half
    rows = tok_ref.shape[0] // slots
    me = lax.axis_index("head")
    f3t = jnp.concatenate(parts(freq_ref[...].T * F32(0.5 / math.pi)), axis=1)
    place = [lax.broadcasted_iota(jnp.int32, (CHUNK, CHUNK), i) for i in (0, 1)]
    keep = place[0] <= place[1]
    units = [(c * CHUNK // rows, c * CHUNK % rows, h) for c in chunks for h in range(heads)]
    base = chunks[0] * CHUNK
    span = slice(base, base + len(chunks) * CHUNK)
    query = nt(tok_ref[span, :], wqt_ref[...]).astype(BF).T
    phase, feats, both = {}, {}, {}

    def spot(u):
        b, j, h = u
        return slice(h * HD, (h + 1) * HD), slice(b * rows + j, b * rows + j + CHUNK), slice(h * feat, (h + 1) * feat)

    def select(b):
        span = slice(b * rows, (b + 1) * rows)
        start = me * wid
        wide = -(-wid // LANES) * LANES
        low = pl.multiple_of(start // LANES * LANES, LANES)
        window = tok_ref[span, pl.ds(low, wide)]
        columns = window[:, :wid]
        for shift in range(math.gcd(wid, LANES), wide - wid + 1, math.gcd(wid, LANES)):
            columns = jnp.where(start % LANES == shift, window[:, shift : shift + wid], columns)
        rest[-1][b] = tn(columns, marks(chosen(me ^ b, pick_refs), rows)).astype(BF)

    def turn(u):
        mine, cols, _ = spot(u)
        q = query[mine, cols.start - base : cols.stop - base]
        phase[u] = nn(f3t, jnp.concatenate([q] * 3, axis=0))

    def feature(u):
        b, j, h = u
        c, s = wave(phase.pop(u), 1 / math.sqrt(half))
        feats[u] = jnp.concatenate([c.astype(BF), s.astype(BF)], axis=0)
        qft_ref[b, h * feat : (h + 1) * feat, j : j + CHUNK] = feats[u]

    def score(u):
        mine, cols, lines = spot(u)
        keys = jnp.concatenate([kf_ref[cols, lines], sc_ref[cols.start // CHUNK, mine, :]], axis=0)
        both[u] = nn(keys, feats.pop(u))

    def total(u):
        b, j, h = u
        mine, cols, _ = spot(u)
        got = both.pop(u)
        scores = jnp.where(keep, got[:CHUNK], 0.0).astype(BF)
        raw_ref[b, mine, j : j + CHUNK] = nn(vt_ref[mine, cols], scores) + got[CHUNK:]

    stages = (turn, feature, score, total)
    lag = 2
    for t in range(len(units) + lag * (len(stages) - 1)):
        if picked and t % heads == heads - 1 and t // heads < slots:
            select(t // heads)
        for i, stage in enumerate(stages):
            if 0 <= t - lag * i < len(units):
                stage(units[t - lag * i])


def query_pass(chunks, tokens, freq, wqt, kf, vt, sc, picks, slots, into):
    total, d = tokens.shape
    rows = total // slots
    wid = wqt.shape[0]
    feat = 2 * freq.shape[1]
    heads = wid // HD
    out_shape = [
        jax.ShapeDtypeStruct((slots, heads * feat, rows), BF),
        jax.ShapeDtypeStruct((slots, wid, rows), F32),
    ]
    if picks:
        out_shape.append(jax.ShapeDtypeStruct((slots, wid, picks[0].shape[1]), BF))
    args = [tokens, freq, wqt, kf, vt, sc, *picks, *into]
    return pl.pallas_call(
        functools.partial(query_kernel, chunks, slots, len(picks)),
        in_specs=[HERE] * (len(args) - len(into)) + [AWAY] * len(into),
        out_specs=[HERE] * len(out_shape),
        out_shape=out_shape,
        input_output_aliases={len(args) - len(into) + i: i for i in range(2) if into},
        compiler_params=params(KEPT),
        cost_estimate=cost(5e8 * len(chunks), 1e6 * len(chunks)),
        name="query_pass",
    )(*args)


def norm_kernel(slots, cap, rounds, raw_ref, qft_ref, seen_ref, *rest):
    got_refs, pick_refs = rest[:rounds], rest[rounds : rounds + slots]
    outs = rest[rounds + slots : rounds + 2 * slots]
    sent_hbm, ready, acc, sent, sems = rest[rounds + 2 * slots :]
    me, at = lax.axis_index("head"), lax.axis_index("seq")
    wid = raw_ref.shape[1]
    heads = wid // HD
    feat = got_refs[0].shape[1]
    before = jnp.zeros(got_refs[0].shape, F32)
    for i, got in enumerate(got_refs):
        before = before + jnp.where((at & (1 << i)) > 0, got[...].astype(F32), 0.0)
    before = before.astype(BF)
    copies = [pltpu.make_async_copy(ready.at[k], outs[k], sems.at[k]) for k in range(slots)]
    picked = {}

    def norm(k):
        block = me ^ k
        for h in range(heads):
            mine = slice(h * HD, (h + 1) * HD)
            raw = raw_ref[block, mine, :] + nn(before[mine, :], qft_ref[block, h * feat : (h + 1) * feat, :])
            meansq = jnp.mean(raw * raw, axis=0, keepdims=True)
            ready[k, mine, :] = (raw * lax.rsqrt(meansq + F32(EPS))).astype(BF)
        copies[k].start()

    def pick(k):
        picked[k] = nn(ready[k], marks(pick_refs[k][...], ready.shape[2])).astype(BF)

    def spread(k):
        both = jnp.concatenate([picked.pop(k), seen_ref[me ^ k]], axis=0)
        n = both.shape[1]
        experts = n // cap
        entry = lax.broadcasted_iota(jnp.int32, (1, n), 1)
        row = (entry % experts * slots + (me ^ k)) * cap + entry // experts
        part = nt(marks(row, acc.shape[0]), both)
        acc[...] = part if k == 0 else acc[...] + part

    stages = (norm, pick, spread)
    for t in range(slots + len(stages) - 1):
        for i, stage in enumerate(stages):
            if 0 <= t - i < slots:
                stage(t - i)
    sent[...] = acc[...].astype(BF)
    last = pltpu.make_async_copy(sent, sent_hbm, sems.at[slots])
    last.start()
    for copy in copies:
        copy.wait()
    last.wait()


def norm_pass(raw, qft, seen, got, picks, cap):
    slots, wid, rows = raw.shape
    n = slots * picks[0].shape[1]
    return pl.pallas_call(
        functools.partial(norm_kernel, slots, cap, len(got)),
        in_specs=[HERE] * (3 + len(got) + slots),
        out_specs=[FAR] * (slots + 1),
        out_shape=[pltpu.HBM((wid, rows), BF)] * slots + [pltpu.HBM((n, 2 * wid), BF)],
        scratch_shapes=[
            pltpu.VMEM((slots, wid, rows), BF),
            pltpu.VMEM((n, 2 * wid), F32),
            pltpu.VMEM((n, 2 * wid), BF),
            pltpu.SemaphoreType.DMA((slots + 1,)),
        ],
        compiler_params=params(KEPT + n * wid * 20 // MIB),
        cost_estimate=cost(3e9, 8e6),
        name="norm_pass",
    )(raw, qft, seen, *got, *picks)


def expert_kernel(cap, tiles, got_hbm, wo_hbm, wi_hbm, wd_hbm, out_ref, got, wo, wi, wd, taken, acc, sems):
    slots, ring, each, both = got.shape
    wid = both // 2
    n, d = ring * each, wo.shape[2]
    ff = wi.shape[1]
    tile = ff // tiles
    landing = [pltpu.make_async_copy(got_hbm.at[:, h], got.at[h], sems.at[h]) for h in range(slots)]
    copies = [pltpu.make_async_copy(wo_hbm, wo, sems.at[slots])]
    first = slots + 1
    for t in range(tiles):
        cut = pl.ds(t * tile, tile)
        copies.append(pltpu.make_async_copy(wi_hbm.at[0, :, cut], wi.at[:, cut], sems.at[first + 2 * t]))
        copies.append(pltpu.make_async_copy(wd_hbm.at[0, cut, :], wd.at[cut, :], sems.at[first + 1 + 2 * t]))
    for c in landing + copies:
        c.start()
    for c in landing:
        c.wait()
    parts_in = [got[h].reshape(n, both) for h in range(slots)]
    mixed = jnp.concatenate([g.astype(F32)[:, wid:] for g in parts_in], axis=1)
    copies[0].wait()
    for h, g in enumerate(parts_in):
        mixed = mixed + nn(g[:, :wid], wo[h])
    taken[...] = mixed.astype(BF)
    acc[...] = jnp.zeros((n, d), F32)
    for t in range(tiles):
        cut = slice(t * tile, (t + 1) * tile)
        copies[1 + 2 * t].wait()
        inner = jax.nn.gelu(nn(taken[...], wi[:, cut]), approximate=True).astype(BF)
        copies[2 + 2 * t].wait()
        acc[...] += nn(inner, wd[cut, :])
    m = out_ref.shape[0]
    at = lax.broadcasted_iota(jnp.int32, (1, n), 1)
    out_ref[...] = nn(marks(at // cap * PAD + at % cap, m), acc[...].astype(BF)).astype(BF)


def expert_pass(arrived, w_out, w_in, w_down, cap, tiles=3):
    ring, slots, each, both = arrived.shape
    d, ff = w_in.shape[1:]
    m = ring * each // cap * PAD
    return pl.pallas_call(
        functools.partial(expert_kernel, cap, tiles),
        in_specs=[AWAY] + [FAR] * 3,
        out_specs=HERE,
        out_shape=jax.ShapeDtypeStruct((m, d), BF),
        scratch_shapes=[
            pltpu.VMEM((slots, ring, each, both), BF),
            pltpu.VMEM(w_out.shape, BF),
            pltpu.VMEM((d, ff), BF),
            pltpu.VMEM((ff, d), BF),
            pltpu.VMEM((ring * each, d), BF),
            pltpu.VMEM((ring * each, d), F32),
            pltpu.SemaphoreType.DMA((slots + 1 + 2 * tiles,)),
        ],
        compiler_params=params(40),
        cost_estimate=cost(2e9, 12e6),
        name="expert_pass",
    )(arrived, *map(far, (w_out, w_in, w_down)))


def mix_kernel(slots, tok_hbm, wo_hbm, *rest):
    attns, (out_ref, tok, wo, sems) = rest[:-4], rest[-4:]
    me = lax.axis_index("head")
    rows = tok.shape[0]
    first = pl.multiple_of(me * rows, rows)
    copies = [pltpu.make_async_copy(tok_hbm.at[pl.ds(first, rows)], tok, sems.at[0])]
    copies += [pltpu.make_async_copy(wo_hbm.at[me ^ k], wo.at[k], sems.at[1 + k]) for k in range(slots)]
    for copy in copies:
        copy.start()
    for copy in copies:
        copy.wait()
    mixed = tok[...].astype(F32)
    for k in range(slots):
        mixed = mixed + tn(attns[k][...], wo[k])
    out_ref[...] = mixed


def mix_pass(tokens, w_out, attns, rows):
    d = tokens.shape[1]
    slots = len(attns)
    return pl.pallas_call(
        functools.partial(mix_kernel, slots),
        in_specs=[FAR] * 2 + [HERE] * slots,
        out_specs=HERE,
        out_shape=jax.ShapeDtypeStruct((rows, d), F32),
        scratch_shapes=[
            pltpu.VMEM((rows, d), BF),
            pltpu.VMEM((slots,) + w_out.shape[1:], BF),
            pltpu.SemaphoreType.DMA((1 + slots,)),
        ],
        compiler_params=params(),
        cost_estimate=cost(2e9, 6e6),
        name="mix_pass",
    )(far(tokens), far(w_out), *attns)


def combine_kernel(last, tiles, mix_hbm, wo_hbm, attn_hbm, router_ref, pick_ref, back_hbm, out_hbm, *scratch):
    mix, wo, attn, back, out, in_sems, out_sems = scratch
    me = lax.axis_index("head")
    rows = mix.shape[0]
    tile = rows // tiles
    cuts = [pl.ds(t * tile, tile) for t in range(tiles)]
    need = [
        pltpu.make_async_copy(wo_hbm.at[me ^ last], wo, in_sems.at[0]),
        pltpu.make_async_copy(attn_hbm, attn, in_sems.at[1]),
    ]
    later = pltpu.make_async_copy(back_hbm, back, in_sems.at[2])
    loads = [pltpu.make_async_copy(mix_hbm.at[c], mix.at[c], in_sems.at[3 + t]) for t, c in enumerate(cuts)]
    stores = [pltpu.make_async_copy(out.at[c], out_hbm.at[c], out_sems.at[t]) for t, c in enumerate(cuts)]
    for copy in [*need, loads[0], later, *loads[1:]]:
        copy.start()
    for copy in need:
        copy.wait()
    experts, n = router_ref.shape[0], pick_ref.shape[1]
    spreads = marks(lax.broadcasted_iota(jnp.int32, (1, n), 1) // PAD, experts)
    for t, cut in enumerate(cuts):
        loads[t].wait()
        hidden = (mix[cut, :] + tn(attn[:, t * tile : (t + 1) * tile], wo[...])).astype(BF)
        gate = jax.nn.sigmoid(nt(hidden, router_ref[...])).astype(BF)
        at = lax.broadcasted_iota(jnp.int32, (tile, n), 0) + t * tile
        comb = jnp.where(pick_ref[...] == at, nn(gate, spreads), 0.0).astype(BF)
        if t == 0:
            later.wait()
        out[cut, :] = (hidden.astype(F32) + nn(comb, back[...])).astype(BF)
        stores[t].start()
    for store in stores:
        store.wait()


def combine_pass(mixed, w_out, attn, router_t, pick_row, back, tiles=2):
    rows, d = mixed.shape
    last = w_out.shape[0] - 1
    return pl.pallas_call(
        functools.partial(combine_kernel, last, tiles),
        in_specs=[FAR, FAR, AWAY, HERE, HERE, AWAY],
        out_specs=AWAY,
        out_shape=jax.ShapeDtypeStruct((rows, d), BF),
        scratch_shapes=[
            pltpu.VMEM((rows, d), F32),
            pltpu.VMEM(w_out.shape[1:], BF),
            pltpu.VMEM(attn.shape, BF),
            pltpu.VMEM(back.shape, BF),
            pltpu.VMEM((rows, d), BF),
            pltpu.SemaphoreType.DMA((3 + tiles,)),
            pltpu.SemaphoreType.DMA((tiles,)),
        ],
        compiler_params=params(40),
        cost_estimate=cost(2e9, 6e6),
        name="combine_pass",
    )(far(mixed), far(w_out), attn, router_t, pick_row, back)


def per_device(tokens, w_query, w_key, w_value, freq, w_out, router, w_in, w_down, picks):
    total, d = tokens.shape
    group = lax.axis_size("head")
    ring = lax.axis_size("seq")
    rows = total // group
    experts, _, cap = picks.shape
    wid = w_query.shape[1]

    pick_row = jnp.pad(picks[:, 0, :], ((0, 0), (0, PAD - cap)), constant_values=-1).reshape(1, experts * PAD)
    swap = lambda x, k: lax.ppermute(x, "head", [(i, i ^ k) for i in range(group)])

    tok_here, kf, vt, sc, held, own = key_pass(
        tokens, w_key.T, w_value.T, freq, picks.transpose(2, 1, 0), rows
    )
    near = [own] + [swap(own, k) for k in range(1, group)]
    got, made = [], []
    chunks = total // CHUNK
    rounds = ring.bit_length() - 1
    for i in range(rounds):
        got.append(lax.ppermute(held, "seq", [(j, j ^ (1 << i)) for j in range(ring)]))
        part = range(chunks * i // rounds, chunks * (i + 1) // rounds)
        made = query_pass(
            part, tok_here, freq, w_query.T, kf, vt, sc, near if i == rounds - 1 else [], group, made
        )
        both = held.astype(F32) + got[-1].astype(F32)
        held, *made = lax.optimization_barrier([both.astype(BF), *made])
    qft, raw, seen = made
    *attns, sent = norm_pass(raw, qft, seen, got, near, cap)

    sent = sent.reshape(experts, group * cap, 2 * wid)
    arrived = lax.all_to_all(sent, ("seq", "head"), split_axis=0, concat_axis=0, tiled=True)
    early = [swap(attns[k], k) for k in range(1, group - 1)]
    arrived, pick_row, *early = lax.optimization_barrier([arrived, pick_row, *early])
    w_out = w_out.reshape(group, wid, d)
    result = expert_pass(
        arrived.reshape(ring, group, group * cap, 2 * wid), w_out, w_in, w_down, cap
    )
    back = lax.all_to_all(
        result.reshape(experts, PAD, d), ("seq", "head"), split_axis=0, concat_axis=0, tiled=True
    )
    late = swap(attns[-1], group - 1)
    mixed = mix_pass(tokens, w_out, [attns[0], *early], rows)
    return combine_pass(
        mixed, w_out, late, router.T, pick_row, back.reshape(experts * PAD, d)
    )


def solution(mesh):
    in_specs = (
        P("seq", None),
        P(None, "head"),
        P(None, "head"),
        P(None, "head"),
        P(),
        P(),
        P(),
        P(("seq", "head"), None, None),
        P(("seq", "head"), None, None),
        P(None, ("seq", "head"), None),
    )
    out_specs = P(("seq", "head"), None)
    return jax.shard_map(
        per_device, mesh=mesh, in_specs=in_specs, out_specs=out_specs, check_vma=False
    )
```

time: 90 us -> 82.5 us (0.917)
  Pallas kernels: 43.1 us -> 37.2 us
  local copies, waits for them, and re-layouts: 2.41 us -> 0.9 us
    pallas_call x6, Pallas kernels: 31.8 us -> 27.8 us  [the longest x3 9.73 us: query_pass(): pl.pallas_call(functools.partial(query_kernel, chunks, slots, len(picks))...]
    ppermute x3, starting transfers between devices: 8.57 us -> 6.5 us  [per_device(): lax.ppermute(held, 'seq', [(j, j ^ 1 << i) for j in range(ring)])]
    all_to_all x1, starting transfers between devices: 4.13 us -> 5.48 us  [per_device(): lax.all_to_all(sent, ('seq', 'head'), split_axis=0, concat_axis=0, tiled=...]
    pallas_call x1, Pallas kernels: 4.01 us -> 3.02 us  [norm_pass(): pl.pallas_call(functools.partial(norm_kernel, slots, cap, len(got)), in_s...]
    pallas_call x1, Pallas kernels: 7.28 us -> 6.36 us  [expert_pass(): pl.pallas_call(functools.partial(expert_kernel, cap, tiles), in_specs=[AW...]
  transfers between devices with their start and end apart: 11 -> 11, of which waited for: 5 -> 5; matrix products, arithmetic and copies ran while one was open for 2% -> 0% of each run, Pallas kernels for 29% -> 18%
where the time goes in v4:
time: 82.5 us; the launch traced here: 82.1 us
  Pallas kernels  37.2 us (45%)
  starting transfers between devices  22.2 us (27%)
  waiting for transfers between devices  21.4 us (26%)
  local copies, waits for them, and re-layouts  0.9 us (1%)
    ppermute x6, waiting for transfers between devices, per_device(): lax.ppermute(x, 'head', [(i, i ^ k) for i in range(group)])  18.8 us
    pallas_call x3, Pallas kernels, query_pass(): pl.pallas_call(functools.partial(query_kernel, chunks, slots, len(picks))...  9.73 us
    pallas_call x1, Pallas kernels, key_pass(): pl.pallas_call(functools.partial(key_kernel, size), in_specs=[FAR] * 4 +...  8.52 us
    ppermute x6, starting transfers between devices, per_device(): lax.ppermute(x, 'head', [(i, i ^ k) for i in range(group)])  6.74 us
    ppermute x3, starting transfers between devices, per_device(): lax.ppermute(held, 'seq', [(j, j ^ 1 << i) for j in range(ring)])  6.5 us
    pallas_call x1, Pallas kernels, expert_pass(): pl.pallas_call(functools.partial(expert_kernel, cap, tiles), in_specs=[AW...  6.36 us
    all_to_all x1, starting transfers between devices, per_device(): lax.all_to_all(sent, ('seq', 'head'), split_axis=0, concat_axis=0, tiled=...  5.48 us
    pallas_call x1, Pallas kernels, mix_pass(): pl.pallas_call(functools.partial(mix_kernel, slots), in_specs=[FAR] * 2 +...  5.22 us
  transfers between devices with their start and end apart: 11, of which 5 were waited for; matrix products, arithmetic and copies ran while one was open for 0% of the time, Pallas kernels for 18%

profile of v4, /device:TPU:0, one launch (start us, length us, event | category | flops | bytes accessed | tf_op | source)
XLA Modules:
  0.0 82.1 jit_solution(10159027195225372525)
XLA Ops:
  0.0 0.0 copy-start.2
  0.0 0.7 copy-done.2
  0.7 0.0 copy-start
  0.7 0.0 copy-start.1
  0.7 8.5 %key_pass.1 = (bf16[3072,768]{1,0:T(8,128)(2,1)S(1)}, bf16[3072,768]{1,0:T(8,128)(2,1)S(1)}, bf16[192,3072]{1,0:T(8,128)(2,1)S(1)}, bf16[12,192,256]{2,1,0:T(8,1...) custom-call(bf16[3072,768]{1,0:T(8,128)(2,1)} %tok_hbm.3, bf16[192,768]{1,0:T(8,128)(2,1)} %bitcast.24, ...), custom_call_target="tpu_custom_call" | custom-call | flops 5000000000 | bytes 12000000 | tf_op jit(solution)/shard_map/key_pass/pallas_call | solution.py:151
  9.2 0.5 collective-permute-start
  9.7 2.6 %collective-permute-start.1 = (s32[1,192]{1,0:T(1,128)S(1)}, s32[1,192]{1,0:T(1,128)S(1)}, u32[]{:S(2)}, u32[]{:S(2)}) collective-permute-start(s32[1,192]{1,0:T(1,128)S(1)} %get-tuple-element.37.rest_0_.rest_3_), channel_id=1, source_target_pairs={{0,2},{1,3},{2,0},{3,1},{4,6},{5,7},{6,4},{7,5},{8,10},{9,11},{10,... | collective-permute-start | bytes 2312 | tf_op jit(solution)/shard_map/ppermute | solution.py:506
  12.3 0.1 collective-permute-start.2
  12.4 1.7 %collective-permute-start.3 = (bf16[192,256]{1,0:T(8,128)(2,1)S(1)}, bf16[192,256]{1,0:T(8,128)(2,1)S(1)}, u32[]{:S(2)}, u32[]{:S(2)}) collective-permute-start(bf16[192,256]{1,0:T(8,128)(2,1)S(1)} %get-tuple-element.38), channel_id=1, source_target_pairs={{0,4},{4,0},{8,12},{12,8},{16,20},{20,16},{24,28},{28,24},{1,5},{5... | collective-permute-start | bytes 294920 | tf_op jit(solution)/shard_map/ppermute | solution.py:516
  14.1 0.0 copy-done
  14.1 0.0 copy-done.1
  14.1 2.8 %query_pass.3 = (bf16[4,768,768]{2,1,0:T(8,128)(2,1)S(1)}, f32[4,192,768]{2,1,0:T(8,128)S(1)}) custom-call(bf16[3072,768]{1,0:T(8,128)(2,1)S(1)} %get-tuple-element.33.tok_ref, f32[64,128]{1,0:T(8,128)S(1)} %copy-done.1, bf16[192,768]{1,0:T(8,128)(2,1)S(1)} %bitcast.12, bf16[3072,768]{1,0:T(8,128)(2,1)S(1)} %get-tuple-element.34.kf_ref, ...), custom_call_target="tpu_custom_call" | custom-call | flops 2000000000 | bytes 4000000 | tf_op jit(solution)/shard_map/query_pass/pallas_call | solution.py:265
  16.9 0.5 collective-permute-done.3.rest_0_
  17.5 1.9 %collective-permute-start.4 = (bf16[192,256]{1,0:T(8,128)(2,1)S(1)}, bf16[192,256]{1,0:T(8,128)(2,1)S(1)}, u32[]{:S(2)}, u32[]{:S(2)}) collective-permute-start(bf16[192,256]{1,0:T(8,128)(2,1)S(1)} %add_convert_fusion.1), channel_id=1, source_target_pairs={{0,8},{4,12},{8,0},{12,4},{16,24},{20,28},{24,16},{28,20},{1,9},{5... | collective-permute-start | bytes 294920 | tf_op jit(solution)/shard_map/ppermute | solution.py:516
  19.3 2.8 %query_pass.4 = (bf16[4,768,768]{2,1,0:T(8,128)(2,1)S(1)}, f32[4,192,768]{2,1,0:T(8,128)S(1)}) custom-call(bf16[3072,768]{1,0:T(8,128)(2,1)S(1)} %get-tuple-element.33.tok_ref, f32[64,128]{1,0:T(8,128)S(1)} %copy-done.1, bf16[192,768]{1,0:T(8,128)(2,1)S(1)} %bitcast.13, ...), custom_call_target="tpu_custom_call", output_to_operand_aliasing={{0}: (6, {}), {1}: (7, {})} | custom-call | flops 2000000000 | bytes 4000000 | tf_op jit(solution)/shard_map/query_pass/pallas_call | solution.py:265
  22.1 0.0 collective-permute-done.4.rest_1_
  22.2 2.9 %collective-permute-start.5 = (bf16[192,256]{1,0:T(8,128)(2,1)S(1)}, bf16[192,256]{1,0:T(8,128)(2,1)S(1)}, u32[]{:S(2)}, u32[]{:S(2)}) collective-permute-start(bf16[192,256]{1,0:T(8,128)(2,1)S(1)} %add_convert_fusion), channel_id=1, source_target_pairs={{0,16},{4,20},{8,24},{12,28},{16,0},{20,4},{24,8},{28,12},{1,17},{... | collective-permute-start | bytes 294920 | tf_op jit(solution)/shard_map/ppermute | solution.py:516
  25.0 0.0 collective-permute-done.rest_1_.rest_4_
  25.0 0.0 collective-permute-done.1.rest_2_.rest_5_
  25.1 0.0 collective-permute-done.2.rest_3_.rest_6_
  25.1 4.2 %query_pass.5 = (bf16[4,768,768]{2,1,0:T(8,128)(2,1)S(1)}, f32[4,192,768]{2,1,0:T(8,128)S(1)}, bf16[4,192,192]{2,1,0:T(8,128)(2,1)S(1)}) custom-call(bf16[3072,768]{1,0:T(8,128)(2,1)S(1)} %get-tuple-element.33.tok_ref, f32[64,128]{1,0:T(8,128)S(1)} %copy-done.1, bf16[192,768]{1,0:T(8,128)(2,1)S(1)} %bitcast.14, ...), custom_call_target="tpu_custom_call", output_to_operand_aliasing={{0}: (10, {}), {1}: (11, {})} | custom-call | flops 2000000000 | bytes 4000000 | tf_op jit(solution)/shard_map/query_pass/pallas_call | solution.py:265
  29.2 0.0 collective-permute-done.5.rest_2_
  29.3 0.0 copy-start.3
  29.3 3.0 %norm_pass.1 = (bf16[192,768]{1,0:T(8,128)(2,1)}, bf16[192,768]{1,0:T(8,128)(2,1)}, bf16[192,768]{1,0:T(8,128)(2,1)}, bf16[192,768]{1,0:T(8,128)(2,1)}, bf16[768,384]{1,0:T(8,128)(2,1)}) custom-call(f32[4,192,768]{2,1,0:T(8,128)S(1)} %get-tuple-element.48.raw_ref, bf16[4,768,768]{2,1,0:T(8,128)(2,1)S(1)} %get-tuple-element.49.qft_ref, ...), custom_call_target="tpu_custom_call" | custom-call | flops 3000000000 | bytes 8000000 | tf_op jit(solution)/shard_map/norm_pass/pallas_call | solution.py:329
  32.3 5.5 %all-to-all-start = ((bf16[32,24,384]{2,1,0:T(8,128)(2,1)}), bf16[32,24,384]{2,1,0:T(8,128)(2,1)S(1)}, u32[]{:S(2)}, u32[]{:S(2)}) async-start(bf16[32,24,384]{2,1,0:T(8,128)(2,1)} %bitcast.22), calls=%async_computation | async-start | bytes 1179648 | tf_op jit(solution)/shard_map/all_to_all | solution.py:527
  37.8 0.3 collective-permute-start.6
  38.1 1.7 %collective-permute-start.7 = (bf16[192,768]{1,0:T(8,128)(2,1)}, bf16[192,768]{1,0:T(8,128)(2,1)S(1)}, u32[]{:S(2)}, u32[]{:S(2)}) collective-permute-start(bf16[192,768]{1,0:T(8,128)(2,1)} %get-tuple-element.55), channel_id=1, source_target_pairs={{0,2},{1,3},{2,0},{3,1},{4,6},{5,7},{6,4},{7,5},{8,10},{9,11},{10,... | collective-permute-start | bytes 884744 | tf_op jit(solution)/shard_map/ppermute | solution.py:506
  39.8 0.0 copy-done.3
  39.8 0.1 copy.19
  39.9 0.1 reshape.20.pick_ref
  40.0 0.0 collective-permute-done.6.rest_1_
  40.0 0.0 copy-start.5
  40.0 12.7 %collective-permute-done.7.rest_2_ = bf16[192,768]{1,0:T(8,128)(2,1)S(1)} collective-permute-done((bf16[192,768]{1,0:T(8,128)(2,1)}, bf16[192,768]{1,0:T(8,128)(2,1)S(1)}, u32[]{:S(2)}, u32[]{:S(2)}) %collective-permute-start.7) | collective-permute-done | bytes 294944 | tf_op jit(solution)/shard_map/ppermute | solution.py:506
  52.7 0.0 copy-start.6
  52.7 1.8 %all-to-all-done = bf16[32,24,384]{2,1,0:T(8,128)(2,1)S(1)} async-done(((bf16[32,24,384]{2,1,0:T(8,128)(2,1)}), bf16[32,24,384]{2,1,0:T(8,128)(2,1)S(1)}, u32[]{:S(2)}, u32[]{:S(2)}) %all-to-all-start) | async-done | bytes 589856 | tf_op jit(solution)/shard_map/all_to_all | solution.py:527
  54.5 0.0 copy-start.7
  54.5 6.4 %expert_pass.1 = bf16[256,768]{1,0:T(8,128)(2,1)} custom-call(bf16[8,4,24,384]{3,2,1,0:T(8,128)(2,1)S(1)} %bitcast.15, bf16[4,192,768]{2,1,0:T(8,128)(2,1)} %bitcast.19, bf16[1,768,3072]{2,1,0:T(8,128)(2,1)} %wi_hbm.1, bf16[1,3072,768]{2,1,0:T(8,128)(2,1)} %wd_hbm.1), custom_call_target="tpu_custom_call" | custom-call | flops 2000000000 | bytes 12000000 | tf_op jit(solution)/shard_map/expert_pass/pallas_call | solution.py:385
  60.9 0.0 copy-done.5
  60.9 0.0 copy-done.6
  60.9 3.4 %all-to-all-start.1 = ((bf16[32,8,768]{2,1,0:T(8,128)(2,1)}), bf16[32,8,768]{2,1,0:T(8,128)(2,1)S(1)}, u32[]{:S(2)}, u32[]{:S(2)}) async-start(bf16[32,8,768]{2,1,0:T(8,128)(2,1)} %bitcast.8), calls=%async_computation.1 | async-start | bytes 786432 | tf_op jit(solution)/shard_map/all_to_all | solution.py:534
  64.4 0.0 copy-start.4
  64.4 0.0 copy-done.7
  64.4 1.6 %collective-permute-start.8 = (bf16[192,768]{1,0:T(8,128)(2,1)S(1)}, bf16[192,768]{1,0:T(8,128)(2,1)S(1)}, u32[]{:S(2)}, u32[]{:S(2)}) collective-permute-start(bf16[192,768]{1,0:T(8,128)(2,1)S(1)} %copy-done.7), channel_id=1, source_target_pairs={{0,3},{1,2},{2,1},{3,0},{4,7},{5,6},{6,5},{7,4},{8,11},{9,10},{10,... | collective-permute-start | bytes 884744 | tf_op jit(solution)/shard_map/ppermute | solution.py:506
  66.0 5.2 %mix_pass.1.mix_hbm = f32[768,768]{1,0:T(8,128)} custom-call(bf16[3072,768]{1,0:T(8,128)(2,1)} %tok_hbm.3, bf16[4,192,768]{2,1,0:T(8,128)(2,1)} %bitcast.20, bf16[192,768]{1,0:T(8,128)(2,1)} %get-tuple-element.52.rest_0_, bf16[192,768]{1,0:T(8,128)(2,1)} %copy-done.5, bf16[192,768]{1,0:T(8,128)(2,1)} %copy-done.6), custom_call_target="tpu_custom_call" | custom-call | flops 2000000000 | bytes 6000000 | tf_op jit(solution)/shard_map/mix_pass/pallas_call | solution.py:425
  71.2 6.1 %collective-permute-done.8.attn_hbm = bf16[192,768]{1,0:T(8,128)(2,1)S(1)} collective-permute-done((bf16[192,768]{1,0:T(8,128)(2,1)S(1)}, bf16[192,768]{1,0:T(8,128)(2,1)S(1)}, u32[]{:S(2)}, u32[]{:S(2)}) %collective-permute-start.8) | collective-permute-done | bytes 294944 | tf_op jit(solution)/shard_map/ppermute | solution.py:506
  77.3 0.3 all-to-all-done.1
  77.6 0.0 copy-done.4
  77.6 4.4 %combine_pass.1 = bf16[768,768]{1,0:T(8,128)(2,1)} custom-call(f32[768,768]{1,0:T(8,128)} %mix_pass.1.mix_hbm, bf16[4,192,768]{2,1,0:T(8,128)(2,1)} %bitcast.21, bf16[192,768]{1,0:T(8,128)(2,1)S(1)} %collective-permute-done.8.attn_hbm, bf16[32,768]{1,0:T(8,128)(2,1)S(1)} %bitcast.18, s32[1,256]{1,0:T(1,128)S(1)} %reshape.20.pick_ref, ...), custom_call_target="tpu_custom_call" | custom-call | flops 2000000000 | bytes 6000000 | tf_op jit(solution)/shard_map/combine_pass/pallas_call | solution.py:477
  (3 shorter events, 0.1 us)
Async XLA Ops:
  0.0 0.7 copy-start.2
  0.7 13.4 %copy-start = (bf16[768,192]{0,1:T(8,128)(2,1)S(1)}, bf16[768,192]{0,1:T(8,128)(2,1)}, u32[]{:S(2)}) copy-start(bf16[768,192]{0,1:T(8,128)(2,1)} %param.11) | copy-start | bytes 884740
  0.7 13.4 %copy-start.1 = (f32[64,128]{1,0:T(8,128)S(1)}, f32[64,128]{1,0:T(8,128)}, u32[]{:S(2)}) copy-start(f32[64,128]{1,0:T(8,128)} %freq_ref.5) | copy-start | bytes 98308
  9.2 15.8 %collective-permute-start = (s32[1,192]{1,0:T(1,128)S(1)}, s32[1,192]{1,0:T(1,128)S(1)}, u32[]{:S(2)}, u32[]{:S(2)}) collective-permute-start(s32[1,192]{1,0:T(1,128)S(1)} %get-tuple-element.37.rest_0_.rest_3_), channel_id=1, source_target_pairs={{0,1},{1,0},{2,3},{3,2},{4,5},{5,4},{6,7},{7,6},{8,9},{9,8},{10,11... | collective-permute-start | bytes 2312 | tf_op jit(solution)/shard_map/ppermute | solution.py:506
  9.7 15.3 %collective-permute-start.1 = (s32[1,192]{1,0:T(1,128)S(1)}, s32[1,192]{1,0:T(1,128)S(1)}, u32[]{:S(2)}, u32[]{:S(2)}) collective-permute-start(s32[1,192]{1,0:T(1,128)S(1)} %get-tuple-element.37.rest_0_.rest_3_), channel_id=1, source_target_pairs={{0,2},{1,3},{2,0},{3,1},{4,6},{5,7},{6,4},{7,5},{8,10},{9,11},{10,... | collective-permute-start | bytes 2312 | tf_op jit(solution)/shard_map/ppermute | solution.py:506
  12.3 12.8 %collective-permute-start.2 = (s32[1,192]{1,0:T(1,128)S(1)}, s32[1,192]{1,0:T(1,128)S(1)}, u32[]{:S(2)}, u32[]{:S(2)}) collective-permute-start(s32[1,192]{1,0:T(1,128)S(1)} %get-tuple-element.37.rest_0_.rest_3_), channel_id=1, source_target_pairs={{0,3},{1,2},{2,1},{3,0},{4,7},{5,6},{6,5},{7,4},{8,11},{9,10},{10,... | collective-permute-start | bytes 2312 | tf_op jit(solution)/shard_map/ppermute | solution.py:506
  12.4 5.0 %collective-permute-start.3 = (bf16[192,256]{1,0:T(8,128)(2,1)S(1)}, bf16[192,256]{1,0:T(8,128)(2,1)S(1)}, u32[]{:S(2)}, u32[]{:S(2)}) collective-permute-start(bf16[192,256]{1,0:T(8,128)(2,1)S(1)} %get-tuple-element.38), channel_id=1, source_target_pairs={{0,4},{4,0},{8,12},{12,8},{16,20},{20,16},{24,28},{28,24},{1,5},{5... | collective-permute-start | bytes 294920 | tf_op jit(solution)/shard_map/ppermute | solution.py:516
  17.5 4.7 %collective-permute-start.4 = (bf16[192,256]{1,0:T(8,128)(2,1)S(1)}, bf16[192,256]{1,0:T(8,128)(2,1)S(1)}, u32[]{:S(2)}, u32[]{:S(2)}) collective-permute-start(bf16[192,256]{1,0:T(8,128)(2,1)S(1)} %add_convert_fusion.1), channel_id=1, source_target_pairs={{0,8},{4,12},{8,0},{12,4},{16,24},{20,28},{24,16},{28,20},{1,9},{5... | collective-permute-start | bytes 294920 | tf_op jit(solution)/shard_map/ppermute | solution.py:516
  22.2 7.1 %collective-permute-start.5 = (bf16[192,256]{1,0:T(8,128)(2,1)S(1)}, bf16[192,256]{1,0:T(8,128)(2,1)S(1)}, u32[]{:S(2)}, u32[]{:S(2)}) collective-permute-start(bf16[192,256]{1,0:T(8,128)(2,1)S(1)} %add_convert_fusion), channel_id=1, source_target_pairs={{0,16},{4,20},{8,24},{12,28},{16,0},{20,4},{24,8},{28,12},{1,17},{... | collective-permute-start | bytes 294920 | tf_op jit(solution)/shard_map/ppermute | solution.py:516
  29.3 10.5 %copy-start.3 = (s32[32,1,6]{0,1,2:T(1,128)S(1)}, s32[32,1,6]{0,1,2:T(1,128)}, u32[]{:S(2)}) copy-start(s32[32,1,6]{0,1,2:T(1,128)} %param.19) | copy-start | bytes 2308
  32.3 22.2 %all-to-all-start = ((bf16[32,24,384]{2,1,0:T(8,128)(2,1)}), bf16[32,24,384]{2,1,0:T(8,128)(2,1)S(1)}, u32[]{:S(2)}, u32[]{:S(2)}) async-start(bf16[32,24,384]{2,1,0:T(8,128)(2,1)} %bitcast.22), calls=%async_computation | async-start | bytes 1179648 | tf_op jit(solution)/shard_map/all_to_all | solution.py:527
  37.8 2.2 %collective-permute-start.6 = (bf16[192,768]{1,0:T(8,128)(2,1)}, bf16[192,768]{1,0:T(8,128)(2,1)S(1)}, u32[]{:S(2)}, u32[]{:S(2)}) collective-permute-start(bf16[192,768]{1,0:T(8,128)(2,1)} %get-tuple-element.54), channel_id=1, source_target_pairs={{0,1},{1,0},{2,3},{3,2},{4,5},{5,4},{6,7},{7,6},{8,9},{9,8},{10,11... | collective-permute-start | bytes 884744 | tf_op jit(solution)/shard_map/ppermute | solution.py:506
  38.1 14.6 %collective-permute-start.7 = (bf16[192,768]{1,0:T(8,128)(2,1)}, bf16[192,768]{1,0:T(8,128)(2,1)S(1)}, u32[]{:S(2)}, u32[]{:S(2)}) collective-permute-start(bf16[192,768]{1,0:T(8,128)(2,1)} %get-tuple-element.55), channel_id=1, source_target_pairs={{0,2},{1,3},{2,0},{3,1},{4,6},{5,7},{6,4},{7,5},{8,10},{9,11},{10,... | collective-permute-start | bytes 884744 | tf_op jit(solution)/shard_map/ppermute | solution.py:506
  40.0 20.9 %copy-start.5 = (bf16[192,768]{1,0:T(8,128)(2,1)}, bf16[192,768]{1,0:T(8,128)(2,1)S(1)}, u32[]{:S(2)}) copy-start(bf16[192,768]{1,0:T(8,128)(2,1)S(1)} %collective-permute-done.6.rest_1_) | copy-start | bytes 884740
  52.7 8.2 %copy-start.6 = (bf16[192,768]{1,0:T(8,128)(2,1)}, bf16[192,768]{1,0:T(8,128)(2,1)S(1)}, u32[]{:S(2)}) copy-start(bf16[192,768]{1,0:T(8,128)(2,1)S(1)} %collective-permute-done.7.rest_2_) | copy-start | bytes 884740
  54.5 9.9 %copy-start.7 = (bf16[192,768]{1,0:T(8,128)(2,1)S(1)}, bf16[192,768]{1,0:T(8,128)(2,1)}, u32[]{:S(2)}) copy-start(bf16[192,768]{1,0:T(8,128)(2,1)} %get-tuple-element.58) | copy-start | bytes 884740
  60.9 16.6 %all-to-all-start.1 = ((bf16[32,8,768]{2,1,0:T(8,128)(2,1)}), bf16[32,8,768]{2,1,0:T(8,128)(2,1)S(1)}, u32[]{:S(2)}, u32[]{:S(2)}) async-start(bf16[32,8,768]{2,1,0:T(8,128)(2,1)} %bitcast.8), calls=%async_computation.1 | async-start | bytes 786432 | tf_op jit(solution)/shard_map/all_to_all | solution.py:534
  64.4 13.2 %copy-start.4 = (bf16[768,32]{0,1:T(8,128)(2,1)S(1)}, bf16[768,32]{0,1:T(8,128)(2,1)}, u32[]{:S(2)}) copy-start(bf16[768,32]{0,1:T(8,128)(2,1)} %param.16) | copy-start | bytes 147460
  64.4 12.9 %collective-permute-start.8 = (bf16[192,768]{1,0:T(8,128)(2,1)S(1)}, bf16[192,768]{1,0:T(8,128)(2,1)S(1)}, u32[]{:S(2)}, u32[]{:S(2)}) collective-permute-start(bf16[192,768]{1,0:T(8,128)(2,1)S(1)} %copy-done.7), channel_id=1, source_target_pairs={{0,3},{1,2},{2,1},{3,0},{4,7},{5,6},{6,5},{7,4},{8,11},{9,10},{10,... | collective-permute-start | bytes 884744 | tf_op jit(solution)/shard_map/ppermute | solution.py:506

commit v5 on v4

--- a/solution.py
+++ b/solution.py
@@ -74,8 +74,8 @@
 FAR = pl.BlockSpec(memory_space=pltpu.HBM)
 
 
-def key_kernel(size, tok_hbm, wkt_hbm, wvt_hbm, freq_hbm, pick_ref, *rest):
-    tok_ref, kf_ref, vt_ref, sc_ref, tot_ref, own_ref, w_ref, freq_ref, sems = rest
+def key_kernel(size, tok_hbm, wkt_hbm, wvt_hbm, freq_hbm, pick_hbm, *rest):
+    tok_ref, kf_ref, vt_ref, sc_ref, tot_ref, own_ref, w_ref, freq_ref, pick_ref, sems = rest
     total = tok_ref.shape[0]
     wid = wkt_hbm.shape[0]
     heads = wid // HD
@@ -87,9 +87,10 @@
         for i, w in enumerate((wkt_hbm, wvt_hbm))
     ]
     weights.append(pltpu.make_async_copy(freq_hbm, freq_ref, sems.at[2]))
+    weights.append(pltpu.make_async_copy(pick_hbm, pick_ref, sems.at[3]))
     loads = [
         pltpu.make_async_copy(
-            tok_hbm.at[pl.ds(i * size, size)], tok_ref.at[pl.ds(i * size, size)], sems.at[3 + i]
+            tok_hbm.at[pl.ds(i * size, size)], tok_ref.at[pl.ds(i * size, size)], sems.at[4 + i]
         )
         for i in range(count)
     ]
@@ -150,7 +151,7 @@
     heads = wid // HD
     return pl.pallas_call(
         functools.partial(key_kernel, size),
-        in_specs=[FAR] * 4 + [HERE],
+        in_specs=[FAR] * 5,
         out_specs=[HERE] * 6,
         out_shape=[
             jax.ShapeDtypeStruct(tokens.shape, BF),
@@ -163,12 +164,13 @@
         scratch_shapes=[
             pltpu.VMEM((2 * wid, d), BF),
             pltpu.VMEM(freq.shape, F32),
-            pltpu.SemaphoreType.DMA((3 + total // size,)),
+            pltpu.VMEM(picks.shape, jnp.int32),
+            pltpu.SemaphoreType.DMA((4 + total // size,)),
         ],
         compiler_params=params(KEPT),
         cost_estimate=cost(5e9, 12e6),
         name="key_pass",
-    )(*map(far, (tokens, wkt, wvt, freq)), picks)
+    )(*map(far, (tokens, wkt, wvt, freq, picks)))
 
 
 def chosen(slot, pick_refs):
@@ -276,8 +278,8 @@
 
 def norm_kernel(slots, cap, rounds, raw_ref, qft_ref, seen_ref, *rest):
     got_refs, pick_refs = rest[:rounds], rest[rounds : rounds + slots]
-    outs = rest[rounds + slots : rounds + 2 * slots]
-    sent_hbm, ready, acc, sent, sems = rest[rounds + 2 * slots :]
+    outs = rest[rounds + slots : rounds + slots + 3]
+    sent_hbm, ready, acc, sent, sems = rest[rounds + slots + 3 :]
     me, at = lax.axis_index("head"), lax.axis_index("seq")
     wid = raw_ref.shape[1]
     heads = wid // HD
@@ -286,7 +288,8 @@
     for i, got in enumerate(got_refs):
         before = before + jnp.where((at & (1 << i)) > 0, got[...].astype(F32), 0.0)
     before = before.astype(BF)
-    copies = [pltpu.make_async_copy(ready.at[k], outs[k], sems.at[k]) for k in range(slots)]
+    goals = [outs[0], outs[1].at[pl.ds(0, wid)], outs[2], outs[1].at[pl.ds(wid, wid)]]
+    copies = [pltpu.make_async_copy(ready.at[k], goals[k], sems.at[k]) for k in range(slots)]
     picked = {}
 
     def norm(k):
@@ -329,8 +332,8 @@
     return pl.pallas_call(
         functools.partial(norm_kernel, slots, cap, len(got)),
         in_specs=[HERE] * (3 + len(got) + slots),
-        out_specs=[FAR] * (slots + 1),
-        out_shape=[pltpu.HBM((wid, rows), BF)] * slots + [pltpu.HBM((n, 2 * wid), BF)],
+        out_specs=[FAR] * 4,
+        out_shape=[pltpu.HBM(x, BF) for x in ((wid, rows), (2 * wid, rows), (wid, rows), (n, 2 * wid))],
         scratch_shapes=[
             pltpu.VMEM((slots, wid, rows), BF),
             pltpu.VMEM((n, 2 * wid), F32),
@@ -343,47 +346,53 @@
     )(raw, qft, seen, *got, *picks)
 
 
-def expert_kernel(cap, tiles, got_hbm, wo_hbm, wi_hbm, wd_hbm, out_ref, got, wo, wi, wd, taken, acc, sems):
+def expert_kernel(cap, ups, downs, got_hbm, wo_hbm, wi_hbm, wd_hbm, out_ref, got, wo, wi, wd, taken, acc, sems):
     slots, ring, each, both = got.shape
     wid = both // 2
     n, d = ring * each, wo.shape[2]
     ff = wi.shape[1]
-    tile = ff // tiles
     landing = [pltpu.make_async_copy(got_hbm.at[:, h], got.at[h], sems.at[h]) for h in range(slots)]
-    copies = [pltpu.make_async_copy(wo_hbm, wo, sems.at[slots])]
-    first = slots + 1
-    for t in range(tiles):
-        cut = pl.ds(t * tile, tile)
-        copies.append(pltpu.make_async_copy(wi_hbm.at[0, :, cut], wi.at[:, cut], sems.at[first + 2 * t]))
-        copies.append(pltpu.make_async_copy(wd_hbm.at[0, cut, :], wd.at[cut, :], sems.at[first + 1 + 2 * t]))
-    for c in landing + copies:
+    landing.append(pltpu.make_async_copy(wo_hbm, wo, sems.at[slots]))
+    up = ff // ups
+    rise = []
+    for t in range(ups):
+        cut = pl.ds(t * up, up)
+        rise.append(pltpu.make_async_copy(wi_hbm.at[0, :, cut], wi.at[:, cut], sems.at[slots + 1 + t]))
+    down = ff // downs
+    fall = []
+    for t in range(downs):
+        cut = pl.ds(t * down, down)
+        fall.append(pltpu.make_async_copy(wd_hbm.at[0, cut, :], wd.at[cut, :], sems.at[slots + 1 + ups + t]))
+    for c in landing + rise + fall:
         c.start()
     for c in landing:
         c.wait()
     parts_in = [got[h].reshape(n, both) for h in range(slots)]
     mixed = jnp.concatenate([g.astype(F32)[:, wid:] for g in parts_in], axis=1)
-    copies[0].wait()
     for h, g in enumerate(parts_in):
         mixed = mixed + nn(g[:, :wid], wo[h])
     taken[...] = mixed.astype(BF)
-    acc[...] = jnp.zeros((n, d), F32)
-    for t in range(tiles):
-        cut = slice(t * tile, (t + 1) * tile)
-        copies[1 + 2 * t].wait()
-        inner = jax.nn.gelu(nn(taken[...], wi[:, cut]), approximate=True).astype(BF)
-        copies[2 + 2 * t].wait()
-        acc[...] += nn(inner, wd[cut, :])
+    inner = []
+    for t in range(ups):
+        rise[t].wait()
+        part = nn(taken[...], wi[:, t * up : (t + 1) * up])
+        inner.append(jax.nn.gelu(part, approximate=True).astype(BF))
+    inner = jnp.concatenate(inner, axis=1)
+    for t in range(downs):
+        fall[t].wait()
+        part = nn(inner[:, t * down : (t + 1) * down], wd[t * down : (t + 1) * down, :])
+        acc[...] = part if t == 0 else acc[...] + part
     m = out_ref.shape[0]
     at = lax.broadcasted_iota(jnp.int32, (1, n), 1)
     out_ref[...] = nn(marks(at // cap * PAD + at % cap, m), acc[...].astype(BF)).astype(BF)
 
 
-def expert_pass(arrived, w_out, w_in, w_down, cap, tiles=3):
+def expert_pass(arrived, w_out, w_in, w_down, cap, ups=3, downs=3):
     ring, slots, each, both = arrived.shape
     d, ff = w_in.shape[1:]
     m = ring * each // cap * PAD
     return pl.pallas_call(
-        functools.partial(expert_kernel, cap, tiles),
+        functools.partial(expert_kernel, cap, ups, downs),
         in_specs=[AWAY] + [FAR] * 3,
         out_specs=HERE,
         out_shape=jax.ShapeDtypeStruct((m, d), BF),
@@ -394,7 +403,7 @@
             pltpu.VMEM((ff, d), BF),
             pltpu.VMEM((ring * each, d), BF),
             pltpu.VMEM((ring * each, d), F32),
-            pltpu.SemaphoreType.DMA((slots + 1 + 2 * tiles,)),
+            pltpu.SemaphoreType.DMA((slots + 1 + ups + downs,)),
         ],
         compiler_params=params(40),
         cost_estimate=cost(2e9, 12e6),
@@ -402,96 +411,99 @@
     )(arrived, *map(far, (w_out, w_in, w_down)))
 
 
-def mix_kernel(slots, tok_hbm, wo_hbm, *rest):
-    attns, (out_ref, tok, wo, sems) = rest[:-4], rest[-4:]
+def hidden_kernel(tok_hbm, wo_hbm, own_hbm, near_hbm, far_hbm, router_ref, pick_ref, *rest):
+    hid_ref, comb_ref, tok, wo, attn, sems = rest
     me = lax.axis_index("head")
     rows = tok.shape[0]
+    group, wid = wo_hbm.shape[:2]
     first = pl.multiple_of(me * rows, rows)
+    pieces = [own_hbm, near_hbm.at[pl.ds(0, wid)], far_hbm.at[pl.ds(0, wid)], far_hbm.at[pl.ds(wid, wid)]]
     copies = [pltpu.make_async_copy(tok_hbm.at[pl.ds(first, rows)], tok, sems.at[0])]
-    copies += [pltpu.make_async_copy(wo_hbm.at[me ^ k], wo.at[k], sems.at[1 + k]) for k in range(slots)]
+    for k in range(group):
+        line = pl.ds(k * wid, wid)
+        copies.append(pltpu.make_async_copy(wo_hbm.at[me ^ k], wo.at[line], sems.at[1 + k]))
+        copies.append(pltpu.make_async_copy(pieces[k], attn.at[line], sems.at[1 + group + k]))
     for copy in copies:
         copy.start()
     for copy in copies:
         copy.wait()
-    mixed = tok[...].astype(F32)
-    for k in range(slots):
-        mixed = mixed + tn(attns[k][...], wo[k])
-    out_ref[...] = mixed
-
-
-def mix_pass(tokens, w_out, attns, rows):
+    experts, n = router_ref.shape[0], pick_ref.shape[1]
+    spreads = marks(lax.broadcasted_iota(jnp.int32, (1, n), 1) // PAD, experts)
+    hidden = (tok[...].astype(F32) + tn(attn[...], wo[...])).astype(BF)
+    hid_ref[...] = hidden
+    gate = jax.nn.sigmoid(nt(hidden, router_ref[...])).astype(BF)
+    at = lax.broadcasted_iota(jnp.int32, (rows, n), 0)
+    comb_ref[...] = jnp.where(pick_ref[...] == at, nn(gate, spreads), 0.0).astype(BF)
+
+
+def hidden_pass(tokens, w_out, own, near, across, router_t, pick_row):
     d = tokens.shape[1]
-    slots = len(attns)
+    group, wid = w_out.shape[:2]
+    rows = tokens.shape[0] // group
+    n = pick_row.shape[1]
     return pl.pallas_call(
-        functools.partial(mix_kernel, slots),
-        in_specs=[FAR] * 2 + [HERE] * slots,
-        out_specs=HERE,
-        out_shape=jax.ShapeDtypeStruct((rows, d), F32),
+        hidden_kernel,
+        in_specs=[FAR] * 2 + [AWAY] * 3 + [HERE] * 2,
+        out_specs=[HERE] * 2,
+        out_shape=[jax.ShapeDtypeStruct((rows, d), BF), jax.ShapeDtypeStruct((rows, n), BF)],
         scratch_shapes=[
             pltpu.VMEM((rows, d), BF),
-            pltpu.VMEM((slots,) + w_out.shape[1:], BF),
-            pltpu.SemaphoreType.DMA((1 + slots,)),
+            pltpu.VMEM((group * wid, d), BF),
+            pltpu.VMEM((group * wid, rows), BF),
+            pltpu.SemaphoreType.DMA((1 + 2 * group,)),
         ],
         compiler_params=params(),
         cost_estimate=cost(2e9, 6e6),
-        name="mix_pass",
-    )(far(tokens), far(w_out), *attns)
-
-
-def combine_kernel(last, tiles, mix_hbm, wo_hbm, attn_hbm, router_ref, pick_ref, back_hbm, out_hbm, *scratch):
-    mix, wo, attn, back, out, in_sems, out_sems = scratch
-    me = lax.axis_index("head")
-    rows = mix.shape[0]
+        name="hidden_pass",
+    )(far(tokens), far(w_out), own, near, across, router_t, pick_row)
+
+
+def combine_kernel(tiles, hid_hbm, comb_hbm, back_hbm, out_hbm, hid, comb, back, out, in_sems, out_sems):
+    rows = hid.shape[0]
     tile = rows // tiles
     cuts = [pl.ds(t * tile, tile) for t in range(tiles)]
-    need = [
-        pltpu.make_async_copy(wo_hbm.at[me ^ last], wo, in_sems.at[0]),
-        pltpu.make_async_copy(attn_hbm, attn, in_sems.at[1]),
+    need = pltpu.make_async_copy(back_hbm, back, in_sems.at[0])
+    loads = [
+        [
+            pltpu.make_async_copy(comb_hbm.at[c], comb.at[c], in_sems.at[1 + 2 * t]),
+            pltpu.make_async_copy(hid_hbm.at[c], hid.at[c], in_sems.at[2 + 2 * t]),
+        ]
+        for t, c in enumerate(cuts)
     ]
-    later = pltpu.make_async_copy(back_hbm, back, in_sems.at[2])
-    loads = [pltpu.make_async_copy(mix_hbm.at[c], mix.at[c], in_sems.at[3 + t]) for t, c in enumerate(cuts)]
     stores = [pltpu.make_async_copy(out.at[c], out_hbm.at[c], out_sems.at[t]) for t, c in enumerate(cuts)]
-    for copy in [*need, loads[0], later, *loads[1:]]:
-        copy.start()
-    for copy in need:
-        copy.wait()
-    experts, n = router_ref.shape[0], pick_ref.shape[1]
-    spreads = marks(lax.broadcasted_iota(jnp.int32, (1, n), 1) // PAD, experts)
+    need.start()
+    for pair in loads:
+        for copy in pair:
+            copy.start()
+    need.wait()
     for t, cut in enumerate(cuts):
-        loads[t].wait()
-        hidden = (mix[cut, :] + tn(attn[:, t * tile : (t + 1) * tile], wo[...])).astype(BF)
-        gate = jax.nn.sigmoid(nt(hidden, router_ref[...])).astype(BF)
-        at = lax.broadcasted_iota(jnp.int32, (tile, n), 0) + t * tile
-        comb = jnp.where(pick_ref[...] == at, nn(gate, spreads), 0.0).astype(BF)
-        if t == 0:
-            later.wait()
-        out[cut, :] = (hidden.astype(F32) + nn(comb, back[...])).astype(BF)
+        for copy in loads[t]:
+            copy.wait()
+        out[cut, :] = (hid[cut, :].astype(F32) + nn(comb[cut, :], back[...])).astype(BF)
         stores[t].start()
     for store in stores:
         store.wait()
 
 
-def combine_pass(mixed, w_out, attn, router_t, pick_row, back, tiles=2):
-    rows, d = mixed.shape
-    last = w_out.shape[0] - 1
+def combine_pass(hidden, comb, back, tiles=2):
+    rows, d = hidden.shape
     return pl.pallas_call(
-        functools.partial(combine_kernel, last, tiles),
-        in_specs=[FAR, FAR, AWAY, HERE, HERE, AWAY],
+        functools.partial(combine_kernel, tiles),
+        in_specs=[FAR, FAR, AWAY],
         out_specs=AWAY,
         out_shape=jax.ShapeDtypeStruct((rows, d), BF),
         scratch_shapes=[
-            pltpu.VMEM((rows, d), F32),
-            pltpu.VMEM(w_out.shape[1:], BF),
-            pltpu.VMEM(attn.shape, BF),
+            pltpu.VMEM(hidden.shape, BF),
+            pltpu.VMEM(comb.shape, BF),
             pltpu.VMEM(back.shape, BF),
-            pltpu.VMEM((rows, d), BF),
-            pltpu.SemaphoreType.DMA((3 + tiles,)),
+            pltpu.VMEM(hidden.shape, BF),
+            pltpu.SemaphoreType.DMA((1 + 2 * tiles,)),
             pltpu.SemaphoreType.DMA((tiles,)),
         ],
         compiler_params=params(40),
-        cost_estimate=cost(2e9, 6e6),
+        cost_estimate=cost(1e9, 4e6),
         name="combine_pass",
-    )(far(mixed), far(w_out), attn, router_t, pick_row, back)
+    )(far(hidden), far(comb), back)
 
 
 def per_device(tokens, w_query, w_key, w_value, freq, w_out, router, w_in, w_down, picks):
@@ -521,12 +533,13 @@
         both = held.astype(F32) + got[-1].astype(F32)
         held, *made = lax.optimization_barrier([both.astype(BF), *made])
     qft, raw, seen = made
-    *attns, sent = norm_pass(raw, qft, seen, got, near, cap)
+    mine, near_out, across, sent = norm_pass(raw, qft, seen, got, near, cap)
 
     sent = sent.reshape(experts, group * cap, 2 * wid)
     arrived = lax.all_to_all(sent, ("seq", "head"), split_axis=0, concat_axis=0, tiled=True)
-    early = [swap(attns[k], k) for k in range(1, group - 1)]
-    arrived, pick_row, *early = lax.optimization_barrier([arrived, pick_row, *early])
+    near_got = swap(near_out, 1)
+    across = swap(jnp.concatenate([across, near_got[wid:]]), 2)
+    arrived, pick_row = lax.optimization_barrier((arrived, pick_row))
     w_out = w_out.reshape(group, wid, d)
     result = expert_pass(
         arrived.reshape(ring, group, group * cap, 2 * wid), w_out, w_in, w_down, cap
@@ -534,11 +547,8 @@
     back = lax.all_to_all(
         result.reshape(experts, PAD, d), ("seq", "head"), split_axis=0, concat_axis=0, tiled=True
     )
-    late = swap(attns[-1], group - 1)
-    mixed = mix_pass(tokens, w_out, [attns[0], *early], rows)
-    return combine_pass(
-        mixed, w_out, late, router.T, pick_row, back.reshape(experts * PAD, d)
-    )
+    hidden, comb = hidden_pass(tokens, w_out, mine, near_got, across, router.T, pick_row)
+    return combine_pass(hidden, comb, back.reshape(experts * PAD, d))
 
 
 def solution(mesh):

time: 82.5 us -> 80.1 us (0.971)
  starting transfers between devices: 22.2 us -> 20.6 us
  Pallas kernels: 37.2 us -> 35.9 us
  other arithmetic: 0.05 us -> 1.26 us
  waiting for transfers between devices: 21.4 us -> 20.2 us
    ppermute x6 -> x5, waiting for transfers between devices: 18.8 us -> 1.21 us  [per_device(): lax.ppermute(x, 'head', [(i, i ^ k) for i in range(group)])]
    all_to_all x1, waiting for transfers between devices: 1.84 us -> 11.4 us  [per_device(): lax.all_to_all(sent, ('seq', 'head'), split_axis=0, concat_axis=0, tiled=...]
    all_to_all x1, waiting for transfers between devices: 0.27 us -> 6.99 us  [per_device(): lax.all_to_all(result.reshape(experts, PAD, d), ('seq', 'head'), split_ax...]
    ppermute x6 -> x5, starting transfers between devices: 6.74 us -> 5.3 us  [per_device(): lax.ppermute(x, 'head', [(i, i ^ k) for i in range(group)])]
    pallas_call x4, Pallas kernels: 24.5 us -> 23.1 us  [the longest x1 8.53 us: key_pass(): pl.pallas_call(functools.partial(key_kernel, size), in_specs=[FAR] * 5, o...]
    concatenate x0 -> x1, other arithmetic: none -> 1.21 us  [per_device(): across = swap(jnp.concatenate([across, near_got[wid:]]), 2)]
  transfers between devices with their start and end apart: 11 -> 10, of which waited for: 5 -> 4; matrix products, arithmetic and copies ran while one was open for 0% -> 3% of each run, Pallas kernels for 18% -> 27%
where the time goes in v5:
time: 80.1 us; the launch traced here: 79.8 us
  Pallas kernels  35.9 us (45%)
  starting transfers between devices  20.6 us (26%)
  waiting for transfers between devices  20.2 us (25%)
  local copies, waits for them, and re-layouts  1.61 us (2%)
  other arithmetic  1.26 us (2%)
    all_to_all x1, waiting for transfers between devices, per_device(): lax.all_to_all(sent, ('seq', 'head'), split_axis=0, concat_axis=0, tiled=...  11.4 us
    pallas_call x3, Pallas kernels, query_pass(): pl.pallas_call(functools.partial(query_kernel, chunks, slots, len(picks))...  9.74 us
    pallas_call x1, Pallas kernels, key_pass(): pl.pallas_call(functools.partial(key_kernel, size), in_specs=[FAR] * 5, o...  8.53 us
    all_to_all x1, waiting for transfers between devices, per_device(): lax.all_to_all(result.reshape(experts, PAD, d), ('seq', 'head'), split_ax...  6.99 us
    ppermute x3, starting transfers between devices, per_device(): lax.ppermute(held, 'seq', [(j, j ^ 1 << i) for j in range(ring)])  6.5 us
    pallas_call x1, Pallas kernels, expert_pass(): pl.pallas_call(functools.partial(expert_kernel, cap, ups, downs), in_spec...  6.27 us
    all_to_all x1, starting transfers between devices, per_device(): lax.all_to_all(sent, ('seq', 'head'), split_axis=0, concat_axis=0, tiled=...  5.48 us
    pallas_call x1, Pallas kernels, hidden_pass(): pl.pallas_call(hidden_kernel, in_specs=[FAR] * 2 + [AWAY] * 3 + [HERE] *...  5.35 us
  transfers between devices with their start and end apart: 10, of which 4 were waited for; matrix products, arithmetic and copies ran while one was open for 3% of the time, Pallas kernels for 27%

profile of v5, /device:TPU:0, one launch (start us, length us, event | category | flops | bytes accessed | tf_op | source)
XLA Modules:
  0.0 79.8 jit_solution(1901845491601898986)
XLA Ops:
  0.0 0.0 copy-start
  0.0 0.0 copy-start.1
  0.0 8.5 %key_pass.1 = (bf16[3072,768]{1,0:T(8,128)(2,1)S(1)}, bf16[3072,768]{1,0:T(8,128)(2,1)S(1)}, bf16[192,3072]{1,0:T(8,128)(2,1)S(1)}, bf16[12,192,256]{2,1,0:T(8,1...) custom-call(bf16[3072,768]{1,0:T(8,128)(2,1)} %tok_hbm.3, bf16[192,768]{1,0:T(8,128)(2,1)} %bitcast.23, ...), custom_call_target="tpu_custom_call" | custom-call | flops 5000000000 | bytes 12000000 | tf_op jit(solution)/shard_map/key_pass/pallas_call | solution.py:152
  8.5 0.5 collective-permute-start
  9.1 2.6 %collective-permute-start.1 = (s32[1,192]{1,0:T(1,128)S(1)}, s32[1,192]{1,0:T(1,128)S(1)}, u32[]{:S(2)}, u32[]{:S(2)}) collective-permute-start(s32[1,192]{1,0:T(1,128)S(1)} %get-tuple-element.36.rest_0_.rest_3_), channel_id=1, source_target_pairs={{0,2},{1,3},{2,0},{3,1},{4,6},{5,7},{6,4},{7,5},{8,10},{9,11},{10,... | collective-permute-start | bytes 2312 | tf_op jit(solution)/shard_map/ppermute | solution.py:518
  11.6 0.1 collective-permute-start.2
  11.7 1.8 %collective-permute-start.3 = (bf16[192,256]{1,0:T(8,128)(2,1)S(1)}, bf16[192,256]{1,0:T(8,128)(2,1)S(1)}, u32[]{:S(2)}, u32[]{:S(2)}) collective-permute-start(bf16[192,256]{1,0:T(8,128)(2,1)S(1)} %get-tuple-element.37), channel_id=1, source_target_pairs={{0,4},{4,0},{8,12},{12,8},{16,20},{20,16},{24,28},{28,24},{1,5},{5... | collective-permute-start | bytes 294920 | tf_op jit(solution)/shard_map/ppermute | solution.py:528
  13.5 0.0 copy-done
  13.5 0.0 copy-done.1
  13.5 2.8 %query_pass.3 = (bf16[4,768,768]{2,1,0:T(8,128)(2,1)S(1)}, f32[4,192,768]{2,1,0:T(8,128)S(1)}) custom-call(bf16[3072,768]{1,0:T(8,128)(2,1)S(1)} %get-tuple-element.32.tok_ref, f32[64,128]{1,0:T(8,128)S(1)} %copy-done.1, bf16[192,768]{1,0:T(8,128)(2,1)S(1)} %bitcast.12, bf16[3072,768]{1,0:T(8,128)(2,1)S(1)} %get-tuple-element.33.kf_ref, ...), custom_call_target="tpu_custom_call" | custom-call | flops 2000000000 | bytes 4000000 | tf_op jit(solution)/shard_map/query_pass/pallas_call | solution.py:267
  16.2 0.5 collective-permute-done.3.rest_0_
  16.8 1.9 %collective-permute-start.4 = (bf16[192,256]{1,0:T(8,128)(2,1)S(1)}, bf16[192,256]{1,0:T(8,128)(2,1)S(1)}, u32[]{:S(2)}, u32[]{:S(2)}) collective-permute-start(bf16[192,256]{1,0:T(8,128)(2,1)S(1)} %add_convert_fusion.1), channel_id=1, source_target_pairs={{0,8},{4,12},{8,0},{12,4},{16,24},{20,28},{24,16},{28,20},{1,9},{5... | collective-permute-start | bytes 294920 | tf_op jit(solution)/shard_map/ppermute | solution.py:528
  18.6 2.8 %query_pass.4 = (bf16[4,768,768]{2,1,0:T(8,128)(2,1)S(1)}, f32[4,192,768]{2,1,0:T(8,128)S(1)}) custom-call(bf16[3072,768]{1,0:T(8,128)(2,1)S(1)} %get-tuple-element.32.tok_ref, f32[64,128]{1,0:T(8,128)S(1)} %copy-done.1, bf16[192,768]{1,0:T(8,128)(2,1)S(1)} %bitcast.13, ...), custom_call_target="tpu_custom_call", output_to_operand_aliasing={{0}: (6, {}), {1}: (7, {})} | custom-call | flops 2000000000 | bytes 4000000 | tf_op jit(solution)/shard_map/query_pass/pallas_call | solution.py:267
  21.4 0.0 collective-permute-done.4.rest_1_
  21.5 2.9 %collective-permute-start.5 = (bf16[192,256]{1,0:T(8,128)(2,1)S(1)}, bf16[192,256]{1,0:T(8,128)(2,1)S(1)}, u32[]{:S(2)}, u32[]{:S(2)}) collective-permute-start(bf16[192,256]{1,0:T(8,128)(2,1)S(1)} %add_convert_fusion), channel_id=1, source_target_pairs={{0,16},{4,20},{8,24},{12,28},{16,0},{20,4},{24,8},{28,12},{1,17},{... | collective-permute-start | bytes 294920 | tf_op jit(solution)/shard_map/ppermute | solution.py:528
  24.4 0.0 collective-permute-done.rest_1_.rest_4_
  24.4 0.0 collective-permute-done.1.rest_2_.rest_5_
  24.4 0.0 collective-permute-done.2.rest_3_.rest_6_
  24.4 4.2 %query_pass.5 = (bf16[4,768,768]{2,1,0:T(8,128)(2,1)S(1)}, f32[4,192,768]{2,1,0:T(8,128)S(1)}, bf16[4,192,192]{2,1,0:T(8,128)(2,1)S(1)}) custom-call(bf16[3072,768]{1,0:T(8,128)(2,1)S(1)} %get-tuple-element.32.tok_ref, f32[64,128]{1,0:T(8,128)S(1)} %copy-done.1, bf16[192,768]{1,0:T(8,128)(2,1)S(1)} %bitcast.14, ...), custom_call_target="tpu_custom_call", output_to_operand_aliasing={{0}: (10, {}), {1}: (11, {})} | custom-call | flops 2000000000 | bytes 4000000 | tf_op jit(solution)/shard_map/query_pass/pallas_call | solution.py:267
  28.6 0.0 collective-permute-done.5.rest_2_
  28.6 0.0 copy-start.4
  28.6 3.0 %norm_pass.1 = (bf16[192,768]{1,0:T(8,128)(2,1)}, bf16[384,768]{1,0:T(8,128)(2,1)}, bf16[192,768]{1,0:T(8,128)(2,1)}, bf16[768,384]{1,0:T(8,128)(2,1)}) custom-call(f32[4,192,768]{2,1,0:T(8,128)S(1)} %get-tuple-element.47.raw_ref, bf16[4,768,768]{2,1,0:T(8,128)(2,1)S(1)} %get-tuple-element.48.qft_ref, bf16[4,192,192]{2,1,0:T(8,128)(2,1)S(1)} %get-tuple-element.49.seen_ref, ...), custom_call_target="tpu_custom_call" | custom-call | flops 3000000000 | bytes 8000000 | tf_op jit(solution)/shard_map/norm_pass/pallas_call | solution.py:332
  31.6 5.5 %all-to-all-start = ((bf16[32,24,384]{2,1,0:T(8,128)(2,1)}), bf16[32,24,384]{2,1,0:T(8,128)(2,1)S(1)}, u32[]{:S(2)}, u32[]{:S(2)}) async-start(bf16[32,24,384]{2,1,0:T(8,128)(2,1)} %bitcast.19), calls=%async_computation | async-start | bytes 1179648 | tf_op jit(solution)/shard_map/all_to_all | solution.py:539
  37.1 0.3 collective-permute-start.6
  37.5 0.0 copy-done.4
  37.5 0.1 copy.19
  37.5 0.7 reshape.20.pick_ref
  38.2 1.2 %collective-permute-done.6.near_hbm = bf16[384,768]{1,0:T(8,128)(2,1)S(1)} collective-permute-done((bf16[384,768]{1,0:T(8,128)(2,1)}, bf16[384,768]{1,0:T(8,128)(2,1)S(1)}, u32[]{:S(2)}, u32[]{:S(2)}) %collective-permute-start.6) | collective-permute-done | bytes 589856 | tf_op jit(solution)/shard_map/ppermute | solution.py:518
  39.4 0.0 copy-start.2
  39.4 1.2 %pad_maximum_fusion = bf16[384,768]{1,0:T(8,128)(2,1)S(1)} fusion(bf16[192,768]{1,0:T(8,128)(2,1)S(1)} %slice.4, bf16[192,768]{1,0:T(8,128)(2,1)} %get-tuple-element.53), kind=kLoop, calls=%fused_computation | loop fusion | flops 1179648 | bytes 1179648 | tf_op jit(solution)/shard_map/concatenate | solution.py:541
  40.6 1.8 %collective-permute-start.7 = (bf16[384,768]{1,0:T(8,128)(2,1)S(1)}, bf16[384,768]{1,0:T(8,128)(2,1)S(1)}, u32[]{:S(2)}, u32[]{:S(2)}) collective-permute-start(bf16[384,768]{1,0:T(8,128)(2,1)S(1)} %pad_maximum_fusion), channel_id=1, source_target_pairs={{0,2},{1,3},{2,0},{3,1},{4,6},{5,7},{6,4},{7,5},{8,10},{9,11},{10,... | collective-permute-start | bytes 1769480 | tf_op jit(solution)/shard_map/ppermute | solution.py:518
  42.5 11.4 %all-to-all-done = bf16[32,24,384]{2,1,0:T(8,128)(2,1)S(1)} async-done(((bf16[32,24,384]{2,1,0:T(8,128)(2,1)}), bf16[32,24,384]{2,1,0:T(8,128)(2,1)S(1)}, u32[]{:S(2)}, u32[]{:S(2)}) %all-to-all-start) | async-done | bytes 589856 | tf_op jit(solution)/shard_map/all_to_all | solution.py:539
  53.9 6.3 %expert_pass.1 = bf16[256,768]{1,0:T(8,128)(2,1)} custom-call(bf16[8,4,24,384]{3,2,1,0:T(8,128)(2,1)S(1)} %bitcast.15, bf16[4,192,768]{2,1,0:T(8,128)(2,1)} %bitcast.17, bf16[1,768,3072]{2,1,0:T(8,128)(2,1)} %wi_hbm.1, bf16[1,3072,768]{2,1,0:T(8,128)(2,1)} %wd_hbm.1), custom_call_target="tpu_custom_call" | custom-call | flops 2000000000 | bytes 12000000 | tf_op jit(solution)/shard_map/expert_pass/pallas_call | solution.py:394
  60.2 0.0 copy-done.2
  60.2 3.3 %all-to-all-start.1 = ((bf16[32,8,768]{2,1,0:T(8,128)(2,1)}), bf16[32,8,768]{2,1,0:T(8,128)(2,1)S(1)}, u32[]{:S(2)}, u32[]{:S(2)}) async-start(bf16[32,8,768]{2,1,0:T(8,128)(2,1)} %bitcast.8), calls=%async_computation.1 | async-start | bytes 786432 | tf_op jit(solution)/shard_map/all_to_all | solution.py:547
  63.5 0.0 collective-permute-done.7.far_hbm
  63.5 0.0 copy-start.3
  63.5 0.8 %copy-done.3 = bf16[384,768]{1,0:T(8,128)(2,1)} copy-done((bf16[384,768]{1,0:T(8,128)(2,1)}, bf16[384,768]{1,0:T(8,128)(2,1)S(1)}, u32[]{:S(2)}) %copy-start.3) | copy-done | bytes 589848
  64.3 5.3 %hidden_pass.1 = (bf16[768,768]{1,0:T(8,128)(2,1)}, bf16[768,256]{1,0:T(8,128)(2,1)}) custom-call(bf16[3072,768]{1,0:T(8,128)(2,1)} %tok_hbm.3, bf16[4,192,768]{2,1,0:T(8,128)(2,1)} %bitcast.18, bf16[192,768]{1,0:T(8,128)(2,1)} %get-tuple-element.51.own_hbm, bf16[384,768]{1,0:T(8,128)(2,1)} %copy-done.2, bf16[384,768]{1,0:T(8,128)(2,1)} %copy-done.3, ...), custom_call_target="tpu_custom_call" | custom-call | flops 2000000000 | bytes 6000000 | tf_op jit(solution)/shard_map/hidden_pass/pallas_call | solution.py:444
  69.7 7.0 %all-to-all-done.1 = bf16[32,8,768]{2,1,0:T(8,128)(2,1)S(1)} async-done(((bf16[32,8,768]{2,1,0:T(8,128)(2,1)}), bf16[32,8,768]{2,1,0:T(8,128)(2,1)S(1)}, u32[]{:S(2)}, u32[]{:S(2)}) %all-to-all-start.1) | async-done | bytes 393248 | tf_op jit(solution)/shard_map/all_to_all | solution.py:547
  76.6 3.0 %combine_pass.1 = bf16[768,768]{1,0:T(8,128)(2,1)} custom-call(bf16[768,768]{1,0:T(8,128)(2,1)} %get-tuple-element.56.hid_hbm, bf16[768,256]{1,0:T(8,128)(2,1)} %get-tuple-element.57.comb_hbm, bf16[256,768]{1,0:T(8,128)(2,1)S(1)} %bitcast.16), custom_call_target="tpu_custom_call" | custom-call | flops 1000000000 | bytes 4000000 | tf_op jit(solution)/shard_map/combine_pass/pallas_call | solution.py:490
  (4 shorter events, 0.1 us)
Async XLA Ops:
  0.0 13.5 %copy-start = (bf16[768,192]{0,1:T(8,128)(2,1)S(1)}, bf16[768,192]{0,1:T(8,128)(2,1)}, u32[]{:S(2)}) copy-start(bf16[768,192]{0,1:T(8,128)(2,1)} %param.11) | copy-start | bytes 884740
  0.0 13.5 %copy-start.1 = (f32[64,128]{1,0:T(8,128)S(1)}, f32[64,128]{1,0:T(8,128)}, u32[]{:S(2)}) copy-start(f32[64,128]{1,0:T(8,128)} %freq_ref.5) | copy-start | bytes 98308
  8.5 15.8 %collective-permute-start = (s32[1,192]{1,0:T(1,128)S(1)}, s32[1,192]{1,0:T(1,128)S(1)}, u32[]{:S(2)}, u32[]{:S(2)}) collective-permute-start(s32[1,192]{1,0:T(1,128)S(1)} %get-tuple-element.36.rest_0_.rest_3_), channel_id=1, source_target_pairs={{0,1},{1,0},{2,3},{3,2},{4,5},{5,4},{6,7},{7,6},{8,9},{9,8},{10,11... | collective-permute-start | bytes 2312 | tf_op jit(solution)/shard_map/ppermute | solution.py:518
  9.1 15.3 %collective-permute-start.1 = (s32[1,192]{1,0:T(1,128)S(1)}, s32[1,192]{1,0:T(1,128)S(1)}, u32[]{:S(2)}, u32[]{:S(2)}) collective-permute-start(s32[1,192]{1,0:T(1,128)S(1)} %get-tuple-element.36.rest_0_.rest_3_), channel_id=1, source_target_pairs={{0,2},{1,3},{2,0},{3,1},{4,6},{5,7},{6,4},{7,5},{8,10},{9,11},{10,... | collective-permute-start | bytes 2312 | tf_op jit(solution)/shard_map/ppermute | solution.py:518
  11.6 12.8 %collective-permute-start.2 = (s32[1,192]{1,0:T(1,128)S(1)}, s32[1,192]{1,0:T(1,128)S(1)}, u32[]{:S(2)}, u32[]{:S(2)}) collective-permute-start(s32[1,192]{1,0:T(1,128)S(1)} %get-tuple-element.36.rest_0_.rest_3_), channel_id=1, source_target_pairs={{0,3},{1,2},{2,1},{3,0},{4,7},{5,6},{6,5},{7,4},{8,11},{9,10},{10,... | collective-permute-start | bytes 2312 | tf_op jit(solution)/shard_map/ppermute | solution.py:518
  11.7 5.1 %collective-permute-start.3 = (bf16[192,256]{1,0:T(8,128)(2,1)S(1)}, bf16[192,256]{1,0:T(8,128)(2,1)S(1)}, u32[]{:S(2)}, u32[]{:S(2)}) collective-permute-start(bf16[192,256]{1,0:T(8,128)(2,1)S(1)} %get-tuple-element.37), channel_id=1, source_target_pairs={{0,4},{4,0},{8,12},{12,8},{16,20},{20,16},{24,28},{28,24},{1,5},{5... | collective-permute-start | bytes 294920 | tf_op jit(solution)/shard_map/ppermute | solution.py:528
  16.8 4.7 %collective-permute-start.4 = (bf16[192,256]{1,0:T(8,128)(2,1)S(1)}, bf16[192,256]{1,0:T(8,128)(2,1)S(1)}, u32[]{:S(2)}, u32[]{:S(2)}) collective-permute-start(bf16[192,256]{1,0:T(8,128)(2,1)S(1)} %add_convert_fusion.1), channel_id=1, source_target_pairs={{0,8},{4,12},{8,0},{12,4},{16,24},{20,28},{24,16},{28,20},{1,9},{5... | collective-permute-start | bytes 294920 | tf_op jit(solution)/shard_map/ppermute | solution.py:528
  21.5 7.1 %collective-permute-start.5 = (bf16[192,256]{1,0:T(8,128)(2,1)S(1)}, bf16[192,256]{1,0:T(8,128)(2,1)S(1)}, u32[]{:S(2)}, u32[]{:S(2)}) collective-permute-start(bf16[192,256]{1,0:T(8,128)(2,1)S(1)} %add_convert_fusion), channel_id=1, source_target_pairs={{0,16},{4,20},{8,24},{12,28},{16,0},{20,4},{24,8},{28,12},{1,17},{... | collective-permute-start | bytes 294920 | tf_op jit(solution)/shard_map/ppermute | solution.py:528
  28.6 8.9 %copy-start.4 = (s32[32,1,6]{0,1,2:T(1,128)S(1)}, s32[32,1,6]{0,1,2:T(1,128)}, u32[]{:S(2)}) copy-start(s32[32,1,6]{0,1,2:T(1,128)} %param.19) | copy-start | bytes 2308
  31.6 22.2 %all-to-all-start = ((bf16[32,24,384]{2,1,0:T(8,128)(2,1)}), bf16[32,24,384]{2,1,0:T(8,128)(2,1)S(1)}, u32[]{:S(2)}, u32[]{:S(2)}) async-start(bf16[32,24,384]{2,1,0:T(8,128)(2,1)} %bitcast.19), calls=%async_computation | async-start | bytes 1179648 | tf_op jit(solution)/shard_map/all_to_all | solution.py:539
  37.1 2.3 %collective-permute-start.6 = (bf16[384,768]{1,0:T(8,128)(2,1)}, bf16[384,768]{1,0:T(8,128)(2,1)S(1)}, u32[]{:S(2)}, u32[]{:S(2)}) collective-permute-start(bf16[384,768]{1,0:T(8,128)(2,1)} %get-tuple-element.52), channel_id=1, source_target_pairs={{0,1},{1,0},{2,3},{3,2},{4,5},{5,4},{6,7},{7,6},{8,9},{9,8},{10,11... | collective-permute-start | bytes 1769480 | tf_op jit(solution)/shard_map/ppermute | solution.py:518
  39.4 20.7 %copy-start.2 = (bf16[384,768]{1,0:T(8,128)(2,1)}, bf16[384,768]{1,0:T(8,128)(2,1)S(1)}, u32[]{:S(2)}) copy-start(bf16[384,768]{1,0:T(8,128)(2,1)S(1)} %collective-permute-done.6.near_hbm) | copy-start | bytes 1769476
  40.6 22.8 %collective-permute-start.7 = (bf16[384,768]{1,0:T(8,128)(2,1)S(1)}, bf16[384,768]{1,0:T(8,128)(2,1)S(1)}, u32[]{:S(2)}, u32[]{:S(2)}) collective-permute-start(bf16[384,768]{1,0:T(8,128)(2,1)S(1)} %pad_maximum_fusion), channel_id=1, source_target_pairs={{0,2},{1,3},{2,0},{3,1},{4,6},{5,7},{6,4},{7,5},{8,10},{9,11},{10,... | collective-permute-start | bytes 1769480 | tf_op jit(solution)/shard_map/ppermute | solution.py:518
  60.2 16.5 %all-to-all-start.1 = ((bf16[32,8,768]{2,1,0:T(8,128)(2,1)}), bf16[32,8,768]{2,1,0:T(8,128)(2,1)S(1)}, u32[]{:S(2)}, u32[]{:S(2)}) async-start(bf16[32,8,768]{2,1,0:T(8,128)(2,1)} %bitcast.8), calls=%async_computation.1 | async-start | bytes 786432 | tf_op jit(solution)/shard_map/all_to_all | solution.py:547
  63.5 0.8 %copy-start.3 = (bf16[384,768]{1,0:T(8,128)(2,1)}, bf16[384,768]{1,0:T(8,128)(2,1)S(1)}, u32[]{:S(2)}) copy-start(bf16[384,768]{1,0:T(8,128)(2,1)S(1)} %collective-permute-done.7.far_hbm) | copy-start | bytes 1769476

commit v6 on v5

--- a/solution.py
+++ b/solution.py
@@ -216,7 +216,9 @@
         columns = window[:, :wid]
         for shift in range(math.gcd(wid, LANES), wide - wid + 1, math.gcd(wid, LANES)):
             columns = jnp.where(start % LANES == shift, window[:, shift : shift + wid], columns)
-        rest[-1][b] = tn(columns, marks(chosen(me ^ b, pick_refs), rows)).astype(BF)
+        line = chosen(me ^ b, pick_refs).T
+        at = lax.broadcasted_iota(jnp.int32, (line.shape[0], rows), 1)
+        rest[-1][b] = nn((at == line).astype(F32).astype(BF), columns).astype(BF).T
 
     def turn(u):
         mine, cols, _ = spot(u)
@@ -344,6 +346,15 @@
         cost_estimate=cost(3e9, 8e6),
         name="norm_pass",
     )(raw, qft, seen, *got, *picks)
+
+
+def packing(d, cap):
+    spare = PAD - cap
+    columns = d // LANES
+    tiles = -(-columns * cap // PAD)
+    left = [(c, first) for c in range(tiles, columns) for first in range(0, cap, spare)]
+    rest = [left[t : t + 1] for t in range(tiles)]
+    return tiles, rest
 
 
 def expert_kernel(cap, ups, downs, got_hbm, wo_hbm, wi_hbm, wd_hbm, out_ref, got, wo, wi, wd, taken, acc, sems):
@@ -382,20 +393,32 @@
         fall[t].wait()
         part = nn(inner[:, t * down : (t + 1) * down], wd[t * down : (t + 1) * down, :])
         acc[...] = part if t == 0 else acc[...] + part
-    m = out_ref.shape[0]
-    at = lax.broadcasted_iota(jnp.int32, (1, n), 1)
-    out_ref[...] = nn(marks(at // cap * PAD + at % cap, m), acc[...].astype(BF)).astype(BF)
+    ready = acc[...].astype(BF)
+    tiles, rest = packing(d, cap)
+    blocks = n // cap
+    line = lax.broadcasted_iota(jnp.int32, (blocks * PAD, n), 0)
+    entry = lax.broadcasted_iota(jnp.int32, (blocks * PAD, n), 1)
+    same = (line // PAD == entry // cap) & (line % PAD < cap)
+    plain = (same & (line % PAD == entry % cap)).astype(F32).astype(BF)
+    body = nn(plain, ready[:, : tiles * LANES])
+    for t in range(tiles):
+        tile = body[:, t * LANES : (t + 1) * LANES]
+        for column, first in rest[t]:
+            extra = (line // PAD == entry // cap) & (line % PAD >= cap) & (entry % cap == line % PAD - cap + first)
+            tile = tile + nn(extra.astype(F32).astype(BF), ready[:, column * LANES : (column + 1) * LANES])
+        out_ref[:, t * PAD : (t + 1) * PAD, :] = tile.reshape(blocks, PAD, LANES).astype(BF)
 
 
 def expert_pass(arrived, w_out, w_in, w_down, cap, ups=3, downs=3):
     ring, slots, each, both = arrived.shape
     d, ff = w_in.shape[1:]
-    m = ring * each // cap * PAD
+    blocks = ring * each // cap
+    tiles = packing(d, cap)[0]
     return pl.pallas_call(
         functools.partial(expert_kernel, cap, ups, downs),
         in_specs=[AWAY] + [FAR] * 3,
         out_specs=HERE,
-        out_shape=jax.ShapeDtypeStruct((m, d), BF),
+        out_shape=jax.ShapeDtypeStruct((blocks, tiles * PAD, LANES), BF),
         scratch_shapes=[
             pltpu.VMEM((slots, ring, each, both), BF),
             pltpu.VMEM(w_out.shape, BF),
@@ -433,19 +456,21 @@
     hid_ref[...] = hidden
     gate = jax.nn.sigmoid(nt(hidden, router_ref[...])).astype(BF)
     at = lax.broadcasted_iota(jnp.int32, (rows, n), 0)
-    comb_ref[...] = jnp.where(pick_ref[...] == at, nn(gate, spreads), 0.0).astype(BF)
+    weight = nn(gate, spreads)
+    for i in range(comb_ref.shape[0]):
+        comb_ref[i] = jnp.where(pick_ref[i : i + 1, :] == at, weight, 0.0).astype(BF)
 
 
 def hidden_pass(tokens, w_out, own, near, across, router_t, pick_row):
     d = tokens.shape[1]
     group, wid = w_out.shape[:2]
     rows = tokens.shape[0] // group
-    n = pick_row.shape[1]
+    kinds, n = pick_row.shape
     return pl.pallas_call(
         hidden_kernel,
         in_specs=[FAR] * 2 + [AWAY] * 3 + [HERE] * 2,
         out_specs=[HERE] * 2,
-        out_shape=[jax.ShapeDtypeStruct((rows, d), BF), jax.ShapeDtypeStruct((rows, n), BF)],
+        out_shape=[jax.ShapeDtypeStruct((rows, d), BF), jax.ShapeDtypeStruct((kinds, rows, n), BF)],
         scratch_shapes=[
             pltpu.VMEM((rows, d), BF),
             pltpu.VMEM((group * wid, d), BF),
@@ -458,14 +483,14 @@
     )(far(tokens), far(w_out), own, near, across, router_t, pick_row)
 
 
-def combine_kernel(tiles, hid_hbm, comb_hbm, back_hbm, out_hbm, hid, comb, back, out, in_sems, out_sems):
+def combine_kernel(tiles, cap, hid_hbm, comb_hbm, back_hbm, out_hbm, hid, comb, back, out, in_sems, out_sems):
     rows = hid.shape[0]
     tile = rows // tiles
     cuts = [pl.ds(t * tile, tile) for t in range(tiles)]
     need = pltpu.make_async_copy(back_hbm, back, in_sems.at[0])
     loads = [
         [
-            pltpu.make_async_copy(comb_hbm.at[c], comb.at[c], in_sems.at[1 + 2 * t]),
+            pltpu.make_async_copy(comb_hbm.at[:, c], comb.at[:, c], in_sems.at[1 + 2 * t]),
             pltpu.make_async_copy(hid_hbm.at[c], hid.at[c], in_sems.at[2 + 2 * t]),
         ]
         for t, c in enumerate(cuts)
@@ -475,20 +500,32 @@
     for pair in loads:
         for copy in pair:
             copy.start()
+    packs, rest = packing(hid.shape[1], cap)
+    left = {}
+    for j, held in enumerate(rest):
+        for column, first in held:
+            left.setdefault(column, []).append((j, first))
     need.wait()
+    got = [back[:, j * PAD : (j + 1) * PAD, :].reshape(comb.shape[2], LANES) for j in range(packs)]
     for t, cut in enumerate(cuts):
         for copy in loads[t]:
             copy.wait()
-        out[cut, :] = (hid[cut, :].astype(F32) + nn(comb[cut, :], back[...])).astype(BF)
+        for j in range(packs):
+            lanes = slice(j * LANES, (j + 1) * LANES)
+            out[cut, lanes] = (hid[cut, lanes].astype(F32) + nn(comb[0, cut, :], got[j])).astype(BF)
+        for column, places in left.items():
+            lanes = slice(column * LANES, (column + 1) * LANES)
+            moe = sum(nn(comb[1 + first // (PAD - cap), cut, :], got[j]) for j, first in places)
+            out[cut, lanes] = (hid[cut, lanes].astype(F32) + moe).astype(BF)
         stores[t].start()
     for store in stores:
         store.wait()
 
 
-def combine_pass(hidden, comb, back, tiles=2):
+def combine_pass(hidden, comb, back, cap, tiles=3):
     rows, d = hidden.shape
     return pl.pallas_call(
-        functools.partial(combine_kernel, tiles),
+        functools.partial(combine_kernel, tiles, cap),
         in_specs=[FAR, FAR, AWAY],
         out_specs=AWAY,
         out_shape=jax.ShapeDtypeStruct((rows, d), BF),
@@ -514,7 +551,12 @@
     experts, _, cap = picks.shape
     wid = w_query.shape[1]
 
-    pick_row = jnp.pad(picks[:, 0, :], ((0, 0), (0, PAD - cap)), constant_values=-1).reshape(1, experts * PAD)
+    spare = PAD - cap
+    own_picks = picks[:, 0, :]
+    kinds = [jnp.pad(own_picks, ((0, 0), (0, spare)), constant_values=-1)]
+    for first in range(0, cap, spare):
+        kinds.append(jnp.pad(own_picks[:, first : first + spare], ((0, 0), (cap, 0)), constant_values=-1))
+    pick_row = jnp.stack(kinds).reshape(len(kinds), experts * PAD)
     swap = lambda x, k: lax.ppermute(x, "head", [(i, i ^ k) for i in range(group)])
 
     tok_here, kf, vt, sc, held, own = key_pass(
@@ -544,11 +586,9 @@
     result = expert_pass(
         arrived.reshape(ring, group, group * cap, 2 * wid), w_out, w_in, w_down, cap
     )
-    back = lax.all_to_all(
-        result.reshape(experts, PAD, d), ("seq", "head"), split_axis=0, concat_axis=0, tiled=True
-    )
+    back = lax.all_to_all(result, ("seq", "head"), split_axis=0, concat_axis=0, tiled=True)
     hidden, comb = hidden_pass(tokens, w_out, mine, near_got, across, router.T, pick_row)
-    return combine_pass(hidden, comb, back.reshape(experts * PAD, d))
+    return combine_pass(hidden, comb, back, cap)
 
 
 def solution(mesh):

time: 80.1 us -> 79.6 us (level)
  waiting for transfers between devices: 20.2 us -> 18.3 us
    all_to_all x1, waiting for transfers between devices: 6.99 us -> 5.44 us  [per_device(): lax.all_to_all(result, ('seq', 'head'), split_axis=0, concat_axis=0, tile...]
    ppermute x5, waiting for transfers between devices: 1.21 us -> 0.39 us  [per_device(): lax.ppermute(x, 'head', [(i, i ^ k) for i in range(group)])]
  transfers between devices with their start and end apart: 10 -> 10, of which waited for: 4 -> 5; matrix products, arithmetic and copies ran while one was open for 3% -> 4% of each run, Pallas kernels for 27% -> 27%
where the time goes in v6:
time: 79.6 us; the launch traced here: 79.2 us
  Pallas kernels  36.3 us (46%)
  starting transfers between devices  20.7 us (26%)
  waiting for transfers between devices  18.3 us (23%)
  other arithmetic  1.87 us (2%)
  local copies, waits for them, and re-layouts  1.79 us (2%)
    all_to_all x1, waiting for transfers between devices, per_device(): lax.all_to_all(sent, ('seq', 'head'), split_axis=0, concat_axis=0, tiled=...  11.4 us
    pallas_call x3, Pallas kernels, query_pass(): pl.pallas_call(functools.partial(query_kernel, chunks, slots, len(picks))...  9.19 us
    pallas_call x1, Pallas kernels, key_pass(): pl.pallas_call(functools.partial(key_kernel, size), in_specs=[FAR] * 5, o...  8.53 us
    ppermute x3, starting transfers between devices, per_device(): lax.ppermute(held, 'seq', [(j, j ^ 1 << i) for j in range(ring)])  6.53 us
    pallas_call x1, Pallas kernels, expert_pass(): pl.pallas_call(functools.partial(expert_kernel, cap, ups, downs), in_spec...  6.44 us
    pallas_call x1, Pallas kernels, hidden_pass(): pl.pallas_call(hidden_kernel, in_specs=[FAR] * 2 + [AWAY] * 3 + [HERE] *...  5.72 us
    all_to_all x1, starting transfers between devices, per_device(): lax.all_to_all(sent, ('seq', 'head'), split_axis=0, concat_axis=0, tiled=...  5.58 us
    all_to_all x1, waiting for transfers between devices, per_device(): lax.all_to_all(result, ('seq', 'head'), split_axis=0, concat_axis=0, tile...  5.44 us
  transfers between devices with their start and end apart: 10, of which 5 were waited for; matrix products, arithmetic and copies ran while one was open for 4% of the time, Pallas kernels for 27%

profile of v6, /device:TPU:0, one launch (start us, length us, event | category | flops | bytes accessed | tf_op | source)
XLA Modules:
  0.0 79.2 jit_solution(12789607677298142166)
XLA Ops:
  0.0 0.0 copy-start
  0.0 8.5 %key_pass.1 = (bf16[3072,768]{1,0:T(8,128)(2,1)S(1)}, bf16[3072,768]{1,0:T(8,128)(2,1)S(1)}, bf16[192,3072]{1,0:T(8,128)(2,1)S(1)}, bf16[12,192,256]{2,1,0:T(8,1...) custom-call(bf16[3072,768]{1,0:T(8,128)(2,1)} %tok_hbm.3, bf16[192,768]{1,0:T(8,128)(2,1)} %bitcast.23, ...), custom_call_target="tpu_custom_call" | custom-call | flops 5000000000 | bytes 12000000 | tf_op jit(solution)/shard_map/key_pass/pallas_call | solution.py:152
  8.5 0.5 collective-permute-start
  9.1 2.6 %collective-permute-start.1 = (s32[1,192]{1,0:T(1,128)S(1)}, s32[1,192]{1,0:T(1,128)S(1)}, u32[]{:S(2)}, u32[]{:S(2)}) collective-permute-start(s32[1,192]{1,0:T(1,128)S(1)} %get-tuple-element.36.rest_0_.rest_3_), channel_id=1, source_target_pairs={{0,2},{1,3},{2,0},{3,1},{4,6},{5,7},{6,4},{7,5},{8,10},{9,11},{10,... | collective-permute-start | bytes 2312 | tf_op jit(solution)/shard_map/ppermute | solution.py:560
  11.6 0.1 collective-permute-start.2
  11.7 1.8 %collective-permute-start.3 = (bf16[192,256]{1,0:T(8,128)(2,1)S(1)}, bf16[192,256]{1,0:T(8,128)(2,1)S(1)}, u32[]{:S(2)}, u32[]{:S(2)}) collective-permute-start(bf16[192,256]{1,0:T(8,128)(2,1)S(1)} %get-tuple-element.37), channel_id=1, source_target_pairs={{0,4},{4,0},{8,12},{12,8},{16,20},{20,16},{24,28},{28,24},{1,5},{5... | collective-permute-start | bytes 294920 | tf_op jit(solution)/shard_map/ppermute | solution.py:570
  13.4 0.0 copy-done
  13.4 0.0 copy-done.1
  13.5 2.8 %query_pass.3 = (bf16[4,768,768]{2,1,0:T(8,128)(2,1)S(1)}, f32[4,192,768]{2,1,0:T(8,128)S(1)}) custom-call(bf16[3072,768]{1,0:T(8,128)(2,1)S(1)} %get-tuple-element.32.tok_ref, f32[64,128]{1,0:T(8,128)S(1)} %copy-done.1, bf16[192,768]{1,0:T(8,128)(2,1)S(1)} %bitcast.12, bf16[3072,768]{1,0:T(8,128)(2,1)S(1)} %get-tuple-element.33.kf_ref, ...), custom_call_target="tpu_custom_call" | custom-call | flops 2000000000 | bytes 4000000 | tf_op jit(solution)/shard_map/query_pass/pallas_call | solution.py:269
  16.2 0.5 collective-permute-done.3.rest_0_
  16.8 1.9 %collective-permute-start.4 = (bf16[192,256]{1,0:T(8,128)(2,1)S(1)}, bf16[192,256]{1,0:T(8,128)(2,1)S(1)}, u32[]{:S(2)}, u32[]{:S(2)}) collective-permute-start(bf16[192,256]{1,0:T(8,128)(2,1)S(1)} %add_convert_fusion.1), channel_id=1, source_target_pairs={{0,8},{4,12},{8,0},{12,4},{16,24},{20,28},{24,16},{28,20},{1,9},{5... | collective-permute-start | bytes 294920 | tf_op jit(solution)/shard_map/ppermute | solution.py:570
  18.7 2.8 %query_pass.4 = (bf16[4,768,768]{2,1,0:T(8,128)(2,1)S(1)}, f32[4,192,768]{2,1,0:T(8,128)S(1)}) custom-call(bf16[3072,768]{1,0:T(8,128)(2,1)S(1)} %get-tuple-element.32.tok_ref, f32[64,128]{1,0:T(8,128)S(1)} %copy-done.1, bf16[192,768]{1,0:T(8,128)(2,1)S(1)} %bitcast.13, ...), custom_call_target="tpu_custom_call", output_to_operand_aliasing={{0}: (6, {}), {1}: (7, {})} | custom-call | flops 2000000000 | bytes 4000000 | tf_op jit(solution)/shard_map/query_pass/pallas_call | solution.py:269
  21.4 0.0 collective-permute-done.4.rest_1_
  21.5 2.9 %collective-permute-start.5 = (bf16[192,256]{1,0:T(8,128)(2,1)S(1)}, bf16[192,256]{1,0:T(8,128)(2,1)S(1)}, u32[]{:S(2)}, u32[]{:S(2)}) collective-permute-start(bf16[192,256]{1,0:T(8,128)(2,1)S(1)} %add_convert_fusion), channel_id=1, source_target_pairs={{0,16},{4,20},{8,24},{12,28},{16,0},{20,4},{24,8},{28,12},{1,17},{... | collective-permute-start | bytes 294920 | tf_op jit(solution)/shard_map/ppermute | solution.py:570
  24.4 0.0 collective-permute-done.rest_1_.rest_4_
  24.4 0.0 collective-permute-done.1.rest_2_.rest_5_
  24.4 0.0 collective-permute-done.2.rest_3_.rest_6_
  24.4 3.6 %query_pass.5 = (bf16[4,768,768]{2,1,0:T(8,128)(2,1)S(1)}, f32[4,192,768]{2,1,0:T(8,128)S(1)}, bf16[4,192,192]{2,1,0:T(8,128)(2,1)S(1)}) custom-call(bf16[3072,768]{1,0:T(8,128)(2,1)S(1)} %get-tuple-element.32.tok_ref, f32[64,128]{1,0:T(8,128)S(1)} %copy-done.1, bf16[192,768]{1,0:T(8,128)(2,1)S(1)} %bitcast.14, ...), custom_call_target="tpu_custom_call", output_to_operand_aliasing={{0}: (10, {}), {1}: (11, {})} | custom-call | flops 2000000000 | bytes 4000000 | tf_op jit(solution)/shard_map/query_pass/pallas_call | solution.py:269
  28.0 0.5 collective-permute-done.5.rest_2_
  28.5 3.1 %norm_pass.1 = (bf16[192,768]{1,0:T(8,128)(2,1)}, bf16[384,768]{1,0:T(8,128)(2,1)}, bf16[192,768]{1,0:T(8,128)(2,1)}, bf16[768,384]{1,0:T(8,128)(2,1)}) custom-call(f32[4,192,768]{2,1,0:T(8,128)S(1)} %get-tuple-element.47.raw_ref, bf16[4,768,768]{2,1,0:T(8,128)(2,1)S(1)} %get-tuple-element.48.qft_ref, bf16[4,192,192]{2,1,0:T(8,128)(2,1)S(1)} %get-tuple-element.49.seen_ref, ...), custom_call_target="tpu_custom_call" | custom-call | flops 3000000000 | bytes 8000000 | tf_op jit(solution)/shard_map/norm_pass/pallas_call | solution.py:334
  31.6 5.6 %all-to-all-start = ((bf16[32,24,384]{2,1,0:T(8,128)(2,1)}), bf16[32,24,384]{2,1,0:T(8,128)(2,1)S(1)}, u32[]{:S(2)}, u32[]{:S(2)}) async-start(bf16[32,24,384]{2,1,0:T(8,128)(2,1)} %bitcast.18), calls=%async_computation | async-start | bytes 1179648 | tf_op jit(solution)/shard_map/all_to_all | solution.py:581
  37.2 0.3 collective-permute-start.6
  37.5 0.0 copy-done.4
  37.5 0.1 copy.28
  37.6 0.1 copy.25
  37.7 0.1 pad.15.clone
  37.8 0.1 stack.16
  37.8 0.1 copy.26
  37.9 0.1 pad.16.clone
  38.0 0.1 stack.17
  38.1 0.1 copy.27
  38.2 0.1 pad.17.clone
  38.3 0.1 stack.18
  38.4 0.1 stack.15
  38.5 0.6 pad_add_fusion.pick_ref
  39.1 0.4 collective-permute-done.6.near_hbm
  39.5 1.2 %pad_maximum_fusion = bf16[384,768]{1,0:T(8,128)(2,1)S(1)} fusion(bf16[192,768]{1,0:T(8,128)(2,1)S(1)} %slice.16, bf16[192,768]{1,0:T(8,128)(2,1)} %get-tuple-element.53), kind=kLoop, calls=%fused_computation | loop fusion | flops 1179648 | bytes 1179648 | tf_op jit(solution)/shard_map/concatenate | solution.py:583
  40.7 1.8 %collective-permute-start.7 = (bf16[384,768]{1,0:T(8,128)(2,1)S(1)}, bf16[384,768]{1,0:T(8,128)(2,1)S(1)}, u32[]{:S(2)}, u32[]{:S(2)}) collective-permute-start(bf16[384,768]{1,0:T(8,128)(2,1)S(1)} %pad_maximum_fusion), channel_id=1, source_target_pairs={{0,2},{1,3},{2,0},{3,1},{4,6},{5,7},{6,4},{7,5},{8,10},{9,11},{10,... | collective-permute-start | bytes 1769480 | tf_op jit(solution)/shard_map/ppermute | solution.py:560
  42.5 11.4 %all-to-all-done = bf16[32,24,384]{2,1,0:T(8,128)(2,1)S(1)} async-done(((bf16[32,24,384]{2,1,0:T(8,128)(2,1)}), bf16[32,24,384]{2,1,0:T(8,128)(2,1)S(1)}, u32[]{:S(2)}, u32[]{:S(2)}) %all-to-all-start) | async-done | bytes 589856 | tf_op jit(solution)/shard_map/all_to_all | solution.py:581
  53.9 6.4 %expert_pass.1 = bf16[32,40,128]{2,1,0:T(8,128)(2,1)} custom-call(bf16[8,4,24,384]{3,2,1,0:T(8,128)(2,1)S(1)} %bitcast.15, bf16[4,192,768]{2,1,0:T(8,128)(2,1)} %bitcast.16, bf16[1,768,3072]{2,1,0:T(8,128)(2,1)} %wi_hbm.1, bf16[1,3072,768]{2,1,0:T(8,128)(2,1)} %wd_hbm.1), custom_call_target="tpu_custom_call" | custom-call | flops 2000000000 | bytes 12000000 | tf_op jit(solution)/shard_map/expert_pass/pallas_call | solution.py:417
  60.4 0.0 copy-done.2
  60.4 3.3 %all-to-all-start.1 = ((bf16[32,40,128]{2,1,0:T(8,128)(2,1)}), bf16[32,40,128]{2,1,0:T(8,128)(2,1)S(1)}, u32[]{:S(2)}, u32[]{:S(2)}) async-start(bf16[32,40,128]{2,1,0:T(8,128)(2,1)} %expert_pass.1), calls=%async_computation.1 | async-start | bytes 655360 | tf_op jit(solution)/shard_map/all_to_all | solution.py:589
  63.7 0.0 collective-permute-done.7.far_hbm
  63.7 0.0 copy-start.3
  63.7 0.8 %copy-done.3 = bf16[384,768]{1,0:T(8,128)(2,1)} copy-done((bf16[384,768]{1,0:T(8,128)(2,1)}, bf16[384,768]{1,0:T(8,128)(2,1)S(1)}, u32[]{:S(2)}) %copy-start.3) | copy-done | bytes 589848
  64.5 5.7 %hidden_pass.1 = (bf16[768,768]{1,0:T(8,128)(2,1)}, bf16[4,768,256]{2,1,0:T(8,128)(2,1)}) custom-call(bf16[3072,768]{1,0:T(8,128)(2,1)} %tok_hbm.3, bf16[4,192,768]{2,1,0:T(8,128)(2,1)} %bitcast.17, bf16[192,768]{1,0:T(8,128)(2,1)} %get-tuple-element.51.own_hbm, bf16[384,768]{1,0:T(8,128)(2,1)} %copy-done.2, bf16[384,768]{1,0:T(8,128)(2,1)} %copy-done.3, ...), custom_call_target="tpu_custom_call" | custom-call | flops 2000000000 | bytes 6000000 | tf_op jit(solution)/shard_map/hidden_pass/pallas_call | solution.py:469
  70.2 5.4 %all-to-all-done.1.back_hbm = bf16[32,40,128]{2,1,0:T(8,128)(2,1)S(1)} async-done(((bf16[32,40,128]{2,1,0:T(8,128)(2,1)}), bf16[32,40,128]{2,1,0:T(8,128)(2,1)S(1)}, u32[]{:S(2)}, u32[]{:S(2)}) %all-to-all-start.1) | async-done | bytes 327712 | tf_op jit(solution)/shard_map/all_to_all | solution.py:589
  75.7 3.4 %combine_pass.1 = bf16[768,768]{1,0:T(8,128)(2,1)} custom-call(bf16[768,768]{1,0:T(8,128)(2,1)} %get-tuple-element.56.hid_hbm, bf16[4,768,256]{2,1,0:T(8,128)(2,1)} %get-tuple-element.57.comb_hbm, bf16[32,40,128]{2,1,0:T(8,128)(2,1)S(1)} %all-to-all-done.1.back_hbm), custom_call_target="tpu_custom_call" | custom-call | flops 1000000000 | bytes 4000000 | tf_op jit(solution)/shard_map/combine_pass/pallas_call | solution.py:527
  (9 shorter events, 0.1 us)
Async XLA Ops:
  0.0 13.4 %copy-start = (bf16[768,192]{0,1:T(8,128)(2,1)S(1)}, bf16[768,192]{0,1:T(8,128)(2,1)}, u32[]{:S(2)}) copy-start(bf16[768,192]{0,1:T(8,128)(2,1)} %param.11) | copy-start | bytes 884740
  0.0 13.4 %copy-start.1 = (f32[64,128]{1,0:T(8,128)S(1)}, f32[64,128]{1,0:T(8,128)}, u32[]{:S(2)}) copy-start(f32[64,128]{1,0:T(8,128)} %freq_ref.5) | copy-start | bytes 98308
  8.5 15.8 %collective-permute-start = (s32[1,192]{1,0:T(1,128)S(1)}, s32[1,192]{1,0:T(1,128)S(1)}, u32[]{:S(2)}, u32[]{:S(2)}) collective-permute-start(s32[1,192]{1,0:T(1,128)S(1)} %get-tuple-element.36.rest_0_.rest_3_), channel_id=1, source_target_pairs={{0,1},{1,0},{2,3},{3,2},{4,5},{5,4},{6,7},{7,6},{8,9},{9,8},{10,11... | collective-permute-start | bytes 2312 | tf_op jit(solution)/shard_map/ppermute | solution.py:560
  9.1 15.3 %collective-permute-start.1 = (s32[1,192]{1,0:T(1,128)S(1)}, s32[1,192]{1,0:T(1,128)S(1)}, u32[]{:S(2)}, u32[]{:S(2)}) collective-permute-start(s32[1,192]{1,0:T(1,128)S(1)} %get-tuple-element.36.rest_0_.rest_3_), channel_id=1, source_target_pairs={{0,2},{1,3},{2,0},{3,1},{4,6},{5,7},{6,4},{7,5},{8,10},{9,11},{10,... | collective-permute-start | bytes 2312 | tf_op jit(solution)/shard_map/ppermute | solution.py:560
  11.6 12.8 %collective-permute-start.2 = (s32[1,192]{1,0:T(1,128)S(1)}, s32[1,192]{1,0:T(1,128)S(1)}, u32[]{:S(2)}, u32[]{:S(2)}) collective-permute-start(s32[1,192]{1,0:T(1,128)S(1)} %get-tuple-element.36.rest_0_.rest_3_), channel_id=1, source_target_pairs={{0,3},{1,2},{2,1},{3,0},{4,7},{5,6},{6,5},{7,4},{8,11},{9,10},{10,... | collective-permute-start | bytes 2312 | tf_op jit(solution)/shard_map/ppermute | solution.py:560
  11.7 5.1 %collective-permute-start.3 = (bf16[192,256]{1,0:T(8,128)(2,1)S(1)}, bf16[192,256]{1,0:T(8,128)(2,1)S(1)}, u32[]{:S(2)}, u32[]{:S(2)}) collective-permute-start(bf16[192,256]{1,0:T(8,128)(2,1)S(1)} %get-tuple-element.37), channel_id=1, source_target_pairs={{0,4},{4,0},{8,12},{12,8},{16,20},{20,16},{24,28},{28,24},{1,5},{5... | collective-permute-start | bytes 294920 | tf_op jit(solution)/shard_map/ppermute | solution.py:570
  16.8 4.7 %collective-permute-start.4 = (bf16[192,256]{1,0:T(8,128)(2,1)S(1)}, bf16[192,256]{1,0:T(8,128)(2,1)S(1)}, u32[]{:S(2)}, u32[]{:S(2)}) collective-permute-start(bf16[192,256]{1,0:T(8,128)(2,1)S(1)} %add_convert_fusion.1), channel_id=1, source_target_pairs={{0,8},{4,12},{8,0},{12,4},{16,24},{20,28},{24,16},{28,20},{1,9},{5... | collective-permute-start | bytes 294920 | tf_op jit(solution)/shard_map/ppermute | solution.py:570
  21.5 7.0 %collective-permute-start.5 = (bf16[192,256]{1,0:T(8,128)(2,1)S(1)}, bf16[192,256]{1,0:T(8,128)(2,1)S(1)}, u32[]{:S(2)}, u32[]{:S(2)}) collective-permute-start(bf16[192,256]{1,0:T(8,128)(2,1)S(1)} %add_convert_fusion), channel_id=1, source_target_pairs={{0,16},{4,20},{8,24},{12,28},{16,0},{20,4},{24,8},{28,12},{1,17},{... | collective-permute-start | bytes 294920 | tf_op jit(solution)/shard_map/ppermute | solution.py:570
  28.5 9.0 %copy-start.4 = (s32[32,1,6]{0,1,2:T(1,128)S(1)}, s32[32,1,6]{0,1,2:T(1,128)}, u32[]{:S(2)}) copy-start(s32[32,1,6]{0,1,2:T(1,128)} %param.19) | copy-start | bytes 2308
  31.6 22.3 %all-to-all-start = ((bf16[32,24,384]{2,1,0:T(8,128)(2,1)}), bf16[32,24,384]{2,1,0:T(8,128)(2,1)S(1)}, u32[]{:S(2)}, u32[]{:S(2)}) async-start(bf16[32,24,384]{2,1,0:T(8,128)(2,1)} %bitcast.18), calls=%async_computation | async-start | bytes 1179648 | tf_op jit(solution)/shard_map/all_to_all | solution.py:581
  37.2 2.3 %collective-permute-start.6 = (bf16[384,768]{1,0:T(8,128)(2,1)}, bf16[384,768]{1,0:T(8,128)(2,1)S(1)}, u32[]{:S(2)}, u32[]{:S(2)}) collective-permute-start(bf16[384,768]{1,0:T(8,128)(2,1)} %get-tuple-element.52), channel_id=1, source_target_pairs={{0,1},{1,0},{2,3},{3,2},{4,5},{5,4},{6,7},{7,6},{8,9},{9,8},{10,11... | collective-permute-start | bytes 1769480 | tf_op jit(solution)/shard_map/ppermute | solution.py:560
  39.5 20.9 %copy-start.2 = (bf16[384,768]{1,0:T(8,128)(2,1)}, bf16[384,768]{1,0:T(8,128)(2,1)S(1)}, u32[]{:S(2)}) copy-start(bf16[384,768]{1,0:T(8,128)(2,1)S(1)} %collective-permute-done.6.near_hbm) | copy-start | bytes 1769476
  40.7 23.0 %collective-permute-start.7 = (bf16[384,768]{1,0:T(8,128)(2,1)S(1)}, bf16[384,768]{1,0:T(8,128)(2,1)S(1)}, u32[]{:S(2)}, u32[]{:S(2)}) collective-permute-start(bf16[384,768]{1,0:T(8,128)(2,1)S(1)} %pad_maximum_fusion), channel_id=1, source_target_pairs={{0,2},{1,3},{2,0},{3,1},{4,6},{5,7},{6,4},{7,5},{8,10},{9,11},{10,... | collective-permute-start | bytes 1769480 | tf_op jit(solution)/shard_map/ppermute | solution.py:560
  60.4 15.3 %all-to-all-start.1 = ((bf16[32,40,128]{2,1,0:T(8,128)(2,1)}), bf16[32,40,128]{2,1,0:T(8,128)(2,1)S(1)}, u32[]{:S(2)}, u32[]{:S(2)}) async-start(bf16[32,40,128]{2,1,0:T(8,128)(2,1)} %expert_pass.1), calls=%async_computation.1 | async-start | bytes 655360 | tf_op jit(solution)/shard_map/all_to_all | solution.py:589
  63.7 0.8 %copy-start.3 = (bf16[384,768]{1,0:T(8,128)(2,1)}, bf16[384,768]{1,0:T(8,128)(2,1)S(1)}, u32[]{:S(2)}) copy-start(bf16[384,768]{1,0:T(8,128)(2,1)S(1)} %collective-permute-done.7.far_hbm) | copy-start | bytes 1769476

commit v7 on v6

--- a/solution.py
+++ b/solution.py
@@ -281,7 +281,7 @@
 def norm_kernel(slots, cap, rounds, raw_ref, qft_ref, seen_ref, *rest):
     got_refs, pick_refs = rest[:rounds], rest[rounds : rounds + slots]
     outs = rest[rounds + slots : rounds + slots + 3]
-    sent_hbm, ready, acc, sent, sems = rest[rounds + slots + 3 :]
+    sent, ready, acc, sems = rest[rounds + slots + 3 :]
     me, at = lax.axis_index("head"), lax.axis_index("seq")
     wid = raw_ref.shape[1]
     heads = wid // HD
@@ -321,11 +321,8 @@
             if 0 <= t - i < slots:
                 stage(t - i)
     sent[...] = acc[...].astype(BF)
-    last = pltpu.make_async_copy(sent, sent_hbm, sems.at[slots])
-    last.start()
     for copy in copies:
         copy.wait()
-    last.wait()
 
 
 def norm_pass(raw, qft, seen, got, picks, cap):
@@ -334,12 +331,12 @@
     return pl.pallas_call(
         functools.partial(norm_kernel, slots, cap, len(got)),
         in_specs=[HERE] * (3 + len(got) + slots),
-        out_specs=[FAR] * 4,
-        out_shape=[pltpu.HBM(x, BF) for x in ((wid, rows), (2 * wid, rows), (wid, rows), (n, 2 * wid))],
+        out_specs=[FAR] * 3 + [HERE],
+        out_shape=[pltpu.HBM(x, BF) for x in ((wid, rows), (2 * wid, rows), (wid, rows))]
+        + [jax.ShapeDtypeStruct((n, 2 * wid), BF)],
         scratch_shapes=[
             pltpu.VMEM((slots, wid, rows), BF),
             pltpu.VMEM((n, 2 * wid), F32),
-            pltpu.VMEM((n, 2 * wid), BF),
             pltpu.SemaphoreType.DMA((slots + 1,)),
         ],
         compiler_params=params(KEPT + n * wid * 20 // MIB),
@@ -560,7 +557,7 @@
     swap = lambda x, k: lax.ppermute(x, "head", [(i, i ^ k) for i in range(group)])
 
     tok_here, kf, vt, sc, held, own = key_pass(
-        tokens, w_key.T, w_value.T, freq, picks.transpose(2, 1, 0), rows
+        tokens, w_key.T, w_value.T, freq, picks.transpose(2, 1, 0), math.gcd(total, 4 * CHUNK)
     )
     near = [own] + [swap(own, k) for k in range(1, group)]
     got, made = [], []

time: 79.6 us -> 79.5 us (level)
  no operation moved by 1% of the time
where the time goes in v7:
time: 79.5 us; the launch traced here: 79.2 us
  Pallas kernels  36.3 us (46%)
  starting transfers between devices  20.7 us (26%)
  waiting for transfers between devices  18.3 us (23%)
  other arithmetic  1.87 us (2%)
  local copies, waits for them, and re-layouts  1.79 us (2%)
    all_to_all x1, waiting for transfers between devices, per_device(): lax.all_to_all(sent, ('seq', 'head'), split_axis=0, concat_axis=0, tiled=...  11.4 us
    pallas_call x3, Pallas kernels, query_pass(): pl.pallas_call(functools.partial(query_kernel, chunks, slots, len(picks))...  9.19 us
    pallas_call x1, Pallas kernels, key_pass(): pl.pallas_call(functools.partial(key_kernel, size), in_specs=[FAR] * 5, o...  8.48 us
    ppermute x3, starting transfers between devices, per_device(): lax.ppermute(held, 'seq', [(j, j ^ 1 << i) for j in range(ring)])  6.51 us
    pallas_call x1, Pallas kernels, expert_pass(): pl.pallas_call(functools.partial(expert_kernel, cap, ups, downs), in_spec...  6.45 us
    pallas_call x1, Pallas kernels, hidden_pass(): pl.pallas_call(hidden_kernel, in_specs=[FAR] * 2 + [AWAY] * 3 + [HERE] *...  5.72 us
    all_to_all x1, starting transfers between devices, per_device(): lax.all_to_all(sent, ('seq', 'head'), split_axis=0, concat_axis=0, tiled=...  5.58 us
    all_to_all x1, waiting for transfers between devices, per_device(): lax.all_to_all(result, ('seq', 'head'), split_axis=0, concat_axis=0, tile...  5.44 us
  transfers between devices with their start and end apart: 10, of which 5 were waited for; matrix products, arithmetic and copies ran while one was open for 4% of the time, Pallas kernels for 27%

profile of v7, /device:TPU:0, one launch (start us, length us, event | category | flops | bytes accessed | tf_op | source)
XLA Modules:
  0.0 79.2 jit_solution(10789415815197548189)
XLA Ops:
  0.0 0.0 copy-start
  0.0 8.5 %key_pass.1 = (bf16[3072,768]{1,0:T(8,128)(2,1)S(1)}, bf16[3072,768]{1,0:T(8,128)(2,1)S(1)}, bf16[192,3072]{1,0:T(8,128)(2,1)S(1)}, bf16[12,192,256]{2,1,0:T(8,1...) custom-call(bf16[3072,768]{1,0:T(8,128)(2,1)} %tok_hbm.3, bf16[192,768]{1,0:T(8,128)(2,1)} %bitcast.22, ...), custom_call_target="tpu_custom_call" | custom-call | flops 5000000000 | bytes 12000000 | tf_op jit(solution)/shard_map/key_pass/pallas_call | solution.py:152
  8.5 0.5 collective-permute-start
  9.0 2.6 %collective-permute-start.1 = (s32[1,192]{1,0:T(1,128)S(1)}, s32[1,192]{1,0:T(1,128)S(1)}, u32[]{:S(2)}, u32[]{:S(2)}) collective-permute-start(s32[1,192]{1,0:T(1,128)S(1)} %get-tuple-element.36.rest_0_.rest_3_), channel_id=1, source_target_pairs={{0,2},{1,3},{2,0},{3,1},{4,6},{5,7},{6,4},{7,5},{8,10},{9,11},{10,... | collective-permute-start | bytes 2312 | tf_op jit(solution)/shard_map/ppermute | solution.py:557
  11.6 0.1 collective-permute-start.2
  11.6 1.8 %collective-permute-start.3 = (bf16[192,256]{1,0:T(8,128)(2,1)S(1)}, bf16[192,256]{1,0:T(8,128)(2,1)S(1)}, u32[]{:S(2)}, u32[]{:S(2)}) collective-permute-start(bf16[192,256]{1,0:T(8,128)(2,1)S(1)} %get-tuple-element.37), channel_id=1, source_target_pairs={{0,4},{4,0},{8,12},{12,8},{16,20},{20,16},{24,28},{28,24},{1,5},{5... | collective-permute-start | bytes 294920 | tf_op jit(solution)/shard_map/ppermute | solution.py:567
  13.4 0.0 copy-done
  13.4 0.0 copy-done.1
  13.4 2.8 %query_pass.3 = (bf16[4,768,768]{2,1,0:T(8,128)(2,1)S(1)}, f32[4,192,768]{2,1,0:T(8,128)S(1)}) custom-call(bf16[3072,768]{1,0:T(8,128)(2,1)S(1)} %get-tuple-element.32.tok_ref, f32[64,128]{1,0:T(8,128)S(1)} %copy-done.1, bf16[192,768]{1,0:T(8,128)(2,1)S(1)} %bitcast.12, bf16[3072,768]{1,0:T(8,128)(2,1)S(1)} %get-tuple-element.33.kf_ref, ...), custom_call_target="tpu_custom_call" | custom-call | flops 2000000000 | bytes 4000000 | tf_op jit(solution)/shard_map/query_pass/pallas_call | solution.py:269
  16.2 0.5 collective-permute-done.3.rest_0_
  16.7 1.9 %collective-permute-start.4 = (bf16[192,256]{1,0:T(8,128)(2,1)S(1)}, bf16[192,256]{1,0:T(8,128)(2,1)S(1)}, u32[]{:S(2)}, u32[]{:S(2)}) collective-permute-start(bf16[192,256]{1,0:T(8,128)(2,1)S(1)} %add_convert_fusion.1), channel_id=1, source_target_pairs={{0,8},{4,12},{8,0},{12,4},{16,24},{20,28},{24,16},{28,20},{1,9},{5... | collective-permute-start | bytes 294920 | tf_op jit(solution)/shard_map/ppermute | solution.py:567
  18.6 2.8 %query_pass.4 = (bf16[4,768,768]{2,1,0:T(8,128)(2,1)S(1)}, f32[4,192,768]{2,1,0:T(8,128)S(1)}) custom-call(bf16[3072,768]{1,0:T(8,128)(2,1)S(1)} %get-tuple-element.32.tok_ref, f32[64,128]{1,0:T(8,128)S(1)} %copy-done.1, bf16[192,768]{1,0:T(8,128)(2,1)S(1)} %bitcast.13, ...), custom_call_target="tpu_custom_call", output_to_operand_aliasing={{0}: (6, {}), {1}: (7, {})} | custom-call | flops 2000000000 | bytes 4000000 | tf_op jit(solution)/shard_map/query_pass/pallas_call | solution.py:269
  21.4 0.0 collective-permute-done.4.rest_1_
  21.4 2.9 %collective-permute-start.5 = (bf16[192,256]{1,0:T(8,128)(2,1)S(1)}, bf16[192,256]{1,0:T(8,128)(2,1)S(1)}, u32[]{:S(2)}, u32[]{:S(2)}) collective-permute-start(bf16[192,256]{1,0:T(8,128)(2,1)S(1)} %add_convert_fusion), channel_id=1, source_target_pairs={{0,16},{4,20},{8,24},{12,28},{16,0},{20,4},{24,8},{28,12},{1,17},{... | collective-permute-start | bytes 294920 | tf_op jit(solution)/shard_map/ppermute | solution.py:567
  24.3 0.0 collective-permute-done.rest_1_.rest_4_
  24.3 0.0 collective-permute-done.1.rest_2_.rest_5_
  24.3 0.0 collective-permute-done.2.rest_3_.rest_6_
  24.3 3.6 %query_pass.5 = (bf16[4,768,768]{2,1,0:T(8,128)(2,1)S(1)}, f32[4,192,768]{2,1,0:T(8,128)S(1)}, bf16[4,192,192]{2,1,0:T(8,128)(2,1)S(1)}) custom-call(bf16[3072,768]{1,0:T(8,128)(2,1)S(1)} %get-tuple-element.32.tok_ref, f32[64,128]{1,0:T(8,128)S(1)} %copy-done.1, bf16[192,768]{1,0:T(8,128)(2,1)S(1)} %bitcast.14, ...), custom_call_target="tpu_custom_call", output_to_operand_aliasing={{0}: (10, {}), {1}: (11, {})} | custom-call | flops 2000000000 | bytes 4000000 | tf_op jit(solution)/shard_map/query_pass/pallas_call | solution.py:269
  28.0 0.5 collective-permute-done.5.rest_2_
  28.5 3.1 %norm_pass.1 = (bf16[192,768]{1,0:T(8,128)(2,1)}, bf16[384,768]{1,0:T(8,128)(2,1)}, bf16[192,768]{1,0:T(8,128)(2,1)}, bf16[768,384]{1,0:T(8,128)(2,1)}) custom-call(f32[4,192,768]{2,1,0:T(8,128)S(1)} %get-tuple-element.47.raw_ref, bf16[4,768,768]{2,1,0:T(8,128)(2,1)S(1)} %get-tuple-element.48.qft_ref, bf16[4,192,192]{2,1,0:T(8,128)(2,1)S(1)} %get-tuple-element.49.seen_ref, ...), custom_call_target="tpu_custom_call" | custom-call | flops 3000000000 | bytes 8000000 | tf_op jit(solution)/shard_map/norm_pass/pallas_call | solution.py:331
  31.5 5.6 %all-to-all-start = ((bf16[32,24,384]{2,1,0:T(8,128)(2,1)}), bf16[32,24,384]{2,1,0:T(8,128)(2,1)S(1)}, u32[]{:S(2)}, u32[]{:S(2)}) async-start(bf16[32,24,384]{2,1,0:T(8,128)(2,1)} %bitcast.6), calls=%async_computation | async-start | bytes 1179648 | tf_op jit(solution)/shard_map/all_to_all | solution.py:578
  37.1 0.3 collective-permute-start.6
  37.5 0.0 copy-done.4
  37.5 0.1 copy.28
  37.6 0.1 copy.25
  37.6 0.1 pad.15.clone
  37.7 0.1 stack.16
  37.8 0.1 copy.26
  37.9 0.1 pad.16.clone
  38.0 0.1 stack.17
  38.1 0.1 copy.27
  38.2 0.1 pad.17.clone
  38.2 0.1 stack.18
  38.3 0.1 stack.15
  38.4 0.6 pad_add_fusion.pick_ref
  39.0 0.4 collective-permute-done.6.near_hbm
  39.4 1.2 %pad_maximum_fusion = bf16[384,768]{1,0:T(8,128)(2,1)S(1)} fusion(bf16[192,768]{1,0:T(8,128)(2,1)S(1)} %slice.16, bf16[192,768]{1,0:T(8,128)(2,1)} %get-tuple-element.53), kind=kLoop, calls=%fused_computation | loop fusion | flops 1179648 | bytes 1179648 | tf_op jit(solution)/shard_map/concatenate | solution.py:580
  40.7 1.8 %collective-permute-start.7 = (bf16[384,768]{1,0:T(8,128)(2,1)S(1)}, bf16[384,768]{1,0:T(8,128)(2,1)S(1)}, u32[]{:S(2)}, u32[]{:S(2)}) collective-permute-start(bf16[384,768]{1,0:T(8,128)(2,1)S(1)} %pad_maximum_fusion), channel_id=1, source_target_pairs={{0,2},{1,3},{2,0},{3,1},{4,6},{5,7},{6,4},{7,5},{8,10},{9,11},{10,... | collective-permute-start | bytes 1769480 | tf_op jit(solution)/shard_map/ppermute | solution.py:557
  42.5 11.4 %all-to-all-done = bf16[32,24,384]{2,1,0:T(8,128)(2,1)S(1)} async-done(((bf16[32,24,384]{2,1,0:T(8,128)(2,1)}), bf16[32,24,384]{2,1,0:T(8,128)(2,1)S(1)}, u32[]{:S(2)}, u32[]{:S(2)}) %all-to-all-start) | async-done | bytes 589856 | tf_op jit(solution)/shard_map/all_to_all | solution.py:578
  53.9 6.5 %expert_pass.1 = bf16[32,40,128]{2,1,0:T(8,128)(2,1)} custom-call(bf16[8,4,24,384]{3,2,1,0:T(8,128)(2,1)S(1)} %bitcast.15, bf16[4,192,768]{2,1,0:T(8,128)(2,1)} %bitcast.16, bf16[1,768,3072]{2,1,0:T(8,128)(2,1)} %wi_hbm.1, bf16[1,3072,768]{2,1,0:T(8,128)(2,1)} %wd_hbm.1), custom_call_target="tpu_custom_call" | custom-call | flops 2000000000 | bytes 12000000 | tf_op jit(solution)/shard_map/expert_pass/pallas_call | solution.py:414
  60.4 0.0 copy-done.2
  60.4 3.3 %all-to-all-start.1 = ((bf16[32,40,128]{2,1,0:T(8,128)(2,1)}), bf16[32,40,128]{2,1,0:T(8,128)(2,1)S(1)}, u32[]{:S(2)}, u32[]{:S(2)}) async-start(bf16[32,40,128]{2,1,0:T(8,128)(2,1)} %expert_pass.1), calls=%async_computation.1 | async-start | bytes 655360 | tf_op jit(solution)/shard_map/all_to_all | solution.py:586
  63.6 0.0 collective-permute-done.7.far_hbm
  63.7 0.0 copy-start.3
  63.7 0.8 %copy-done.3 = bf16[384,768]{1,0:T(8,128)(2,1)} copy-done((bf16[384,768]{1,0:T(8,128)(2,1)}, bf16[384,768]{1,0:T(8,128)(2,1)S(1)}, u32[]{:S(2)}) %copy-start.3) | copy-done | bytes 589848
  64.5 5.7 %hidden_pass.1 = (bf16[768,768]{1,0:T(8,128)(2,1)}, bf16[4,768,256]{2,1,0:T(8,128)(2,1)}) custom-call(bf16[3072,768]{1,0:T(8,128)(2,1)} %tok_hbm.3, bf16[4,192,768]{2,1,0:T(8,128)(2,1)} %bitcast.17, bf16[192,768]{1,0:T(8,128)(2,1)} %get-tuple-element.51.own_hbm, bf16[384,768]{1,0:T(8,128)(2,1)} %copy-done.2, bf16[384,768]{1,0:T(8,128)(2,1)} %copy-done.3, ...), custom_call_target="tpu_custom_call" | custom-call | flops 2000000000 | bytes 6000000 | tf_op jit(solution)/shard_map/hidden_pass/pallas_call | solution.py:466
  70.2 5.4 %all-to-all-done.1.back_hbm = bf16[32,40,128]{2,1,0:T(8,128)(2,1)S(1)} async-done(((bf16[32,40,128]{2,1,0:T(8,128)(2,1)}), bf16[32,40,128]{2,1,0:T(8,128)(2,1)S(1)}, u32[]{:S(2)}, u32[]{:S(2)}) %all-to-all-start.1) | async-done | bytes 327712 | tf_op jit(solution)/shard_map/all_to_all | solution.py:586
  75.6 3.4 %combine_pass.1 = bf16[768,768]{1,0:T(8,128)(2,1)} custom-call(bf16[768,768]{1,0:T(8,128)(2,1)} %get-tuple-element.56.hid_hbm, bf16[4,768,256]{2,1,0:T(8,128)(2,1)} %get-tuple-element.57.comb_hbm, bf16[32,40,128]{2,1,0:T(8,128)(2,1)S(1)} %all-to-all-done.1.back_hbm), custom_call_target="tpu_custom_call" | custom-call | flops 1000000000 | bytes 4000000 | tf_op jit(solution)/shard_map/combine_pass/pallas_call | solution.py:524
  (9 shorter events, 0.1 us)
Async XLA Ops:
  0.0 13.4 %copy-start = (bf16[768,192]{0,1:T(8,128)(2,1)S(1)}, bf16[768,192]{0,1:T(8,128)(2,1)}, u32[]{:S(2)}) copy-start(bf16[768,192]{0,1:T(8,128)(2,1)} %param.11) | copy-start | bytes 884740
  0.0 13.4 %copy-start.1 = (f32[64,128]{1,0:T(8,128)S(1)}, f32[64,128]{1,0:T(8,128)}, u32[]{:S(2)}) copy-start(f32[64,128]{1,0:T(8,128)} %freq_ref.5) | copy-start | bytes 98308
  8.5 15.8 %collective-permute-start = (s32[1,192]{1,0:T(1,128)S(1)}, s32[1,192]{1,0:T(1,128)S(1)}, u32[]{:S(2)}, u32[]{:S(2)}) collective-permute-start(s32[1,192]{1,0:T(1,128)S(1)} %get-tuple-element.36.rest_0_.rest_3_), channel_id=1, source_target_pairs={{0,1},{1,0},{2,3},{3,2},{4,5},{5,4},{6,7},{7,6},{8,9},{9,8},{10,11... | collective-permute-start | bytes 2312 | tf_op jit(solution)/shard_map/ppermute | solution.py:557
  9.0 15.3 %collective-permute-start.1 = (s32[1,192]{1,0:T(1,128)S(1)}, s32[1,192]{1,0:T(1,128)S(1)}, u32[]{:S(2)}, u32[]{:S(2)}) collective-permute-start(s32[1,192]{1,0:T(1,128)S(1)} %get-tuple-element.36.rest_0_.rest_3_), channel_id=1, source_target_pairs={{0,2},{1,3},{2,0},{3,1},{4,6},{5,7},{6,4},{7,5},{8,10},{9,11},{10,... | collective-permute-start | bytes 2312 | tf_op jit(solution)/shard_map/ppermute | solution.py:557
  11.6 12.8 %collective-permute-start.2 = (s32[1,192]{1,0:T(1,128)S(1)}, s32[1,192]{1,0:T(1,128)S(1)}, u32[]{:S(2)}, u32[]{:S(2)}) collective-permute-start(s32[1,192]{1,0:T(1,128)S(1)} %get-tuple-element.36.rest_0_.rest_3_), channel_id=1, source_target_pairs={{0,3},{1,2},{2,1},{3,0},{4,7},{5,6},{6,5},{7,4},{8,11},{9,10},{10,... | collective-permute-start | bytes 2312 | tf_op jit(solution)/shard_map/ppermute | solution.py:557
  11.6 5.1 %collective-permute-start.3 = (bf16[192,256]{1,0:T(8,128)(2,1)S(1)}, bf16[192,256]{1,0:T(8,128)(2,1)S(1)}, u32[]{:S(2)}, u32[]{:S(2)}) collective-permute-start(bf16[192,256]{1,0:T(8,128)(2,1)S(1)} %get-tuple-element.37), channel_id=1, source_target_pairs={{0,4},{4,0},{8,12},{12,8},{16,20},{20,16},{24,28},{28,24},{1,5},{5... | collective-permute-start | bytes 294920 | tf_op jit(solution)/shard_map/ppermute | solution.py:567
  16.7 4.7 %collective-permute-start.4 = (bf16[192,256]{1,0:T(8,128)(2,1)S(1)}, bf16[192,256]{1,0:T(8,128)(2,1)S(1)}, u32[]{:S(2)}, u32[]{:S(2)}) collective-permute-start(bf16[192,256]{1,0:T(8,128)(2,1)S(1)} %add_convert_fusion.1), channel_id=1, source_target_pairs={{0,8},{4,12},{8,0},{12,4},{16,24},{20,28},{24,16},{28,20},{1,9},{5... | collective-permute-start | bytes 294920 | tf_op jit(solution)/shard_map/ppermute | solution.py:567
  21.4 7.0 %collective-permute-start.5 = (bf16[192,256]{1,0:T(8,128)(2,1)S(1)}, bf16[192,256]{1,0:T(8,128)(2,1)S(1)}, u32[]{:S(2)}, u32[]{:S(2)}) collective-permute-start(bf16[192,256]{1,0:T(8,128)(2,1)S(1)} %add_convert_fusion), channel_id=1, source_target_pairs={{0,16},{4,20},{8,24},{12,28},{16,0},{20,4},{24,8},{28,12},{1,17},{... | collective-permute-start | bytes 294920 | tf_op jit(solution)/shard_map/ppermute | solution.py:567
  28.5 9.0 %copy-start.4 = (s32[32,1,6]{0,1,2:T(1,128)S(1)}, s32[32,1,6]{0,1,2:T(1,128)}, u32[]{:S(2)}) copy-start(s32[32,1,6]{0,1,2:T(1,128)} %param.19) | copy-start | bytes 2308
  31.5 22.3 %all-to-all-start = ((bf16[32,24,384]{2,1,0:T(8,128)(2,1)}), bf16[32,24,384]{2,1,0:T(8,128)(2,1)S(1)}, u32[]{:S(2)}, u32[]{:S(2)}) async-start(bf16[32,24,384]{2,1,0:T(8,128)(2,1)} %bitcast.6), calls=%async_computation | async-start | bytes 1179648 | tf_op jit(solution)/shard_map/all_to_all | solution.py:578
  37.1 2.3 %collective-permute-start.6 = (bf16[384,768]{1,0:T(8,128)(2,1)}, bf16[384,768]{1,0:T(8,128)(2,1)S(1)}, u32[]{:S(2)}, u32[]{:S(2)}) collective-permute-start(bf16[384,768]{1,0:T(8,128)(2,1)} %get-tuple-element.52), channel_id=1, source_target_pairs={{0,1},{1,0},{2,3},{3,2},{4,5},{5,4},{6,7},{7,6},{8,9},{9,8},{10,11... | collective-permute-start | bytes 1769480 | tf_op jit(solution)/shard_map/ppermute | solution.py:557
  39.4 20.9 %copy-start.2 = (bf16[384,768]{1,0:T(8,128)(2,1)}, bf16[384,768]{1,0:T(8,128)(2,1)S(1)}, u32[]{:S(2)}) copy-start(bf16[384,768]{1,0:T(8,128)(2,1)S(1)} %collective-permute-done.6.near_hbm) | copy-start | bytes 1769476
  40.7 23.0 %collective-permute-start.7 = (bf16[384,768]{1,0:T(8,128)(2,1)S(1)}, bf16[384,768]{1,0:T(8,128)(2,1)S(1)}, u32[]{:S(2)}, u32[]{:S(2)}) collective-permute-start(bf16[384,768]{1,0:T(8,128)(2,1)S(1)} %pad_maximum_fusion), channel_id=1, source_target_pairs={{0,2},{1,3},{2,0},{3,1},{4,6},{5,7},{6,4},{7,5},{8,10},{9,11},{10,... | collective-permute-start | bytes 1769480 | tf_op jit(solution)/shard_map/ppermute | solution.py:557
  60.4 15.3 %all-to-all-start.1 = ((bf16[32,40,128]{2,1,0:T(8,128)(2,1)}), bf16[32,40,128]{2,1,0:T(8,128)(2,1)S(1)}, u32[]{:S(2)}, u32[]{:S(2)}) async-start(bf16[32,40,128]{2,1,0:T(8,128)(2,1)} %expert_pass.1), calls=%async_computation.1 | async-start | bytes 655360 | tf_op jit(solution)/shard_map/all_to_all | solution.py:586
  63.7 0.8 %copy-start.3 = (bf16[384,768]{1,0:T(8,128)(2,1)}, bf16[384,768]{1,0:T(8,128)(2,1)S(1)}, u32[]{:S(2)}) copy-start(bf16[384,768]{1,0:T(8,128)(2,1)S(1)} %collective-permute-done.7.far_hbm) | copy-start | bytes 1769476

commit v8 on v7

--- a/solution.py
+++ b/solution.py
@@ -563,9 +563,10 @@
     got, made = [], []
     chunks = total // CHUNK
     rounds = ring.bit_length() - 1
+    edges = [chunks * i // rounds - (0 < i < rounds) for i in range(rounds + 1)]
     for i in range(rounds):
         got.append(lax.ppermute(held, "seq", [(j, j ^ (1 << i)) for j in range(ring)]))
-        part = range(chunks * i // rounds, chunks * (i + 1) // rounds)
+        part = range(edges[i], edges[i + 1])
         made = query_pass(
             part, tok_here, freq, w_query.T, kf, vt, sc, near if i == rounds - 1 else [], group, made
         )

time: 79.5 us -> 79.5 us (level)
  transfers between devices with their start and end apart: 10 -> 10, of which waited for: 5 -> 4; matrix products, arithmetic and copies ran while one was open for 4% -> 4% of each run, Pallas kernels for 27% -> 27%
where the time goes in v8:
time: 79.5 us; the launch traced here: 79.2 us
  Pallas kernels  36.2 us (46%)
  starting transfers between devices  20.7 us (26%)
  waiting for transfers between devices  18.4 us (23%)
  other arithmetic  1.87 us (2%)
  local copies, waits for them, and re-layouts  1.79 us (2%)
    all_to_all x1, waiting for transfers between devices, per_device(): lax.all_to_all(sent, ('seq', 'head'), split_axis=0, concat_axis=0, tiled=...  11.4 us
    pallas_call x3, Pallas kernels, query_pass(): pl.pallas_call(functools.partial(query_kernel, chunks, slots, len(picks))...  9.09 us
    pallas_call x1, Pallas kernels, key_pass(): pl.pallas_call(functools.partial(key_kernel, size), in_specs=[FAR] * 5, o...  8.48 us
    ppermute x3, starting transfers between devices, per_device(): lax.ppermute(held, 'seq', [(j, j ^ 1 << i) for j in range(ring)])  6.51 us
    pallas_call x1, Pallas kernels, expert_pass(): pl.pallas_call(functools.partial(expert_kernel, cap, ups, downs), in_spec...  6.45 us
    pallas_call x1, Pallas kernels, hidden_pass(): pl.pallas_call(hidden_kernel, in_specs=[FAR] * 2 + [AWAY] * 3 + [HERE] *...  5.72 us
    all_to_all x1, starting transfers between devices, per_device(): lax.all_to_all(sent, ('seq', 'head'), split_axis=0, concat_axis=0, tiled=...  5.58 us
    all_to_all x1, waiting for transfers between devices, per_device(): lax.all_to_all(result, ('seq', 'head'), split_axis=0, concat_axis=0, tile...  5.44 us
  transfers between devices with their start and end apart: 10, of which 4 were waited for; matrix products, arithmetic and copies ran while one was open for 4% of the time, Pallas kernels for 27%

profile of v8, /device:TPU:0, one launch (start us, length us, event | category | flops | bytes accessed | tf_op | source)
XLA Modules:
  0.0 79.2 jit_solution(10603982285681970677)
XLA Ops:
  0.0 0.0 copy-start
  0.0 8.5 %key_pass.1 = (bf16[3072,768]{1,0:T(8,128)(2,1)S(1)}, bf16[3072,768]{1,0:T(8,128)(2,1)S(1)}, bf16[192,3072]{1,0:T(8,128)(2,1)S(1)}, bf16[12,192,256]{2,1,0:T(8,1...) custom-call(bf16[3072,768]{1,0:T(8,128)(2,1)} %tok_hbm.3, bf16[192,768]{1,0:T(8,128)(2,1)} %bitcast.22, ...), custom_call_target="tpu_custom_call" | custom-call | flops 5000000000 | bytes 12000000 | tf_op jit(solution)/shard_map/key_pass/pallas_call | solution.py:152
  8.5 0.5 collective-permute-start
  9.0 2.6 %collective-permute-start.1 = (s32[1,192]{1,0:T(1,128)S(1)}, s32[1,192]{1,0:T(1,128)S(1)}, u32[]{:S(2)}, u32[]{:S(2)}) collective-permute-start(s32[1,192]{1,0:T(1,128)S(1)} %get-tuple-element.36.rest_0_.rest_3_), channel_id=1, source_target_pairs={{0,2},{1,3},{2,0},{3,1},{4,6},{5,7},{6,4},{7,5},{8,10},{9,11},{10,... | collective-permute-start | bytes 2312 | tf_op jit(solution)/shard_map/ppermute | solution.py:557
  11.6 0.1 collective-permute-start.2
  11.6 1.8 %collective-permute-start.3 = (bf16[192,256]{1,0:T(8,128)(2,1)S(1)}, bf16[192,256]{1,0:T(8,128)(2,1)S(1)}, u32[]{:S(2)}, u32[]{:S(2)}) collective-permute-start(bf16[192,256]{1,0:T(8,128)(2,1)S(1)} %get-tuple-element.37), channel_id=1, source_target_pairs={{0,4},{4,0},{8,12},{12,8},{16,20},{20,16},{24,28},{28,24},{1,5},{5... | collective-permute-start | bytes 294920 | tf_op jit(solution)/shard_map/ppermute | solution.py:568
  13.4 0.0 copy-done
  13.4 0.0 copy-done.1
  13.4 2.2 %query_pass.3 = (bf16[4,768,768]{2,1,0:T(8,128)(2,1)S(1)}, f32[4,192,768]{2,1,0:T(8,128)S(1)}) custom-call(bf16[3072,768]{1,0:T(8,128)(2,1)S(1)} %get-tuple-element.32.tok_ref, f32[64,128]{1,0:T(8,128)S(1)} %copy-done.1, bf16[192,768]{1,0:T(8,128)(2,1)S(1)} %bitcast.12, bf16[3072,768]{1,0:T(8,128)(2,1)S(1)} %get-tuple-element.33.kf_ref, ...), custom_call_target="tpu_custom_call" | custom-call | flops 1500000000 | bytes 3000000 | tf_op jit(solution)/shard_map/query_pass/pallas_call | solution.py:269
  15.6 1.1 %collective-permute-done.3.rest_0_ = bf16[192,256]{1,0:T(8,128)(2,1)S(1)} collective-permute-done((bf16[192,256]{1,0:T(8,128)(2,1)S(1)}, bf16[192,256]{1,0:T(8,128)(2,1)S(1)}, u32[]{:S(2)}, u32[]{:S(2)}) %collective-permute-start.3) | collective-permute-done | bytes 98336 | tf_op jit(solution)/shard_map/ppermute | solution.py:568
  16.7 1.9 %collective-permute-start.4 = (bf16[192,256]{1,0:T(8,128)(2,1)S(1)}, bf16[192,256]{1,0:T(8,128)(2,1)S(1)}, u32[]{:S(2)}, u32[]{:S(2)}) collective-permute-start(bf16[192,256]{1,0:T(8,128)(2,1)S(1)} %add_convert_fusion.1), channel_id=1, source_target_pairs={{0,8},{4,12},{8,0},{12,4},{16,24},{20,28},{24,16},{28,20},{1,9},{5... | collective-permute-start | bytes 294920 | tf_op jit(solution)/shard_map/ppermute | solution.py:568
  18.6 2.8 %query_pass.4 = (bf16[4,768,768]{2,1,0:T(8,128)(2,1)S(1)}, f32[4,192,768]{2,1,0:T(8,128)S(1)}) custom-call(bf16[3072,768]{1,0:T(8,128)(2,1)S(1)} %get-tuple-element.32.tok_ref, f32[64,128]{1,0:T(8,128)S(1)} %copy-done.1, bf16[192,768]{1,0:T(8,128)(2,1)S(1)} %bitcast.13, ...), custom_call_target="tpu_custom_call", output_to_operand_aliasing={{0}: (6, {}), {1}: (7, {})} | custom-call | flops 2000000000 | bytes 4000000 | tf_op jit(solution)/shard_map/query_pass/pallas_call | solution.py:269
  21.4 0.0 collective-permute-done.4.rest_1_
  21.4 2.9 %collective-permute-start.5 = (bf16[192,256]{1,0:T(8,128)(2,1)S(1)}, bf16[192,256]{1,0:T(8,128)(2,1)S(1)}, u32[]{:S(2)}, u32[]{:S(2)}) collective-permute-start(bf16[192,256]{1,0:T(8,128)(2,1)S(1)} %add_convert_fusion), channel_id=1, source_target_pairs={{0,16},{4,20},{8,24},{12,28},{16,0},{20,4},{24,8},{28,12},{1,17},{... | collective-permute-start | bytes 294920 | tf_op jit(solution)/shard_map/ppermute | solution.py:568
  24.3 0.0 collective-permute-done.rest_1_.rest_4_
  24.3 0.0 collective-permute-done.1.rest_2_.rest_5_
  24.3 0.0 collective-permute-done.2.rest_3_.rest_6_
  24.3 4.1 %query_pass.5 = (bf16[4,768,768]{2,1,0:T(8,128)(2,1)S(1)}, f32[4,192,768]{2,1,0:T(8,128)S(1)}, bf16[4,192,192]{2,1,0:T(8,128)(2,1)S(1)}) custom-call(bf16[3072,768]{1,0:T(8,128)(2,1)S(1)} %get-tuple-element.32.tok_ref, f32[64,128]{1,0:T(8,128)S(1)} %copy-done.1, bf16[192,768]{1,0:T(8,128)(2,1)S(1)} %bitcast.14, ...), custom_call_target="tpu_custom_call", output_to_operand_aliasing={{0}: (10, {}), {1}: (11, {})} | custom-call | flops 2500000000 | bytes 5000000 | tf_op jit(solution)/shard_map/query_pass/pallas_call | solution.py:269
  28.4 0.0 collective-permute-done.5.rest_2_
  28.5 3.1 %norm_pass.1 = (bf16[192,768]{1,0:T(8,128)(2,1)}, bf16[384,768]{1,0:T(8,128)(2,1)}, bf16[192,768]{1,0:T(8,128)(2,1)}, bf16[768,384]{1,0:T(8,128)(2,1)}) custom-call(f32[4,192,768]{2,1,0:T(8,128)S(1)} %get-tuple-element.47.raw_ref, bf16[4,768,768]{2,1,0:T(8,128)(2,1)S(1)} %get-tuple-element.48.qft_ref, bf16[4,192,192]{2,1,0:T(8,128)(2,1)S(1)} %get-tuple-element.49.seen_ref, ...), custom_call_target="tpu_custom_call" | custom-call | flops 3000000000 | bytes 8000000 | tf_op jit(solution)/shard_map/norm_pass/pallas_call | solution.py:331
  31.6 5.6 %all-to-all-start = ((bf16[32,24,384]{2,1,0:T(8,128)(2,1)}), bf16[32,24,384]{2,1,0:T(8,128)(2,1)S(1)}, u32[]{:S(2)}, u32[]{:S(2)}) async-start(bf16[32,24,384]{2,1,0:T(8,128)(2,1)} %bitcast.6), calls=%async_computation | async-start | bytes 1179648 | tf_op jit(solution)/shard_map/all_to_all | solution.py:579
  37.1 0.3 collective-permute-start.6
  37.5 0.0 copy-done.4
  37.5 0.1 copy.28
  37.6 0.1 copy.25
  37.6 0.1 pad.15.clone
  37.7 0.1 stack.16
  37.8 0.1 copy.26
  37.9 0.1 pad.16.clone
  38.0 0.1 stack.17
  38.1 0.1 copy.27
  38.2 0.1 pad.17.clone
  38.2 0.1 stack.18
  38.3 0.1 stack.15
  38.4 0.6 pad_add_fusion.pick_ref
  39.0 0.4 collective-permute-done.6.near_hbm
  39.4 1.2 %pad_maximum_fusion = bf16[384,768]{1,0:T(8,128)(2,1)S(1)} fusion(bf16[192,768]{1,0:T(8,128)(2,1)S(1)} %slice.16, bf16[192,768]{1,0:T(8,128)(2,1)} %get-tuple-element.53), kind=kLoop, calls=%fused_computation | loop fusion | flops 1179648 | bytes 1179648 | tf_op jit(solution)/shard_map/concatenate | solution.py:581
  40.7 1.8 %collective-permute-start.7 = (bf16[384,768]{1,0:T(8,128)(2,1)S(1)}, bf16[384,768]{1,0:T(8,128)(2,1)S(1)}, u32[]{:S(2)}, u32[]{:S(2)}) collective-permute-start(bf16[384,768]{1,0:T(8,128)(2,1)S(1)} %pad_maximum_fusion), channel_id=1, source_target_pairs={{0,2},{1,3},{2,0},{3,1},{4,6},{5,7},{6,4},{7,5},{8,10},{9,11},{10,... | collective-permute-start | bytes 1769480 | tf_op jit(solution)/shard_map/ppermute | solution.py:557
  42.5 11.4 %all-to-all-done = bf16[32,24,384]{2,1,0:T(8,128)(2,1)S(1)} async-done(((bf16[32,24,384]{2,1,0:T(8,128)(2,1)}), bf16[32,24,384]{2,1,0:T(8,128)(2,1)S(1)}, u32[]{:S(2)}, u32[]{:S(2)}) %all-to-all-start) | async-done | bytes 589856 | tf_op jit(solution)/shard_map/all_to_all | solution.py:579
  53.9 6.5 %expert_pass.1 = bf16[32,40,128]{2,1,0:T(8,128)(2,1)} custom-call(bf16[8,4,24,384]{3,2,1,0:T(8,128)(2,1)S(1)} %bitcast.15, bf16[4,192,768]{2,1,0:T(8,128)(2,1)} %bitcast.16, bf16[1,768,3072]{2,1,0:T(8,128)(2,1)} %wi_hbm.1, bf16[1,3072,768]{2,1,0:T(8,128)(2,1)} %wd_hbm.1), custom_call_target="tpu_custom_call" | custom-call | flops 2000000000 | bytes 12000000 | tf_op jit(solution)/shard_map/expert_pass/pallas_call | solution.py:414
  60.4 0.0 copy-done.2
  60.4 3.3 %all-to-all-start.1 = ((bf16[32,40,128]{2,1,0:T(8,128)(2,1)}), bf16[32,40,128]{2,1,0:T(8,128)(2,1)S(1)}, u32[]{:S(2)}, u32[]{:S(2)}) async-start(bf16[32,40,128]{2,1,0:T(8,128)(2,1)} %expert_pass.1), calls=%async_computation.1 | async-start | bytes 655360 | tf_op jit(solution)/shard_map/all_to_all | solution.py:587
  63.6 0.0 collective-permute-done.7.far_hbm
  63.7 0.0 copy-start.3
  63.7 0.8 %copy-done.3 = bf16[384,768]{1,0:T(8,128)(2,1)} copy-done((bf16[384,768]{1,0:T(8,128)(2,1)}, bf16[384,768]{1,0:T(8,128)(2,1)S(1)}, u32[]{:S(2)}) %copy-start.3) | copy-done | bytes 589848
  64.5 5.7 %hidden_pass.1 = (bf16[768,768]{1,0:T(8,128)(2,1)}, bf16[4,768,256]{2,1,0:T(8,128)(2,1)}) custom-call(bf16[3072,768]{1,0:T(8,128)(2,1)} %tok_hbm.3, bf16[4,192,768]{2,1,0:T(8,128)(2,1)} %bitcast.17, bf16[192,768]{1,0:T(8,128)(2,1)} %get-tuple-element.51.own_hbm, bf16[384,768]{1,0:T(8,128)(2,1)} %copy-done.2, bf16[384,768]{1,0:T(8,128)(2,1)} %copy-done.3, ...), custom_call_target="tpu_custom_call" | custom-call | flops 2000000000 | bytes 6000000 | tf_op jit(solution)/shard_map/hidden_pass/pallas_call | solution.py:466
  70.2 5.4 %all-to-all-done.1.back_hbm = bf16[32,40,128]{2,1,0:T(8,128)(2,1)S(1)} async-done(((bf16[32,40,128]{2,1,0:T(8,128)(2,1)}), bf16[32,40,128]{2,1,0:T(8,128)(2,1)S(1)}, u32[]{:S(2)}, u32[]{:S(2)}) %all-to-all-start.1) | async-done | bytes 327712 | tf_op jit(solution)/shard_map/all_to_all | solution.py:587
  75.6 3.4 %combine_pass.1 = bf16[768,768]{1,0:T(8,128)(2,1)} custom-call(bf16[768,768]{1,0:T(8,128)(2,1)} %get-tuple-element.56.hid_hbm, bf16[4,768,256]{2,1,0:T(8,128)(2,1)} %get-tuple-element.57.comb_hbm, bf16[32,40,128]{2,1,0:T(8,128)(2,1)S(1)} %all-to-all-done.1.back_hbm), custom_call_target="tpu_custom_call" | custom-call | flops 1000000000 | bytes 4000000 | tf_op jit(solution)/shard_map/combine_pass/pallas_call | solution.py:524
  (9 shorter events, 0.1 us)
Async XLA Ops:
  0.0 13.4 %copy-start = (bf16[768,192]{0,1:T(8,128)(2,1)S(1)}, bf16[768,192]{0,1:T(8,128)(2,1)}, u32[]{:S(2)}) copy-start(bf16[768,192]{0,1:T(8,128)(2,1)} %param.11) | copy-start | bytes 884740
  0.0 13.4 %copy-start.1 = (f32[64,128]{1,0:T(8,128)S(1)}, f32[64,128]{1,0:T(8,128)}, u32[]{:S(2)}) copy-start(f32[64,128]{1,0:T(8,128)} %freq_ref.5) | copy-start | bytes 98308
  8.5 15.8 %collective-permute-start = (s32[1,192]{1,0:T(1,128)S(1)}, s32[1,192]{1,0:T(1,128)S(1)}, u32[]{:S(2)}, u32[]{:S(2)}) collective-permute-start(s32[1,192]{1,0:T(1,128)S(1)} %get-tuple-element.36.rest_0_.rest_3_), channel_id=1, source_target_pairs={{0,1},{1,0},{2,3},{3,2},{4,5},{5,4},{6,7},{7,6},{8,9},{9,8},{10,11... | collective-permute-start | bytes 2312 | tf_op jit(solution)/shard_map/ppermute | solution.py:557
  9.0 15.3 %collective-permute-start.1 = (s32[1,192]{1,0:T(1,128)S(1)}, s32[1,192]{1,0:T(1,128)S(1)}, u32[]{:S(2)}, u32[]{:S(2)}) collective-permute-start(s32[1,192]{1,0:T(1,128)S(1)} %get-tuple-element.36.rest_0_.rest_3_), channel_id=1, source_target_pairs={{0,2},{1,3},{2,0},{3,1},{4,6},{5,7},{6,4},{7,5},{8,10},{9,11},{10,... | collective-permute-start | bytes 2312 | tf_op jit(solution)/shard_map/ppermute | solution.py:557
  11.6 12.8 %collective-permute-start.2 = (s32[1,192]{1,0:T(1,128)S(1)}, s32[1,192]{1,0:T(1,128)S(1)}, u32[]{:S(2)}, u32[]{:S(2)}) collective-permute-start(s32[1,192]{1,0:T(1,128)S(1)} %get-tuple-element.36.rest_0_.rest_3_), channel_id=1, source_target_pairs={{0,3},{1,2},{2,1},{3,0},{4,7},{5,6},{6,5},{7,4},{8,11},{9,10},{10,... | collective-permute-start | bytes 2312 | tf_op jit(solution)/shard_map/ppermute | solution.py:557
  11.6 5.1 %collective-permute-start.3 = (bf16[192,256]{1,0:T(8,128)(2,1)S(1)}, bf16[192,256]{1,0:T(8,128)(2,1)S(1)}, u32[]{:S(2)}, u32[]{:S(2)}) collective-permute-start(bf16[192,256]{1,0:T(8,128)(2,1)S(1)} %get-tuple-element.37), channel_id=1, source_target_pairs={{0,4},{4,0},{8,12},{12,8},{16,20},{20,16},{24,28},{28,24},{1,5},{5... | collective-permute-start | bytes 294920 | tf_op jit(solution)/shard_map/ppermute | solution.py:568
  16.7 4.7 %collective-permute-start.4 = (bf16[192,256]{1,0:T(8,128)(2,1)S(1)}, bf16[192,256]{1,0:T(8,128)(2,1)S(1)}, u32[]{:S(2)}, u32[]{:S(2)}) collective-permute-start(bf16[192,256]{1,0:T(8,128)(2,1)S(1)} %add_convert_fusion.1), channel_id=1, source_target_pairs={{0,8},{4,12},{8,0},{12,4},{16,24},{20,28},{24,16},{28,20},{1,9},{5... | collective-permute-start | bytes 294920 | tf_op jit(solution)/shard_map/ppermute | solution.py:568
  21.4 7.0 %collective-permute-start.5 = (bf16[192,256]{1,0:T(8,128)(2,1)S(1)}, bf16[192,256]{1,0:T(8,128)(2,1)S(1)}, u32[]{:S(2)}, u32[]{:S(2)}) collective-permute-start(bf16[192,256]{1,0:T(8,128)(2,1)S(1)} %add_convert_fusion), channel_id=1, source_target_pairs={{0,16},{4,20},{8,24},{12,28},{16,0},{20,4},{24,8},{28,12},{1,17},{... | collective-permute-start | bytes 294920 | tf_op jit(solution)/shard_map/ppermute | solution.py:568
  28.5 9.0 %copy-start.4 = (s32[32,1,6]{0,1,2:T(1,128)S(1)}, s32[32,1,6]{0,1,2:T(1,128)}, u32[]{:S(2)}) copy-start(s32[32,1,6]{0,1,2:T(1,128)} %param.19) | copy-start | bytes 2308
  31.6 22.3 %all-to-all-start = ((bf16[32,24,384]{2,1,0:T(8,128)(2,1)}), bf16[32,24,384]{2,1,0:T(8,128)(2,1)S(1)}, u32[]{:S(2)}, u32[]{:S(2)}) async-start(bf16[32,24,384]{2,1,0:T(8,128)(2,1)} %bitcast.6), calls=%async_computation | async-start | bytes 1179648 | tf_op jit(solution)/shard_map/all_to_all | solution.py:579
  37.1 2.3 %collective-permute-start.6 = (bf16[384,768]{1,0:T(8,128)(2,1)}, bf16[384,768]{1,0:T(8,128)(2,1)S(1)}, u32[]{:S(2)}, u32[]{:S(2)}) collective-permute-start(bf16[384,768]{1,0:T(8,128)(2,1)} %get-tuple-element.52), channel_id=1, source_target_pairs={{0,1},{1,0},{2,3},{3,2},{4,5},{5,4},{6,7},{7,6},{8,9},{9,8},{10,11... | collective-permute-start | bytes 1769480 | tf_op jit(solution)/shard_map/ppermute | solution.py:557
  39.4 20.9 %copy-start.2 = (bf16[384,768]{1,0:T(8,128)(2,1)}, bf16[384,768]{1,0:T(8,128)(2,1)S(1)}, u32[]{:S(2)}) copy-start(bf16[384,768]{1,0:T(8,128)(2,1)S(1)} %collective-permute-done.6.near_hbm) | copy-start | bytes 1769476
  40.7 23.0 %collective-permute-start.7 = (bf16[384,768]{1,0:T(8,128)(2,1)S(1)}, bf16[384,768]{1,0:T(8,128)(2,1)S(1)}, u32[]{:S(2)}, u32[]{:S(2)}) collective-permute-start(bf16[384,768]{1,0:T(8,128)(2,1)S(1)} %pad_maximum_fusion), channel_id=1, source_target_pairs={{0,2},{1,3},{2,0},{3,1},{4,6},{5,7},{6,4},{7,5},{8,10},{9,11},{10,... | collective-permute-start | bytes 1769480 | tf_op jit(solution)/shard_map/ppermute | solution.py:557
  60.4 15.3 %all-to-all-start.1 = ((bf16[32,40,128]{2,1,0:T(8,128)(2,1)}), bf16[32,40,128]{2,1,0:T(8,128)(2,1)S(1)}, u32[]{:S(2)}, u32[]{:S(2)}) async-start(bf16[32,40,128]{2,1,0:T(8,128)(2,1)} %expert_pass.1), calls=%async_computation.1 | async-start | bytes 655360 | tf_op jit(solution)/shard_map/all_to_all | solution.py:587
  63.7 0.8 %copy-start.3 = (bf16[384,768]{1,0:T(8,128)(2,1)}, bf16[384,768]{1,0:T(8,128)(2,1)S(1)}, u32[]{:S(2)}) copy-start(bf16[384,768]{1,0:T(8,128)(2,1)S(1)} %collective-permute-done.7.far_hbm) | copy-start | bytes 1769476
